TPU v7x, 128 devices: a whole 4x4x4 slice. The times are simulated.
128 devices in a mesh: dp: 16 (over y, z_hi, core), tensor: 8 (over z_lo, x).
Axes of the slice: x: 4, y: 4, z: 4 (z_hi: 2, z_lo: 2; z = z_hi * 2 + z_lo), core: 2. Of those that a mesh axis runs over, the one named last changes fastest.
Arguments:
- tokens: bfloat16 [2, 64, 16, 2304], P(None, None, 'dp'), may hold values from -6 to 6
- cotangent: bfloat16 [3, 2, 64, 16, 2304], P(None, None, None, 'dp'), may hold values from -6 to 6
- segments: int32 [2, 1024], replicated, may hold values from 0 to 4, never falling along the last dimension, each value on 1 to 512 neighbouring positions
- codes_query: int32 [2304, 2048], P('dp', 'tensor'), may hold values from -128 to 127
- codes_key: int32 [2304, 1024], P('dp', 'tensor'), may hold values from -128 to 127
- codes_value: int32 [2304, 1024], P('dp', 'tensor'), may hold values from -128 to 127
- codes_out: int32 [2048, 2304], P('tensor', 'dp'), may hold values from -128 to 127
- codes_gate: int32 [2304, 9216], P('dp', 'tensor'), may hold values from -128 to 127
- codes_up: int32 [2304, 9216], P('dp', 'tensor'), may hold values from -128 to 127
- codes_down: int32 [9216, 2304], P('tensor', 'dp'), may hold values from -128 to 127
- query_column_scale: float32 [2048], P('tensor'), may hold values from 0.00014583333 to 0.0005833333
- key_column_scale: float32 [1024], P('tensor'), may hold values from 0.00014583333 to 0.0005833333
- value_column_scale: float32 [1024], P('tensor'), may hold values from 0.00014583333 to 0.0005833333
- output_column_scale: float32 [2304], replicated, may hold values from 0.00015467961 to 0.00061871845
- gate_column_scale: float32 [9216], P('tensor'), may hold values from 0.00014583333 to 0.0005833333
- up_column_scale: float32 [9216], P('tensor'), may hold values from 0.00014583333 to 0.0005833333
- down_column_scale: float32 [2304], replicated, may hold values from 7.2916664e-05 to 0.00029166666
- gain_first: float32 [2304], replicated, may hold values from -0.5 to 0.5
- gain_second: float32 [2304], replicated, may hold values from -0.5 to 0.5
- gain_third: float32 [2304], replicated, may hold values from -0.5 to 0.5
- gain_fourth: float32 [2304], replicated, may hold values from -0.5 to 0.5
Outputs:
- results: bfloat16 [3, 2, 64, 16, 2304], P(None, None, None, 'dp')
- input_token_gradient: float32 [2, 64, 16, 2304], P(None, None, 'dp')
- query_grad: float32 [2304, 2048], P('dp', 'tensor')
- key_grad: float32 [2304, 1024], P('dp', 'tensor')
- value_grad: float32 [2304, 1024], P('dp', 'tensor')
- out_grad: float32 [2048, 2304], P('tensor', 'dp')
- gate_grad: float32 [2304, 9216], P('dp', 'tensor')
- up_grad: float32 [2304, 9216], P('dp', 'tensor')
- down_grad: float32 [9216, 2304], P('tensor', 'dp')
- query_scale_grad: float32 [2048], P('tensor')
- key_scale_grad: float32 [1024], P('tensor')
- value_scale_grad: float32 [1024], P('tensor')
- out_scale_grad: float32 [2304], P('dp')
- gate_scale_grad: float32 [9216], P('tensor')
- up_scale_grad: float32 [9216], P('tensor')
- down_scale_grad: float32 [2304], P('dp')
- gain_first_grad: float32 [2304], P('dp')
- gain_second_grad: float32 [2304], P('dp')
- gain_third_grad: float32 [2304], P('dp')
- gain_fourth_grad: float32 [2304], P('dp')
Inputs may be any that keep to these rules, and one draw needn't show every extreme that they name: `segments`: in each micro-batch the document number starts at 0, never falls, and each of the 5 documents covers 1 to min(512, 1020) positions; one covers exactly that many.
All inputs are finite; a program needn't handle non-finite values.
Results may differ from a plain program's by a relative error of at most 0.025.
Values may be sent and summed in bfloat16 or wider, within the bound.
A program may use at most 640 MiB of HBM per device.

v0:
```python
import jax
import jax.numpy as jnp
from jax import lax
from jax.sharding import PartitionSpec as P

HD = 256


EPSILON = 1e-06
SOFTCAP = 50.0
ROPE_BASE = 10000.0
SHIFTS = (0, 4, 6)
MASKED = -1e30
F32 = jnp.float32
B16 = jnp.bfloat16


def partner(value, axis, apart):
    return lax.ppermute(value, axis, [(i, i ^ 1 << apart) for i in range(lax.axis_size(axis))])


def rms_gain(signal, gain):
    inverse = lax.rsqrt(jnp.mean(signal * signal, axis=-1, keepdims=True) + EPSILON)
    return signal * inverse * (1.0 + gain)


def norm_back(signal, gain, upstream):
    _, backward_step = jax.vjp(rms_gain, signal, gain)
    return backward_step(upstream)


def geglu(gate_pre, up_pre):
    return jax.nn.gelu(gate_pre, approximate=True) * up_pre


def level_widths(code_array, shift_bits):
    if shift_bits == 0:
        return code_array.astype(jnp.float32)
    stride = 2**shift_bits
    return (jnp.floor_divide(code_array, stride) * stride + stride // 2).astype(jnp.float32)


def angles(places, head_size):
    halfway = head_size // 2
    expo = jnp.arange(halfway, dtype=jnp.float32) * (2.0 / head_size)
    freqs = places.astype(jnp.float32)[:, None] * jnp.power(ROPE_BASE, -expo)[None, :]
    return (jnp.cos(freqs), jnp.sin(freqs))


def rotate(signal, cosine, sine):
    halfway = signal.shape[-1] // 2
    former = signal[..., :halfway]
    latter = signal[..., halfway:]
    return jnp.concatenate(
        [former * cosine - latter * sine, latter * cosine + former * sine], axis=-1
    )


def unrotate(upstream, cosine, sine):
    halfway = upstream.shape[-1] // 2
    former = upstream[..., :halfway]
    latter = upstream[..., halfway:]
    return jnp.concatenate(
        [former * cosine + latter * sine, latter * cosine - former * sine], axis=-1
    )


def restore_weights(code_low, scaling):
    whole = code_low.astype(jnp.int32)
    return jnp.stack(
        [(level_widths(whole, shift_bits) * scaling).astype(B16) for shift_bits in SHIFTS]
    )


def weight_terms(per_width, code_low):
    whole = code_low.astype(jnp.int32)
    scaled = jnp.zeros((per_width.shape[-1],), F32)
    for width_id in range(len(SHIFTS)):
        scaled = scaled + jnp.sum(
            per_width[width_id] * level_widths(whole, SHIFTS[width_id]), axis=0
        )
    return (jnp.sum(per_width, axis=0), scaled)


def accumulate(stored, latest):
    if stored is None:
        return latest
    return tuple((earlier + update for earlier, update in zip(stored, latest)))


def body(
    tokens,
    cotangent,
    segments,
    codes_query,
    codes_key,
    codes_value,
    codes_out,
    codes_gate,
    codes_up,
    codes_down,
    query_column_scale,
    key_column_scale,
    value_column_scale,
    output_column_scale,
    gate_column_scale,
    up_column_scale,
    down_column_scale,
    gain_first,
    gain_second,
    gain_third,
    gain_fourth,
):
    ranks = lax.axis_size("dp")
    my_rank = lax.axis_index("dp")
    parity = lax.axis_index("tensor") % 2
    micros = tokens.shape[0]
    tok_rows = tokens.shape[1]
    seq_len = tok_rows * ranks
    head_size = HD
    query_cols = codes_query.shape[1]
    key_cols = codes_key.shape[1]
    heads_here = query_cols // head_size
    halved = key_cols < head_size
    kv_here = 1
    repeat = heads_here // kv_here
    widths = len(SHIFTS)
    low_codes = tuple(
        (
            matrix.astype(B16)
            for matrix in (
                codes_query,
                codes_key,
                codes_value,
                codes_out,
                codes_gate,
                codes_up,
                codes_down,
            )
        )
    )
    scaling_factors = (
        query_column_scale,
        key_column_scale,
        value_column_scale,
        output_column_scale,
        gate_column_scale,
        up_column_scale,
        down_column_scale,
    )
    layer_outputs = []
    input_grads = []
    totals = None
    shards = None
    col_totals = None
    for micro_batch in range(micros):
        collected = (
            lax.all_gather(low_codes[0], "dp", axis=0, tiled=True),
            lax.all_gather(low_codes[1], "dp", axis=0, tiled=True),
            lax.all_gather(low_codes[2], "dp", axis=0, tiled=True),
            lax.all_gather(low_codes[3], "dp", axis=1, tiled=True),
            lax.all_gather(low_codes[4], "dp", axis=0, tiled=True),
            lax.all_gather(low_codes[5], "dp", axis=0, tiled=True),
            lax.all_gather(low_codes[6], "dp", axis=1, tiled=True),
        )
        weight_matrices = [
            restore_weights(collected[level_choice], scaling_factors[level_choice])
            for level_choice in range(7)
        ]
        w_query, w_key, w_value, w_out, w_gate, w_up, w_down = weight_matrices
        doc_all = segments[micro_batch]
        doc_grid = doc_all.reshape(tok_rows, ranks)
        doc_mine = lax.dynamic_slice_in_dim(doc_grid, my_rank, 1, 1)[:, 0]
        place = jnp.arange(tok_rows, dtype=jnp.int32) * ranks + my_rank
        starts = jnp.sum((doc_all[None, :] < doc_mine[:, None]).astype(jnp.int32), axis=1)
        cosine, sine = angles(place - starts, head_size)
        cos_b = cosine[None, :, None, :]
        sin_b = sine[None, :, None, :]
        key_doc = doc_grid.T.reshape(seq_len)
        key_place = jnp.arange(seq_len, dtype=jnp.int32).reshape(tok_rows, ranks).T.reshape(seq_len)
        allowed = (key_doc[None, :] == doc_mine[:, None]) & (key_place[None, :] <= place[:, None])
        layer_inputs = tokens[micro_batch, :, 0, :].astype(F32)
        normed_input = rms_gain(layer_inputs, gain_first).astype(B16)
        query_pre = jnp.einsum("rd,wdc->wrc", normed_input, w_query, preferred_element_type=F32)
        key_pre = jnp.einsum("rd,wdc->wrc", normed_input, w_key, preferred_element_type=F32)
        value_pre = jnp.einsum("rd,wdc->wrc", normed_input, w_value, preferred_element_type=F32)
        query = rotate(
            query_pre.reshape(widths, tok_rows, heads_here, head_size), cos_b, sin_b
        ).astype(B16)
        other_key, other_value = partner((key_pre, value_pre), "tensor", 0)
        leading = parity == 0
        key_pre = jnp.where(
            leading,
            jnp.concatenate([key_pre, other_key], -1),
            jnp.concatenate([other_key, key_pre], -1),
        )
        value_pre = jnp.where(
            leading,
            jnp.concatenate([value_pre, other_value], -1),
            jnp.concatenate([other_value, value_pre], -1),
        )
        key_here = rotate(
            key_pre.reshape(widths, tok_rows, kv_here, head_size), cos_b, sin_b
        ).astype(B16)
        value_here = value_pre.reshape(widths, tok_rows, kv_here, head_size).astype(B16)
        keys, values = (
            lax.all_gather(key_here, "dp", axis=1, tiled=True),
            lax.all_gather(value_here, "dp", axis=1, tiled=True),
        )
        query_grp = query.reshape(widths, tok_rows, kv_here, repeat, head_size)
        scores = (
            jnp.einsum("wrgph,wsgh->wgprs", query_grp, keys, preferred_element_type=F32) * 0.0625
        )
        bent = jnp.tanh(scores / SOFTCAP)
        capped = jnp.where(allowed, SOFTCAP * bent, MASKED)
        peak = jnp.max(capped, axis=-1, keepdims=True)
        expo = jnp.exp(capped - peak)
        total = jnp.sum(expo, axis=-1, keepdims=True)
        logsum = peak + jnp.log(total)
        probs = (expo / total).astype(B16)
        attended = jnp.einsum("wgprs,wsgh->wrgph", probs, values, preferred_element_type=F32)
        attended = attended.astype(B16).reshape(widths, tok_rows, query_cols)
        branch = lax.psum(
            jnp.einsum("wrc,wcd->wrd", attended, w_out, preferred_element_type=F32), "tensor"
        )
        middle = layer_inputs[None] + rms_gain(branch, gain_second)
        normed_middle = rms_gain(middle, gain_third).astype(B16)
        gate_pre = jnp.einsum("wrd,wdc->wrc", normed_middle, w_gate, preferred_element_type=F32)
        up_pre = jnp.einsum("wrd,wdc->wrc", normed_middle, w_up, preferred_element_type=F32)
        hidden = geglu(gate_pre, up_pre).astype(B16)
        feedforward = lax.psum(
            jnp.einsum("wrc,wcd->wrd", hidden, w_down, preferred_element_type=F32), "tensor"
        )
        layer_outputs.append((middle + rms_gain(feedforward, gain_fourth)).astype(B16))
        backward_codes = (
            lax.all_gather(low_codes[0], "dp", axis=0, tiled=True),
            lax.all_gather(low_codes[1], "dp", axis=0, tiled=True),
            lax.all_gather(low_codes[2], "dp", axis=0, tiled=True),
            lax.all_gather(low_codes[3], "dp", axis=1, tiled=True),
            lax.all_gather(low_codes[4], "dp", axis=0, tiled=True),
            lax.all_gather(low_codes[5], "dp", axis=0, tiled=True),
            lax.all_gather(low_codes[6], "dp", axis=1, tiled=True),
        )
        backward_matrices = [
            restore_weights(backward_codes[level_choice], scaling_factors[level_choice])
            for level_choice in range(7)
        ]
        b_query, b_key, b_value, b_out, b_gate, b_up, b_down = backward_matrices
        upstream = cotangent[:, micro_batch, :, 0, :].astype(F32)
        d_feed, fourth_term = norm_back(feedforward, gain_fourth, upstream)
        d_feed = d_feed.astype(B16)
        d_hidden = jnp.einsum("wrd,wcd->wrc", d_feed, b_down, preferred_element_type=F32)
        down_w, down_s = weight_terms(
            jnp.einsum("wrc,wrd->wcd", hidden, d_feed, preferred_element_type=F32),
            backward_codes[6],
        )
        _, pull_geglu = jax.vjp(geglu, gate_pre, up_pre)
        d_gate, d_up = pull_geglu(d_hidden)
        d_gate = d_gate.astype(B16)
        d_up = d_up.astype(B16)
        d_normed_middle = jnp.einsum(
            "wrc,wdc->wrd", d_gate, b_gate, preferred_element_type=F32
        ) + jnp.einsum("wrc,wdc->wrd", d_up, b_up, preferred_element_type=F32)
        gate_w, gate_s = weight_terms(
            jnp.einsum("wrd,wrc->wdc", normed_middle, d_gate, preferred_element_type=F32),
            backward_codes[4],
        )
        upper_w, upper_s = weight_terms(
            jnp.einsum("wrd,wrc->wdc", normed_middle, d_up, preferred_element_type=F32),
            backward_codes[5],
        )
        d_normed_middle = lax.psum(d_normed_middle, "tensor")
        d_mid_norm, third_term = norm_back(middle, gain_third, d_normed_middle)
        d_middle = upstream + d_mid_norm
        d_branch, second_term = norm_back(branch, gain_second, d_middle)
        d_branch = d_branch.astype(B16)
        d_attended = jnp.einsum("wrd,wcd->wrc", d_branch, b_out, preferred_element_type=F32).astype(
            B16
        )
        out_w, out_s = weight_terms(
            jnp.einsum("wrc,wrd->wcd", attended, d_branch, preferred_element_type=F32),
            backward_codes[3],
        )
        scores = (
            jnp.einsum("wrgph,wsgh->wgprs", query_grp, keys, preferred_element_type=F32) * 0.0625
        )
        bent = jnp.tanh(scores / SOFTCAP)
        capped = jnp.where(allowed, SOFTCAP * bent, MASKED)
        weights_f = jnp.exp(capped - logsum)
        d_att_grp = d_attended.reshape(widths, tok_rows, kv_here, repeat, head_size)
        d_probs = jnp.einsum("wrgph,wsgh->wgprs", d_att_grp, values, preferred_element_type=F32)
        centre = jnp.sum(weights_f * d_probs, axis=-1, keepdims=True)
        d_scores = (weights_f * (d_probs - centre) * (1.0 - bent * bent)).astype(B16)
        d_query = (
            jnp.einsum("wgprs,wsgh->wrgph", d_scores, keys, preferred_element_type=F32) * 0.0625
        )
        d_keys = (
            jnp.einsum("wgprs,wrgph->wsgh", d_scores, query_grp, preferred_element_type=F32)
            * 0.0625
        )
        d_values = jnp.einsum(
            "wgprs,wrgph->wsgh", weights_f.astype(B16), d_att_grp, preferred_element_type=F32
        )
        d_keys, d_values = (
            lax.psum_scatter(
                d_keys.astype(jnp.bfloat16), "dp", scatter_dimension=1, tiled=True
            ).astype(jnp.float32),
            lax.psum_scatter(
                d_values.astype(jnp.bfloat16), "dp", scatter_dimension=1, tiled=True
            ).astype(jnp.float32),
        )
        other_dk, other_dv = (
            partner(d_keys.astype(jnp.bfloat16), "tensor", 0).astype(d_keys.dtype),
            partner(d_values.astype(jnp.bfloat16), "tensor", 0).astype(d_values.dtype),
        )
        d_keys = (
            unrotate(d_keys + other_dk, cos_b, sin_b)
            .astype(B16)
            .reshape(widths, tok_rows, head_size)
        )
        d_values = (d_values + other_dv).astype(B16).reshape(widths, tok_rows, head_size)
        offset = parity * key_cols
        d_key_pre = lax.dynamic_slice_in_dim(d_keys, offset, key_cols, 2)
        d_value_pre = lax.dynamic_slice_in_dim(d_values, offset, key_cols, 2)
        d_query_pre = (
            unrotate(d_query.reshape(widths, tok_rows, heads_here, head_size), cos_b, sin_b)
            .astype(B16)
            .reshape(widths, tok_rows, query_cols)
        )
        d_normed_input = jnp.einsum("wrc,wdc->rd", d_query_pre, b_query, preferred_element_type=F32)
        d_normed_input = d_normed_input + jnp.einsum(
            "wrc,wdc->rd", d_key_pre, b_key, preferred_element_type=F32
        )
        d_normed_input = d_normed_input + jnp.einsum(
            "wrc,wdc->rd", d_value_pre, b_value, preferred_element_type=F32
        )
        query_w, query_s = weight_terms(
            jnp.einsum("rd,wrc->wdc", normed_input, d_query_pre, preferred_element_type=F32),
            backward_codes[0],
        )
        key_w, key_s = weight_terms(
            jnp.einsum("rd,wrc->wdc", normed_input, d_key_pre, preferred_element_type=F32),
            backward_codes[1],
        )
        value_w, value_s = weight_terms(
            jnp.einsum("rd,wrc->wdc", normed_input, d_value_pre, preferred_element_type=F32),
            backward_codes[2],
        )
        d_normed_input = lax.psum(d_normed_input.astype(jnp.bfloat16), "tensor").astype(jnp.float32)
        d_inputs, first_term = norm_back(layer_inputs, gain_first, d_normed_input)
        input_grads.append(d_inputs + jnp.sum(d_middle, axis=0))
        terms = (
            query_w,
            key_w,
            value_w,
            out_w,
            gate_w,
            upper_w,
            down_w,
            first_term,
            second_term,
            third_term,
            fourth_term,
            out_s,
            down_s,
        )
        totals = accumulate(totals, terms)
        col_totals = accumulate(col_totals, (query_s, key_s, value_s, gate_s, upper_s))
    shards = (
        lax.psum_scatter(
            totals[0].astype(jnp.bfloat16), "dp", scatter_dimension=0, tiled=True
        ).astype(jnp.float32),
        lax.psum_scatter(
            totals[1].astype(jnp.bfloat16), "dp", scatter_dimension=0, tiled=True
        ).astype(jnp.float32),
        lax.psum_scatter(
            totals[2].astype(jnp.bfloat16), "dp", scatter_dimension=0, tiled=True
        ).astype(jnp.float32),
        lax.psum_scatter(
            totals[3].astype(jnp.bfloat16), "dp", scatter_dimension=1, tiled=True
        ).astype(jnp.float32),
        lax.psum_scatter(
            totals[4].astype(jnp.bfloat16), "dp", scatter_dimension=0, tiled=True
        ).astype(jnp.float32),
        lax.psum_scatter(
            totals[5].astype(jnp.bfloat16), "dp", scatter_dimension=0, tiled=True
        ).astype(jnp.float32),
        lax.psum_scatter(
            totals[6].astype(jnp.bfloat16), "dp", scatter_dimension=1, tiled=True
        ).astype(jnp.float32),
        lax.psum_scatter(
            totals[7].astype(jnp.bfloat16), "dp", scatter_dimension=0, tiled=True
        ).astype(jnp.float32),
        lax.psum_scatter(
            totals[8].astype(jnp.bfloat16), "dp", scatter_dimension=0, tiled=True
        ).astype(jnp.float32),
        lax.psum_scatter(
            totals[9].astype(jnp.bfloat16), "dp", scatter_dimension=0, tiled=True
        ).astype(jnp.float32),
        lax.psum_scatter(
            totals[10].astype(jnp.bfloat16), "dp", scatter_dimension=0, tiled=True
        ).astype(jnp.float32),
        lax.psum_scatter(
            totals[11].astype(jnp.bfloat16), "dp", scatter_dimension=0, tiled=True
        ).astype(jnp.float32),
        lax.psum_scatter(
            totals[12].astype(jnp.bfloat16), "dp", scatter_dimension=0, tiled=True
        ).astype(jnp.float32),
    )
    row_sums = lax.psum((shards[11], shards[12]), "tensor")
    col_sums = lax.psum(
        (col_totals[0], col_totals[1], col_totals[2], col_totals[3], col_totals[4]), "dp"
    )
    results = jnp.stack(layer_outputs, axis=1)[:, :, :, None, :]
    input_token_gradient = jnp.stack(input_grads)[:, :, None, :]
    return (
        results,
        input_token_gradient,
        shards[0],
        shards[1],
        shards[2],
        shards[3],
        shards[4],
        shards[5],
        shards[6],
        col_sums[0],
        col_sums[1],
        col_sums[2],
        row_sums[0],
        col_sums[3],
        col_sums[4],
        row_sums[1],
        shards[7],
        shards[8],
        shards[9],
        shards[10],
    )


def solution(mesh):
    in_specs = (
        P(None, None, "dp", None),
        P(None, None, None, "dp", None),
        P(),
        P("dp", "tensor"),
        P("dp", "tensor"),
        P("dp", "tensor"),
        P("tensor", "dp"),
        P("dp", "tensor"),
        P("dp", "tensor"),
        P("tensor", "dp"),
        P("tensor"),
        P("tensor"),
        P("tensor"),
        P(),
        P("tensor"),
        P("tensor"),
        P(),
        P(),
        P(),
        P(),
        P(),
    )
    out_specs = (
        P(None, None, None, "dp", None),
        P(None, None, "dp", None),
        P("dp", "tensor"),
        P("dp", "tensor"),
        P("dp", "tensor"),
        P("tensor", "dp"),
        P("dp", "tensor"),
        P("dp", "tensor"),
        P("tensor", "dp"),
        P("tensor"),
        P("tensor"),
        P("tensor"),
        P("dp"),
        P("tensor"),
        P("tensor"),
        P("dp"),
        P("dp"),
        P("dp"),
        P("dp"),
        P("dp"),
    )
    return jax.shard_map(body, mesh=mesh, in_specs=in_specs, out_specs=out_specs, check_vma=False)
```

profile of v0, /device:TPU:0, one launch (start us, length us, event | category | flops | bytes accessed | tf_op | source)
XLA Modules:
  0.0 1822.9 jit_solution(16056382615619068401)
XLA Ops:
  11.9 27.1 %all_gather.24 = bf16[2304,128]{1,0:T(8,128)(2,1)S(1)} all-gather(bf16[144,128]{1,0:T(8,128)(2,1)S(1)} %convert_element_type.783), channel_id=1, replica_groups=mesh['dp'=16,'tensor'=8] {'dp'}, dimensions={0}, use_global_device_ids=true | all-gather | bytes 626688 | tf_op jit(solution)/shard_map/all_gather | solution.py:159
  47.7 11.5 all-gather.14.cloned.1.call-done
  59.2 4.8 fusion.252
  70.0 3.5 collective-permute-done.1
  75.9 22.9 %all_gather.22 = bf16[2304,128]{1,0:T(8,128)(2,1)S(1)} all-gather(bf16[144,128]{1,0:T(8,128)(2,1)S(1)} %convert_element_type.773), channel_id=1, replica_groups=mesh['dp'=16,'tensor'=8] {'dp'}, dimensions={0}, use_global_device_ids=true | all-gather | bytes 626688 | tf_op jit(solution)/shard_map/all_gather | solution.py:160
  113.9 4.7 fusion.253
  118.6 36.2 %all-gather.26.cloned.1.call-done = bf16[3,1024,1,256]{3,1,0,2:T(8,128)(2,1)} async-done(((bf16[3,64,1,256]{3,1,0,2:T(8,128)(2,1)}), bf16[3,1024,1,256]{3,1,0,2:T(8,128)(2,1)}) %all-gather.26.cloned.1.call-update) | async-done | bytes 1572880 | tf_op jit(solution)/shard_map/all_gather | solution.py:207
  157.2 45.9 %all-gather.12.cloned.1.call-done = bf16[3,1024,1,256]{3,1,0,2:T(8,128)(2,1)} async-done(((bf16[3,64,1,256]{3,1,0,2:T(8,128)(2,1)}), bf16[3,1024,1,256]{3,1,0,2:T(8,128)(2,1)}) %all-gather.12.cloned.1.call-update) | async-done | bytes 1572880 | tf_op jit(solution)/shard_map/all_gather | solution.py:207
  205.6 45.9 %all-gather.24.cloned.1.call-done = bf16[3,1024,1,256]{3,1,0,2:T(8,128)(2,1)} async-done(((bf16[3,64,1,256]{3,1,0,2:T(8,128)(2,1)}), bf16[3,1024,1,256]{3,1,0,2:T(8,128)(2,1)}) %all-gather.24.cloned.1.call-update) | async-done | bytes 1572880 | tf_op jit(solution)/shard_map/all_gather | solution.py:208
  256.2 43.6 %all-gather.10.cloned.1.call-done = bf16[3,1024,1,256]{3,1,0,2:T(8,128)(2,1)} async-done(((bf16[3,64,1,256]{3,1,0,2:T(8,128)(2,1)}), bf16[3,1024,1,256]{3,1,0,2:T(8,128)(2,1)}) %all-gather.10.cloned.1.call-update) | async-done | bytes 1572880 | tf_op jit(solution)/shard_map/all_gather | solution.py:208
  307.8 89.9 %all-reduce.26.cloned.1.call-done = (f32[3,64,2304]{2,1,0:T(8,128)}, f32[3,64,2304]{2,1,0:T(8,128)}) async-done(((f32[3,64,2304]{2,1,0:T(8,128)}, f32[3,64,2304]{2,1,0:T(8,128)}), (f32[3,64,2304]{2,1,0:T(8,128)}, f32[3,64,2304]{2,1,0:T(8,128)})) %all-reduce.26.cloned.1.call-update) | async-done | bytes 3538960 | tf_op jit(solution)/shard_map/psum | solution.py:223
  404.7 55.3 %all-gather.18.cloned.1.call-done = bf16[2304,1152]{1,0:T(8,128)(2,1)} async-done(((bf16[144,1152]{1,0:T(8,128)(2,1)}), bf16[2304,1152]{1,0:T(8,128)(2,1)}) %all-gather.18.cloned.1.call-update) | async-done | bytes 5308432 | tf_op jit(solution)/shard_map/all_gather | solution.py:162
  460.0 19.0 %fusion.93 = (bf16[1,2304,1152]{2,1,0:T(8,128)(2,1)S(1)}, bf16[1,2304,1152]{2,1,0:T(8,128)(2,1)S(1)}, bf16[1,2304,1152]{2,1,0:T(8,128)(2,1)}) fusion(bf16[2304,1152]{1,0:T(8,128)(2,1)} %all-gather.18.cloned.1.call-done, f32[1152]{0:T(1024)S(1)} %copy-done.185), kind=kLoop, calls=%fused_computation.158 | loop fusion | flops 103514112 | bytes 21238272 | tf_op jit(solution)/shard_map/stack | solution.py:70
  479.0 5.9 pad_maximum_fusion
  484.9 4.4 fusion.474
  493.3 28.1 %all-gather.20.cloned.1.call-done = bf16[2304,1152]{1,0:T(8,128)(2,1)} async-done(((bf16[144,1152]{1,0:T(8,128)(2,1)}), bf16[2304,1152]{1,0:T(8,128)(2,1)}) %all-gather.20.cloned.1.call-update) | async-done | bytes 5308432 | tf_op jit(solution)/shard_map/all_gather | solution.py:163
  521.4 17.6 fusion.94
  539.1 5.5 multiply_convert_fusion.20
  544.9 4.2 multiply_convert_fusion.21
  549.0 33.7 %all-gather.22.cloned.1.call-done = bf16[1152,2304]{0,1:T(8,128)(2,1)} async-done(((bf16[1152,144]{0,1:T(8,128)(2,1)}), bf16[1152,2304]{0,1:T(8,128)(2,1)}) %all-gather.22.cloned.1.call-update) | async-done | bytes 5308432 | tf_op jit(solution)/shard_map/all_gather | solution.py:164
  582.7 8.6 copy.119
  591.3 17.5 fusion.95
  610.7 4.1 fusion.475
  616.8 3.5 fusion.473
  621.0 93.1 %all-reduce.24.cloned.1.call-done = (f32[3,64,2304]{2,1,0:T(8,128)}, f32[3,64,2304]{2,1,0:T(8,128)}) async-done(((f32[3,64,2304]{2,1,0:T(8,128)}, f32[3,64,2304]{2,1,0:T(8,128)}), (f32[3,64,2304]{2,1,0:T(8,128)}, f32[3,64,2304]{2,1,0:T(8,128)})) %all-reduce.24.cloned.1.call-update) | async-done | bytes 3538960 | tf_op jit(solution)/shard_map/psum | solution.py:231
  721.0 11.9 multiply_convert_fusion.18
  732.9 11.6 fusion.477
  744.5 11.2 multiply_convert_fusion.19
  755.7 12.0 fusion.476
  767.7 9.8 convolution_add_fusion
  777.6 7.4 convolution_add_fusion.1
  786.6 93.1 %all-reduce.22.cloned.1.call-done = (f32[3,64,2304]{2,1,0:T(8,128)}, f32[3,64,2304]{2,1,0:T(8,128)}) async-done(((f32[3,64,2304]{2,1,0:T(8,128)}, f32[3,64,2304]{2,1,0:T(8,128)}), (f32[3,64,2304]{2,1,0:T(8,128)}, f32[3,64,2304]{2,1,0:T(8,128)})) %all-reduce.22.cloned.1.call-update) | async-done | bytes 3538960 | tf_op jit(solution)/shard_map/psum | solution.py:272
  879.8 4.4 multiply_reduce_fusion.1
  884.4 3.4 multiply_reduce_fusion.2
  887.9 3.5 multiply_reduce_fusion.3
  899.3 3.2 convolution_convert_fusion.2
  906.9 17.7 fusion.471
  926.5 4.2 copy.123
  935.2 17.6 fusion.470
  952.8 4.3 fusion.465
  957.1 4.2 fusion.464
  970.6 69.3 %reduce-scatter.16.cloned.1.call-done = bf16[3,64,1,256]{3,1,0,2:T(8,128)(2,1)} async-done(((bf16[3,1024,1,256]{3,1,0,2:T(8,128)(2,1)}), bf16[3,64,1,256]{3,1,0,2:T(8,128)(2,1)}) %reduce-scatter.16.cloned.1.call-update) | async-done | bytes 98320 | tf_op jit(solution)/shard_map/reduce_scatter | solution.py:305
  1054.7 4.3 fusion.459
  1063.0 130.1 %all-reduce.28.cloned.1.call-done = (bf16[3,1024,1,256]{3,0,2,1:T(4,128)(2,1)}, bf16[3,1024,1,256]{3,0,2,1:T(4,128)(2,1)}) async-done(((bf16[3,1024,1,256]{3,0,2,1:T(4,128)(2,1)}, bf16[3,1024,1,256]{3,0,2,1:T(4,128)(2,1)}), (bf16[3,1024,1,256]{3,0,2,1:T(4,128)(2,1)}, bf16[3,1024,1,256]{3,0,2,1:T(4,128)(2,1)})) %all-reduce.28.cloned.1.call-update) | async-done | bytes 3145744
  1210.6 4.2 fusion.458
  1216.2 10.2 add_convert_fusion
  1226.5 8.6 copy.151
  1236.3 17.3 fusion.469
  1253.6 17.4 fusion.468
  1270.9 17.5 fusion.467
  1288.5 10.0 add_convert_fusion.1
  1299.5 17.4 fusion.466
  1316.9 10.1 add_convert_fusion.2
  1327.0 26.6 %fusion.64 = (f32[2304]{0:T(1024)S(1)}, f32[2304]{0:T(1024)S(1)}, f32[2304]{0:T(1024)S(1)}, f32[2304]{0:T(1024)S(1)}, f32[2304]{0:T(1024)S(1)}, /*index=5*/f32[2304]{0:T(1024)S(1)}) fusion(f32[3,1152,2304]{2,1,0:T(8,128)} %get-tuple-element.346, bf16[1152,2304]{1,0:T(8,128)(2,1)} %copy.119, f32[3,1152,2304]{2,1,0:T(8,128)} %get-tuple-element.348), kind=kLoop, calls=%fused_computation.105 | loop fusion | flops 119425536 | bytes 69064704 | tf_op jit(solution)/shard_map/reduce_sum | solution.py:79
  1353.7 28.1 %fusion.72 = (f32[1152]{0:T(1024)S(1)}, f32[1152]{0:T(1024)S(1)}, f32[1152]{0:T(1024)S(1)}, f32[1152]{0:T(1024)S(1)}, f32[1152]{0:T(1024)S(1)}, /*index=5*/f32[1152]{0:T(1024)S(1)}) fusion(f32[3,2304,1152]{2,1,0:T(8,128)} %get-tuple-element.342, bf16[2304,1152]{1,0:T(8,128)(2,1)} %all-gather.20.cloned.1.call-done, f32[3,2304,1152]{2,1,0:T(8,128)} %get-tuple-element.344), kind=kLoop, calls=%fused_computation.119 | loop fusion | flops 119432448 | bytes 69037056 | tf_op jit(solution)/shard_map/reduce_sum | solution.py:79
  1381.9 27.9 %fusion.80 = (f32[1152]{0:T(1024)S(1)}, f32[1152]{0:T(1024)S(1)}, f32[1152]{0:T(1024)S(1)}, f32[1152]{0:T(1024)S(1)}, f32[1152]{0:T(1024)S(1)}, /*index=5*/f32[1152]{0:T(1024)S(1)}) fusion(f32[3,2304,1152]{2,1,0:T(8,128)} %get-tuple-element.338, bf16[2304,1152]{1,0:T(8,128)(2,1)} %all-gather.18.cloned.1.call-done, f32[3,2304,1152]{2,1,0:T(8,128)} %get-tuple-element.340), kind=kLoop, calls=%fused_computation.133 | loop fusion | flops 119432448 | bytes 69037056 | tf_op jit(solution)/shard_map/reduce_sum | solution.py:79
  1412.0 4.6 fusion.147
  1418.3 7.4 fusion.155
  1431.1 67.5 %all-reduce.8 = (f32[256]{0:T(256)}, f32[128]{0:T(128)}, f32[128]{0:T(128)}, f32[1152]{0:T(1024)}, f32[1152]{0:T(1024)}) all-reduce(f32[256]{0:T(256)S(1)} %add_add_fusion.10, f32[128]{0:T(128)S(1)} %get-tuple-element.354, f32[128]{0:T(128)S(1)} %get-tuple-element.353, ...), channel_id=1, replica_groups=mesh['dp'=16,'tensor'=8] {'dp'}, use_global_device_ids=true, to_apply=%region_65.66 | all-reduce | flops 2816 | bytes 22528 | tf_op jit(solution)/shard_map/psum | solution.py:411
  1505.5 65.2 %all-reduce.13 = (bf16[2304]{0:T(1024)(128)(2,1)S(1)}, bf16[2304]{0:T(1024)(128)(2,1)S(1)}, bf16[2304]{0:T(1024)(128)(2,1)S(1)}, bf16[2304]{0:T(1024)(128)(2,1)S...) all-reduce(bf16[2304]{0:T(1024)(128)(2,1)S(1)} %add_convert_fusion., ...), channel_id=13, replica_groups=mesh['dp'=16,'tensor'=8] {'dp'}, use_global_device_ids=true, to_apply=%region_86.87.clone | all-reduce | flops 13824 | bytes 55296
  1570.7 19.6 %all-reduce.9 = (f32[144]{0:T(256)}, f32[144]{0:T(256)}) all-reduce(f32[144]{0:T(256)S(1)} %get-tuple-element.360, f32[144]{0:T(256)S(1)} %get-tuple-element.359), channel_id=1, replica_groups=mesh['dp'=16,'tensor'=8] {'tensor'}, use_global_device_ids=true, to_apply=%region_87.88 | all-reduce | flops 288 | bytes 2304 | tf_op jit(solution)/shard_map/psum | solution.py:410
  1594.5 42.6 %reduce-scatter.30.cloned.1.call-done = bf16[144,1152]{1,0:T(8,128)(2,1)} async-done(((bf16[2304,1152]{1,0:T(8,128)(2,1)}), bf16[144,1152]{1,0:T(8,128)(2,1)}) %reduce-scatter.30.cloned.1.call-update) | async-done | bytes 331792
  1639.4 85.9 %reduce-scatter.26.cloned.1.call-done = bf16[144,1152]{1,0:T(8,128)(2,1)} async-done(((bf16[2304,1152]{1,0:T(8,128)(2,1)}), bf16[144,1152]{1,0:T(8,128)(2,1)}) %reduce-scatter.26.cloned.1.call-update) | async-done | bytes 331792 | tf_op jit(solution)/shard_map/reduce_scatter | solution.py:385
  1727.2 87.0 %reduce-scatter.24.cloned.1.call-done = bf16[144,1152]{1,0:T(8,128)(2,1)} async-done(((bf16[2304,1152]{1,0:T(8,128)(2,1)}), bf16[144,1152]{1,0:T(8,128)(2,1)}) %reduce-scatter.24.cloned.1.call-update) | async-done | bytes 331792 | tf_op jit(solution)/shard_map/reduce_scatter | solution.py:382
  (642 shorter events, 169.9 us)
Async XLA Ops:
  7.2 52.0 %all-gather.14.cloned.1.call-start = ((), (), s32[]{:S(2)}) async-start(), calls=%async_computation.11 | async-start | bytes 1253376 | tf_op jit(solution)/shard_map/all_gather | solution.py:158
  8.9 103.4 %all-gather.16.cloned.1.call-start = ((), (), s32[]{:S(2)}) async-start(), calls=%async_computation.12 | async-start | bytes 1253376 | tf_op jit(solution)/shard_map/all_gather | solution.py:161
  11.1 89.5 %copy-start.173 = (f32[64]{0:T(128)}, f32[64]{0:T(128)S(1)}, u32[]{:S(2)}) copy-start(f32[64]{0:T(128)S(1)} %fusion.421) | copy-start | bytes 772
  11.8 94.2 %copy-start.97 = (f32[2304]{0:T(1024)}, f32[2304]{0:T(1024)S(1)}, u32[]{:S(2)}) copy-start(f32[2304]{0:T(1024)S(1)} %broadcast_add_fusion.3) | copy-start | bytes 27652
  42.7 5.0 collective-permute-start.3
  44.8 110.0 %all-gather.26.cloned.1.call-start = ((), (), s32[]{:S(2)}) async-start(), calls=%async_computation.17 | async-start | bytes 1671168 | tf_op jit(solution)/shard_map/all_gather | solution.py:207
  65.7 89.1 %copy-start.137 = (bf16[3,64,128]{2,1,0:T(8,128)(2,1)}, bf16[3,64,128]{2,1,0:T(8,128)(2,1)S(1)}, u32[]{:S(2)}) copy-start(bf16[3,64,128]{2,1,0:T(8,128)(2,1)S(1)} %get-tuple-element.279) | copy-start | bytes 147460
  66.4 136.8 %all-gather.12.cloned.1.call-start = ((), (), s32[]{:S(2)}) async-start(), calls=%async_computation.10 | async-start | bytes 1671168 | tf_op jit(solution)/shard_map/all_gather | solution.py:207
  68.5 5.0 collective-permute-start.1
  75.8 175.7 %all-gather.24.cloned.1.call-start = ((), (), s32[]{:S(2)}) async-start(), calls=%async_computation.16 | async-start | bytes 1671168 | tf_op jit(solution)/shard_map/all_gather | solution.py:208
  101.1 4.2 collective-permute-start.2
  106.0 193.9 %all-gather.10.cloned.1.call-start = ((), (), s32[]{:S(2)}) async-start(), calls=%async_computation.9 | async-start | bytes 1671168 | tf_op jit(solution)/shard_map/all_gather | solution.py:208
  106.5 4.2 collective-permute-start
  111.4 286.4 %all-reduce.26.cloned.1.call-start = ((), (), s32[]{:S(2)}) async-start(), calls=%async_computation.29 | async-start | bytes 7077888 | tf_op jit(solution)/shard_map/psum | solution.py:223
  112.2 139.3 %copy-start.79 = (pred[64,1024]{1,0:T(8,128)(4,1)}, pred[64,1024]{1,0:T(8,128)(4,1)S(1)}, u32[]{:S(2)}) copy-start(pred[64,1024]{1,0:T(8,128)(4,1)S(1)} %get-tuple-element.301) | copy-start | bytes 196612
  112.2 187.7 %copy-start.81 = (pred[64,1024]{1,0:T(8,128)(4,1)}, pred[64,1024]{1,0:T(8,128)(4,1)S(1)}, u32[]{:S(2)}) copy-start(pred[64,1024]{1,0:T(8,128)(4,1)S(1)} %get-tuple-element.302) | copy-start | bytes 196612
  118.6 183.4 %copy-start.41 = (bf16[1,256,2304]{2,1,0:T(8,128)(2,1)}, bf16[1,256,2304]{2,1,0:T(8,128)(2,1)S(1)}, u32[]{:S(2)}) copy-start(bf16[1,256,2304]{2,1,0:T(8,128)(2,1)S(1)} %get-tuple-element.255) | copy-start | bytes 3538948
  156.9 96.6 %copy-start.34 = (f32[3,1024,64]{1,2,0:T(8,128)}, f32[3,1024,64]{1,2,0:T(8,128)S(1)}, u32[]{:S(2)}) copy-start(f32[3,1024,64]{1,2,0:T(8,128)S(1)} %get-tuple-element.312) | copy-start | bytes 2359300
  156.9 96.6 %copy-start.187 = (f32[3,64]{1,0:T(4,128)}, f32[3,64]{1,0:T(4,128)S(1)}, u32[]{:S(2)}) copy-start(f32[3,64]{1,0:T(4,128)S(1)} %get-tuple-element.311) | copy-start | bytes 2308
  157.2 96.3 %copy-start.189 = (f32[3,64]{1,0:T(4,128)}, f32[3,64]{1,0:T(4,128)S(1)}, u32[]{:S(2)}) copy-start(f32[3,64]{1,0:T(4,128)S(1)} %fusion.321) | copy-start | bytes 2308
  205.3 94.6 %copy-start.36 = (f32[3,1024,64]{1,2,0:T(8,128)}, f32[3,1024,64]{1,2,0:T(8,128)S(1)}, u32[]{:S(2)}) copy-start(f32[3,1024,64]{1,2,0:T(8,128)S(1)} %get-tuple-element.310) | copy-start | bytes 2359300
  205.3 94.6 %copy-start.191 = (f32[3,64]{1,0:T(4,128)}, f32[3,64]{1,0:T(4,128)S(1)}, u32[]{:S(2)}) copy-start(f32[3,64]{1,0:T(4,128)S(1)} %get-tuple-element.309) | copy-start | bytes 2308
  205.6 94.3 %copy-start.192 = (f32[3,64]{1,0:T(4,128)}, f32[3,64]{1,0:T(4,128)S(1)}, u32[]{:S(2)}) copy-start(f32[3,64]{1,0:T(4,128)S(1)} %fusion.320) | copy-start | bytes 2308
  304.0 156.0 %all-gather.18.cloned.1.call-start = ((), (), s32[]{:S(2)}) async-start(), calls=%async_computation.13 | async-start | bytes 5640192 | tf_op jit(solution)/shard_map/all_gather | solution.py:162
  305.9 215.5 %all-gather.20.cloned.1.call-start = ((), (), s32[]{:S(2)}) async-start(), calls=%async_computation.14 | async-start | bytes 5640192 | tf_op jit(solution)/shard_map/all_gather | solution.py:163
  306.7 276.0 %all-gather.22.cloned.1.call-start = ((), (), s32[]{:S(2)}) async-start(), calls=%async_computation.15 | async-start | bytes 5640192 | tf_op jit(solution)/shard_map/all_gather | solution.py:164
  307.6 406.5 %all-reduce.24.cloned.1.call-start = ((), (), s32[]{:S(2)}) async-start(), calls=%async_computation.28 | async-start | bytes 7077888 | tf_op jit(solution)/shard_map/psum | solution.py:231
  307.8 95.4 %copy-start.26 = (f32[64,2304]{1,0:T(8,128)}, f32[64,2304]{1,0:T(8,128)S(1)}, u32[]{:S(2)}) copy-start(f32[64,2304]{1,0:T(8,128)S(1)} %get-tuple-element.270) | copy-start | bytes 1769476
  307.8 95.4 %copy-start.28 = (f32[64,2304]{1,0:T(8,128)}, f32[64,2304]{1,0:T(8,128)S(1)}, u32[]{:S(2)}) copy-start(f32[64,2304]{1,0:T(8,128)S(1)} %get-tuple-element.269) | copy-start | bytes 1769476
  307.8 95.4 %copy-start.103 = (f32[2304]{0:T(1024)}, f32[2304]{0:T(1024)S(1)}, u32[]{:S(2)}) copy-start(f32[2304]{0:T(1024)S(1)} %broadcast_add_fusion.2) | copy-start | bytes 27652
  307.8 95.4 %copy-start.119 = (f32[2304]{0:T(1024)}, f32[2304]{0:T(1024)S(1)}, u32[]{:S(2)}) copy-start(f32[2304]{0:T(1024)S(1)} %broadcast_add_fusion.1) | copy-start | bytes 27652
  404.7 134.4 %copy-start.4 = (bf16[3,64,2304]{2,1,0:T(8,128)(2,1)}, bf16[3,64,2304]{2,1,0:T(8,128)(2,1)S(1)}, u32[]{:S(2)}) copy-start(bf16[3,64,2304]{2,1,0:T(8,128)(2,1)S(1)} %get-tuple-element.295) | copy-start | bytes 2654212
  404.7 139.9 %copy-start.2 = (bf16[3,64,2304]{2,1,0:T(8,128)(2,1)}, bf16[3,64,2304]{2,1,0:T(8,128)(2,1)S(1)}, u32[]{:S(2)}) copy-start(bf16[3,64,2304]{2,1,0:T(8,128)(2,1)S(1)} %get-tuple-element.296) | copy-start | bytes 2654212
  620.3 97.4 %copy-start.23 = (bf16[3,2,64,1,2304]{4,2,3,1,0:T(8,128)(2,1)S(1)}, bf16[3,2,64,1,2304]{4,2,3,1,0:T(8,128)(2,1)}, u32[]{:S(2)}) copy-start(bf16[3,2,64,1,2304]{4,2,3,1,0:T(8,128)(2,1)} %param.22) | copy-start | bytes 5308420
  620.3 259.4 %all-reduce.22.cloned.1.call-start = ((), (), s32[]{:S(2)}) async-start(), calls=%async_computation.27 | async-start | bytes 7077888 | tf_op jit(solution)/shard_map/psum | solution.py:272
  621.0 98.4 %copy-start.121 = (f32[2304]{0:T(1024)}, f32[2304]{0:T(1024)S(1)}, u32[]{:S(2)}) copy-start(f32[2304]{0:T(1024)S(1)} %broadcast_add_fusion) | copy-start | bytes 27652
  785.0 94.6 %copy-start.7 = (f32[3,64,2304]{2,1,0:T(8,128)S(1)}, f32[3,64,2304]{2,1,0:T(8,128)}, u32[]{:S(2)}) copy-start(f32[3,64,2304]{2,1,0:T(8,128)} %get-tuple-element.224) | copy-start | bytes 5308420
  785.0 94.6 %copy-start.9 = (f32[3,64,2304]{2,1,0:T(8,128)S(1)}, f32[3,64,2304]{2,1,0:T(8,128)}, u32[]{:S(2)}) copy-start(f32[3,64,2304]{2,1,0:T(8,128)} %get-tuple-element.225) | copy-start | bytes 5308420
  785.0 94.6 %copy-start.104 = (f32[2304]{0:T(1024)S(1)}, f32[2304]{0:T(1024)}, u32[]{:S(2)}) copy-start(f32[2304]{0:T(1024)} %copy-done.103) | copy-start | bytes 27652
  785.0 94.6 %copy-start.147 = (f32[3,64]{1,0:T(4,128)S(1)}, f32[3,64]{1,0:T(4,128)}, u32[]{:S(2)}) copy-start(f32[3,64]{1,0:T(4,128)} %copy-done.146) | copy-start | bytes 2308
  785.1 182.3 %reduce-scatter.14.cloned.1.call-start = ((), (), s32[]{:S(2)}) async-start(), calls=%async_computation.18 | async-start | bytes 1671168 | tf_op jit(solution)/shard_map/reduce_scatter | solution.py:305
  899.0 140.9 %reduce-scatter.16.cloned.1.call-start = ((), (), s32[]{:S(2)}) async-start(), calls=%async_computation.19 | async-start | bytes 1671168 | tf_op jit(solution)/shard_map/reduce_scatter | solution.py:305
  905.5 287.6 %all-reduce.28.cloned.1.call-start = ((), (), s32[]{:S(2)}) async-start(), calls=%async_computation.30 | async-start | bytes 8388608
  934.0 482.6 %reduce-scatter.28.cloned.1.call-start = ((), (), s32[]{:S(2)}) async-start(), calls=%async_computation.25 | async-start | bytes 1253376
  963.0 79.4 %copy-start.128 = (f32[64,128]{1,0:T(8,128)S(1)}, f32[64,128]{1,0:T(8,128)}, u32[]{:S(2)}) copy-start(f32[64,128]{1,0:T(8,128)} %copy-done.127) | copy-start | bytes 98308
  963.0 79.4 %copy-start.130 = (f32[64,128]{1,0:T(8,128)S(1)}, f32[64,128]{1,0:T(8,128)}, u32[]{:S(2)}) copy-start(f32[64,128]{1,0:T(8,128)} %copy-done.129) | copy-start | bytes 98308
  963.0 79.5 %copy-start.91 = (bf16[1,2304,256]{2,1,0:T(8,128)(2,1)S(1)}, bf16[1,2304,256]{2,1,0:T(8,128)(2,1)}, u32[]{:S(2)}) copy-start(bf16[1,2304,256]{2,1,0:T(8,128)(2,1)} %copy-done.90) | copy-start | bytes 3538948
  963.0 535.6 %reduce-scatter.20.cloned.1.call-start = ((), (), s32[]{:S(2)}) async-start(), calls=%async_computation.21 | async-start | bytes 626688 | tf_op jit(solution)/shard_map/reduce_scatter | solution.py:373
  967.3 74.2 %collective-permute-start.4 = (bf16[3,64,1,256]{3,1,0,2:T(8,128)(2,1)}, bf16[3,64,1,256]{3,1,0,2:T(8,128)(2,1)S(1)}, u32[]{:S(2)}, u32[]{:S(2)}) collective-permute-start(bf16[3,64,1,256]{3,1,0,2:T(8,128)(2,1)} %reduce-scatter.14.cloned.1.call-done), channel_id=1, source_target_pairs={{0,1},{1,0},{2,3},{3,2},{4,5},{5,4},{6,7},{7,6},{8,9},{9,8},{10,11... | collective-permute-start | bytes 294920 | tf_op jit(solution)/shard_map/ppermute | solution.py:19
  1039.9 5.7 collective-permute-start.6
  1060.0 440.1 %all-reduce.30.cloned.1.call-start = ((), (), s32[]{:S(2)}) async-start(), calls=%async_computation.31 | async-start | bytes 1179648 | tf_op jit(solution)/shard_map/psum | solution.py:349
  1194.1 5.7 collective-permute-start.5
  1196.8 6.0 collective-permute-start.7
  1204.3 387.3 %reduce-scatter.22.cloned.1.call-start = ((), (), s32[]{:S(2)}) async-start(), calls=%async_computation.22 | async-start | bytes 626688 | tf_op jit(solution)/shard_map/reduce_scatter | solution.py:376
  1210.5 382.4 %reduce-scatter.18.cloned.1.call-start = ((), (), s32[]{:S(2)}) async-start(), calls=%async_computation.20 | async-start | bytes 1253376 | tf_op jit(solution)/shard_map/reduce_scatter | solution.py:370
  1216.2 421.0 %reduce-scatter.30.cloned.1.call-start = ((), (), s32[]{:S(2)}) async-start(), calls=%async_computation.26 | async-start | bytes 5640192
  1235.0 490.3 %reduce-scatter.26.cloned.1.call-start = ((), (), s32[]{:S(2)}) async-start(), calls=%async_computation.24 | async-start | bytes 5640192 | tf_op jit(solution)/shard_map/reduce_scatter | solution.py:385
  1298.5 515.6 %reduce-scatter.24.cloned.1.call-start = ((), (), s32[]{:S(2)}) async-start(), calls=%async_computation.23 | async-start | bytes 5640192 | tf_op jit(solution)/shard_map/reduce_scatter | solution.py:382
  1429.0 71.1 %copy-start.175 = (f32[64]{0:T(128)S(1)}, f32[64]{0:T(128)}, u32[]{:S(2)}) copy-start(f32[64]{0:T(128)} %copy-done.173) | copy-start | bytes 772
  1429.0 71.1 %copy-start.179 = (f32[64]{0:T(128)S(1)}, f32[64]{0:T(128)}, u32[]{:S(2)}) copy-start(f32[64]{0:T(128)} %copy-done.176) | copy-start | bytes 772
  1429.0 72.7 %copy-start.195 = (f32[64]{0:T(128)S(1)}, f32[64]{0:T(128)}, u32[]{:S(2)}) copy-start(f32[64]{0:T(128)} %copy-done.194) | copy-start | bytes 772
  1429.0 72.7 %copy-start.197 = (f32[64]{0:T(128)S(1)}, f32[64]{0:T(128)}, u32[]{:S(2)}) copy-start(f32[64]{0:T(128)} %copy-done.196) | copy-start | bytes 772
  1429.0 72.7 %copy-start.77 = (f32[64,2304]{1,0:T(8,128)S(1)}, f32[64,2304]{1,0:T(8,128)}, u32[]{:S(2)}) copy-start(f32[64,2304]{1,0:T(8,128)} %get-tuple-element.185) | copy-start | bytes 1769476
  1429.0 72.7 %copy-start.78 = (f32[64,2304]{1,0:T(8,128)S(1)}, f32[64,2304]{1,0:T(8,128)}, u32[]{:S(2)}) copy-start(f32[64,2304]{1,0:T(8,128)} %get-tuple-element.186) | copy-start | bytes 1769476
  (177 other events, 1700.5 us)
Sparse Core Ops, SparseCore 0:
  11.0 48.1 all-gather.13
  62.2 44.1 all-gather.15
  108.9 45.9 all-gather.25
  157.7 45.4 all-gather.11
  206.1 45.4 all-gather.23
  254.4 45.4 all-gather.9
  304.1 93.5 all-reduce.25
  400.4 59.5 all-gather.17
  462.6 58.8 all-gather.19
  523.9 58.8 all-gather.21
  620.4 93.6 all-reduce.23
  785.2 94.4 all-reduce.21
  899.1 68.1 reduce-scatter.13
  972.1 67.7 reduce-scatter.15
  1042.4 150.6 all-reduce.27
  1197.3 67.9 reduce-scatter.27
  1268.9 63.1 reduce-scatter.19
  1335.1 74.4 all-reduce.29
  1413.9 63.7 reduce-scatter.21
  1481.4 66.4 reduce-scatter.17
  1552.8 84.3 reduce-scatter.29
  1641.4 83.8 reduce-scatter.25
  1730.1 83.9 reduce-scatter.23
where the time goes:
time: 1830 us; the launch traced here: 1820 us
  waiting for transfers between devices  1010 us (55%)
  matrix products  267 us (15%)
  other arithmetic  262 us (14%)
  blocking collectives  202 us (11%)
  local copies, waits for them, and re-layouts  52.5 us (3%)
  between operations  18.5 us (1%)
    unnamed x26, waiting for transfers between devices  173 us
    reduce_sum x7, other arithmetic, weight_terms(): jnp.sum(per_width[width_id] * level_widths(whole, SHIFTS[width_id]), axis=0)  98.7 us
    psum x1, waiting for transfers between devices, body(): d_normed_middle = lax.psum(d_normed_middle, 'tensor')  93.1 us
    psum x1, waiting for transfers between devices, body(): lax.psum(jnp.einsum('wrc,wcd->wrd', hidden, w_down, preferred_element_typ...  93.1 us
    psum x1, waiting for transfers between devices, body(): lax.psum(jnp.einsum('wrc,wcd->wrd', attended, w_out, preferred_element_ty...  89.9 us
    all_gather x2, waiting for transfers between devices, body(): lax.all_gather(value_here, 'dp', axis=1, tiled=True)  89.5 us
    reduce_scatter x1, waiting for transfers between devices, body(): lax.psum_scatter(totals[4].astype(jnp.bfloat16), 'dp', scatter_dimension=...  87 us
    reduce_scatter x1, waiting for transfers between devices, body(): lax.psum_scatter(totals[5].astype(jnp.bfloat16), 'dp', scatter_dimension=...  85.9 us
  transfers between devices with their start and end apart: 31, of which 22 were waited for; matrix products, arithmetic and copies ran while one was open for 24% of the time, Pallas kernels for 0%

commit v1 on v0

v1 whole, which is shorter than its diff:
```python
import functools

import jax
import jax.numpy as jnp
from jax import lax
from jax.experimental import pallas as pl
from jax.experimental.pallas import tpu as pltpu
from jax.sharding import PartitionSpec as P

MESH = pl.DeviceIdType.MESH
F32 = jnp.float32
B16 = jnp.bfloat16
EPSILON = 1e-06
SOFTCAP = 50.0
ROPE_BASE = 10000.0
MASKED = -1e30
HD = 256
WIDE = 2304
SHARD = 144
LOW = 64
HIGH = SHARD - LOW
TENSOR = 8
ROWS = 128
SLICE = ROWS // TENSOR
VMEM_BYTES = 56 * 2**20


def here():
    dp = lax.axis_index("dp")
    return lax.div(dp, 4), lax.rem(lax.div(dp, 2), 2), lax.rem(dp, 2), lax.axis_index("tensor")


def rank(y, z_hi, core):
    return (y * 2 + z_hi) * 2 + core


def remote(src, dst, send, recv, dp, tensor):
    return pltpu.make_async_remote_copy(
        src, dst, send, recv, device_id=(dp, tensor), device_id_type=MESH
    )


def greet(devices):
    barrier = pltpu.get_barrier_semaphore()
    for device in devices:
        pl.semaphore_signal(barrier, inc=1, device_id=device, device_id_type=MESH)
    pl.semaphore_wait(barrier, len(devices))


def any_space(count):
    return [pl.BlockSpec(memory_space=pl.ANY)] * count


def vmem_space(count):
    return [pl.BlockSpec(memory_space=pltpu.VMEM)] * count


def params(collective_id):
    return pltpu.CompilerParams(
        collective_id=collective_id, has_side_effects=True, vmem_limit_bytes=VMEM_BYTES
    )


def gather_kernel(count, *refs):
    srcs, outs = refs[:count], refs[count : 2 * count]
    send, recv, local = refs[2 * count :]
    y, zh, core, t = here()
    me, sib, zz = rank(y, zh, core), rank(y, zh, 1 - core), rank(y, 1 - zh, core)
    fore = [rank(lax.rem(y + dy, 4), zh, core) for dy in (1, 2, 3)]
    behind = [lax.rem(y + 4 - dy, 4) for dy in (1, 2, 3)]
    low, high = pl.ds(0, LOW), pl.ds(LOW, HIGH)
    greet([(sib, t), (zz, t)] + [(dp, t) for dp in fore])
    started = []

    def push(k, slot, src, dst, dp):
        copy = remote(src, dst, send.at[k, slot], recv.at[k, slot], dp, t)
        copy.start()
        started.append(copy)

    def arrive(k, slot, ref):
        remote(ref, ref, send.at[k, slot], recv.at[k, slot], sib, t).wait_recv()

    mine = []
    for k in range(count):
        src, out = srcs[k], outs[k]
        copy = pltpu.make_async_copy(src, out.at[me], local.at[k])
        copy.start()
        mine.append(copy)
        push(k, 0, src.at[low], out.at[me, low], zz)
        for i in range(3):
            push(k, 4 + i, src.at[high], out.at[me, high], fore[i])
        for i in range(3):
            push(k, 1 + i, src.at[low], out.at[me, low], fore[i])
        push(k, 7, src.at[high], out.at[me, high], zz)
        push(k, 14, src, out.at[me], sib)
    for k in range(count):
        out = outs[k]
        block = out.at[zz, low]
        arrive(k, 0, block)
        for i in range(3):
            push(k, 8 + i, block, block, fore[i])
        push(k, 15, block, block, sib)
        for i in range(3):
            block = out.at[rank(behind[i], zh, core), high]
            arrive(k, 4 + i, block)
            push(k, 11 + i, block, block, zz)
            push(k, 16 + i, block, block, sib)
        for i in range(3):
            block = out.at[rank(behind[i], zh, core), low]
            arrive(k, 1 + i, block)
            push(k, 19 + i, block, block, sib)
        block = out.at[zz, high]
        arrive(k, 7, block)
        push(k, 22, block, block, sib)
        for i in range(3):
            block = out.at[rank(behind[i], 1 - zh, core), low]
            arrive(k, 8 + i, block)
            push(k, 23 + i, block, block, sib)
            block = out.at[rank(behind[i], 1 - zh, core), high]
            arrive(k, 11 + i, block)
            push(k, 26 + i, block, block, sib)
    for k in range(count):
        out = outs[k]
        zz_sib = rank(y, 1 - zh, 1 - core)
        arrive(k, 14, out.at[sib])
        arrive(k, 15, out.at[zz_sib, low])
        arrive(k, 22, out.at[zz_sib, high])
        for i in range(3):
            near, far = rank(behind[i], zh, 1 - core), rank(behind[i], 1 - zh, 1 - core)
            arrive(k, 16 + i, out.at[near, high])
            arrive(k, 19 + i, out.at[near, low])
            arrive(k, 23 + i, out.at[far, low])
            arrive(k, 26 + i, out.at[far, high])
    for copy in mine:
        copy.wait()
    for copy in started:
        copy.wait_send()


def gather_weights(shards):
    count = len(shards)
    return pl.pallas_call(
        functools.partial(gather_kernel, count),
        name="gather_weights",
        out_shape=[jax.ShapeDtypeStruct((16,) + s.shape, s.dtype) for s in shards],
        in_specs=any_space(count),
        out_specs=any_space(count),
        scratch_shapes=[
            pltpu.SemaphoreType.DMA((count, 29)),
            pltpu.SemaphoreType.DMA((count, 29)),
            pltpu.SemaphoreType.DMA((count,)),
        ],
        compiler_params=params(1),
    )(*shards)


def scatter_kernel(count, *refs):
    parts, outs = refs[:count], refs[count : 2 * count]
    own, sibs, yrecv, zrecv, ylast, zlast = (
        refs[(2 + i) * count : (3 + i) * count] for i in range(6)
    )
    send, recv, local = refs[8 * count :]
    y, zh, core, t = here()
    sib, zz = rank(y, zh, 1 - core), rank(y, 1 - zh, core)
    ahead = [lax.rem(y + dy, 4) for dy in (1, 2, 3)]
    fore = [rank(place, zh, core) for place in ahead]
    greet([(sib, t), (zz, t)] + [(dp, t) for dp in fore])
    started = []

    def push(k, slot, src, dst, dp):
        copy = remote(src, dst, send.at[k, slot], recv.at[k, slot], dp, t)
        copy.start()
        started.append(copy)

    def arrive(k, slot, ref):
        remote(ref, ref, send.at[k, slot], recv.at[k, slot], sib, t).wait_recv()

    order = ahead + [y]
    for k in range(count):
        for i, place in enumerate(order):
            pair = pl.ds(place * 2, 2)
            back = lax.rem(y + 4 - (i + 1), 4)
            push(k, i, parts[k].at[pair, 1 - core], sibs[k].at[pair], sib)
            pltpu.make_async_copy(
                parts[k].at[pair, core], own[k].at[pair], local.at[k, i]
            ).start()
    for k in range(count):
        for i, place in enumerate(order):
            pair = pl.ds(place * 2, 2)
            pltpu.make_async_copy(
                parts[k].at[pair, core], own[k].at[pair], local.at[k, i]
            ).wait()
            arrive(k, i, sibs[k].at[pair])

            def add(step, _, k=k, place=place):
                chip = place * 2 + lax.div(step, SHARD // 16)
                rows = pl.ds(pl.multiple_of(lax.rem(step, SHARD // 16) * 16, 16), 16)
                own[k][chip, rows] = (
                    own[k][chip, rows].astype(F32) + sibs[k][chip, rows].astype(F32)
                ).astype(B16)
                return 0

            lax.fori_loop(0, 2 * SHARD // 16, add, 0)
            if i < 3:
                push(k, 4 + i, own[k].at[pair, pl.ds(0, LOW)], yrecv[k].at[i], fore[i])
            push(
                k, 7 + i, own[k].at[place * 2 + 1 - zh, pl.ds(LOW, HIGH)], zrecv[k].at[place], zz
            )
    for k in range(count):
        for i, place in enumerate(order):
            arrive(k, 7 + i, zrecv[k].at[place])

            def merge(step, _, k=k, place=place):
                rows = pl.ds(pl.multiple_of(step * 16, 16), 16)
                mine = pl.ds(pl.multiple_of(step * 16 + LOW, 16), 16)
                zrecv[k][place, rows] = (
                    zrecv[k][place, rows].astype(F32) + own[k][place * 2 + zh, mine].astype(F32)
                ).astype(B16)
                return 0

            lax.fori_loop(0, HIGH // 16, merge, 0)
            if i < 3:
                push(k, 11 + i, zrecv[k].at[place], ylast[k].at[i], fore[i])
        for i in range(3):
            arrive(k, 4 + i, yrecv[k].at[i])

        def pool(step, _, k=k):
            chip = lax.div(step, LOW // 16)
            rows = pl.ds(pl.multiple_of(lax.rem(step, LOW // 16) * 16, 16), 16)
            total = own[k][y * 2 + chip, rows].astype(F32)
            for i in range(3):
                total = total + yrecv[k][i, chip, rows].astype(F32)
            own[k][y * 2 + chip, rows] = total.astype(B16)
            return 0

        lax.fori_loop(0, 2 * LOW // 16, pool, 0)
        push(k, 14, own[k].at[y * 2 + 1 - zh, pl.ds(0, LOW)], zlast[k], zz)
    for k in range(count):
        arrive(k, 14, zlast[k])

        def end_low(step, _, k=k):
            rows = pl.ds(pl.multiple_of(step * 16, 16), 16)
            outs[k][rows] = own[k][y * 2 + zh, rows].astype(F32) + zlast[k][rows].astype(F32)
            return 0

        lax.fori_loop(0, LOW // 16, end_low, 0)
        for i in range(3):
            arrive(k, 11 + i, ylast[k].at[i])

        def end_high(step, _, k=k):
            rows = pl.ds(pl.multiple_of(step * 16, 16), 16)
            total = zrecv[k][y, rows].astype(F32)
            for i in range(3):
                total = total + ylast[k][i, rows].astype(F32)
            outs[k][pl.ds(pl.multiple_of(step * 16 + LOW, 16), 16)] = total
            return 0

        lax.fori_loop(0, HIGH // 16, end_high, 0)
    for copy in started:
        copy.wait_send()


def scatter_gradients(parts):
    count = len(parts)
    columns = [part.shape[-1] for part in parts]
    scratch = [pltpu.VMEM((8, SHARD, c), B16) for c in columns]
    scratch += [pltpu.VMEM((8, SHARD, c), B16) for c in columns]
    scratch += [pltpu.VMEM((3, 2, LOW, c), B16) for c in columns]
    scratch += [pltpu.VMEM((4, HIGH, c), B16) for c in columns]
    scratch += [pltpu.VMEM((3, HIGH, c), B16) for c in columns]
    scratch += [pltpu.VMEM((LOW, c), B16) for c in columns]
    return pl.pallas_call(
        functools.partial(scatter_kernel, count),
        name="scatter_gradients",
        out_shape=[jax.ShapeDtypeStruct((SHARD, c), F32) for c in columns],
        in_specs=any_space(count),
        out_specs=vmem_space(count),
        scratch_shapes=scratch
        + [
            pltpu.SemaphoreType.DMA((count, 15)),
            pltpu.SemaphoreType.DMA((count, 15)),
            pltpu.SemaphoreType.DMA((count, 4)),
        ],
        compiler_params=params(2),
    )(*[part.reshape(8, 2, SHARD, part.shape[-1]) for part in parts])


def row_block(index):
    return pl.ds(pl.multiple_of(index * SLICE, SLICE), SLICE)


def tensor_peers():
    t = lax.axis_index("tensor")
    return [lax.rem(t + k, TENSOR) for k in range(TENSOR)]


def greet_tensor():
    dp = lax.axis_index("dp")
    greet([(dp, peer) for peer in tensor_peers()[1:]])


def scatter_rows(part, held, send, recv, local):
    dp = lax.axis_index("dp")
    peers = tensor_peers()
    copies = []
    for k in range(1, TENSOR):
        copy = remote(
            part.at[:, row_block(peers[k])], held.at[k], send.at[k], recv.at[k], dp, peers[k]
        )
        copy.start()
        copies.append(copy)
    mine = pltpu.make_async_copy(part.at[:, row_block(peers[0])], held.at[0], local)
    mine.start()
    mine.wait()
    return copies


def summed(held, copies):
    total = held[0].astype(F32)
    for k in range(1, TENSOR):
        copies[k - 1].wait_recv()
        total = total + held[k].astype(F32)
    return total


def spread_rows(block, whole, send, recv, local):
    dp = lax.axis_index("dp")
    peers = tensor_peers()
    here_rows = whole.at[:, row_block(peers[0])]
    copies = []
    for k in range(1, TENSOR):
        copy = remote(block, here_rows, send.at[k], recv.at[k], dp, peers[k])
        copy.start()
        copies.append(copy)
    mine = pltpu.make_async_copy(block, here_rows, local)
    mine.start()

    def finish():
        mine.wait()
        for k in range(1, TENSOR):
            source = whole.at[:, row_block(peers[TENSOR - k])]
            remote(source, source, send.at[k], recv.at[k], dp, peers[k]).wait_recv()
        for copy in copies:
            copy.wait_send()

    return finish


def inverse_rms(signal):
    return lax.rsqrt(jnp.mean(signal * signal, axis=-1, keepdims=True) + EPSILON)


def norm_back(normed, inverse, gain, upstream):
    inner = upstream * (1.0 + gain)
    return inverse * (inner - normed * jnp.mean(inner * normed, axis=-1, keepdims=True))


def over_rows(term):
    return jnp.sum(term, axis=(0, 1))[None]


def load_rows(whole, block, local):
    copy = pltpu.make_async_copy(
        whole.at[:, row_block(lax.axis_index("tensor"))], block, local
    )
    copy.start()
    return copy


def middle_kernel(
    part, tokens, gains, normed, branch, middle, held, mine, block, send, recv, local
):
    greet_tensor()
    copies = scatter_rows(part, held, send.at[0], recv.at[0], local.at[0])
    load = load_rows(tokens, mine, local.at[1])
    load.wait()
    signal = summed(held, copies)
    branch[...] = signal
    total = mine[...].astype(F32) + signal * inverse_rms(signal) * (1.0 + gains[1:2])
    middle[...] = total
    block[...] = (total * inverse_rms(total) * (1.0 + gains[2:3])).astype(B16)
    finish = spread_rows(block, normed, send.at[1], recv.at[1], local.at[2])
    for copy in copies:
        copy.wait_send()
    finish()


def feed_kernel(
    part, cotangent, middle, gains, d_feed, results, sums, held, mine, block, final, send, recv, local
):
    greet_tensor()
    copies = scatter_rows(part, held, send.at[0], recv.at[0], local.at[0])
    load = load_rows(cotangent, mine, local.at[1])
    load.wait()
    signal = summed(held, copies)
    inverse = inverse_rms(signal)
    normed = signal * inverse
    upstream = mine[...].astype(F32)
    lowered = norm_back(normed, inverse, gains[3:4], upstream).astype(B16)
    block[...] = lowered
    finish = spread_rows(block, d_feed, send.at[1], recv.at[1], local.at[2])
    final[...] = (middle[...] + normed * (1.0 + gains[3:4])).astype(B16)
    finish_results = spread_rows(final, results, send.at[2], recv.at[2], local.at[3])
    sums[0:1] = over_rows(upstream * normed)
    sums[1:2] = over_rows(lowered.astype(F32) * signal)
    for copy in copies:
        copy.wait_send()
    finish()
    finish_results()


def branch_kernel(
    part, cotangent, middle, branch, gains, d_branch, d_middle, sums, held, mine, block, send, recv, local
):
    greet_tensor()
    copies = scatter_rows(part, held, send.at[0], recv.at[0], local.at[0])
    load = load_rows(cotangent, mine, local.at[1])
    load.wait()
    upstream = summed(held, copies)
    signal = middle[...]
    inverse = inverse_rms(signal)
    normed = signal * inverse
    gradient = mine[...].astype(F32) + norm_back(normed, inverse, gains[2:3], upstream)
    lower = branch[...]
    inverse_lower = inverse_rms(lower)
    normed_lower = lower * inverse_lower
    lowered = norm_back(normed_lower, inverse_lower, gains[1:2], gradient).astype(B16)
    block[...] = lowered
    finish = spread_rows(block, d_branch, send.at[1], recv.at[1], local.at[2])
    d_middle[...] = jnp.sum(gradient, axis=0, keepdims=True)
    sums[0:1] = over_rows(upstream * normed)
    sums[1:2] = over_rows(gradient * normed_lower)
    sums[2:3] = over_rows(lowered.astype(F32) * lower)
    for copy in copies:
        copy.wait_send()
    finish()


def input_kernel(
    part, tokens, d_middle, gains, gradient, sums, held, mine, block, send, recv, local
):
    greet_tensor()
    copies = scatter_rows(part, held, send.at[0], recv.at[0], local.at[0])
    load = load_rows(tokens, mine, local.at[1])
    load.wait()
    upstream = summed(held, copies)
    signal = mine[...].astype(F32)
    inverse = inverse_rms(signal)
    normed = signal * inverse
    block[...] = d_middle[...] + norm_back(normed, inverse, gains[0:1], upstream)
    finish = spread_rows(block, gradient, send.at[1], recv.at[1], local.at[2])
    sums[0:1] = over_rows(upstream * normed)
    for copy in copies:
        copy.wait_send()
    finish()


def tensor_call(
    kernel, name, collective_id, depth, loaded, operands, in_specs, outs, out_specs, blocks
):
    return pl.pallas_call(
        kernel,
        name=name,
        out_shape=outs,
        in_specs=in_specs,
        out_specs=out_specs,
        scratch_shapes=[
            pltpu.VMEM((TENSOR, depth, SLICE, WIDE), B16),
            pltpu.VMEM((loaded, SLICE, WIDE), B16),
        ]
        + blocks
        + [
            pltpu.SemaphoreType.DMA((3, TENSOR)),
            pltpu.SemaphoreType.DMA((3, TENSOR)),
            pltpu.SemaphoreType.DMA((4,)),
        ],
        compiler_params=params(collective_id),
    )(*operands)


def struct(shape, dtype):
    return jax.ShapeDtypeStruct(shape, dtype)


def unit_owner(micro, width):
    return rank(width, micro, 0)


def rotate(signal, cosine, sine):
    former, latter = signal[:, : HD // 2], signal[:, HD // 2 :]
    return jnp.concatenate([former * cosine - latter * sine, latter * cosine + former * sine], -1)


def unrotate(signal, cosine, sine):
    former, latter = signal[:, : HD // 2], signal[:, HD // 2 :]
    return jnp.concatenate([former * cosine + latter * sine, latter * cosine - former * sine], -1)


def block_scores(queries, keys, first, b, kb):
    scores = lax.dot_general(queries, keys, (((1,), (1,)), ((), ())), preferred_element_type=F32)
    bent = jnp.tanh(scores * (0.0625 / SOFTCAP))
    lane = lax.broadcasted_iota(jnp.int32, (256, 256), 1)
    row = lax.broadcasted_iota(jnp.int32, (256, 256), 0)
    key_place = (16 * kb + (lane & 15)) * 16 + (lane >> 4)
    query_place = (16 * b + (row & 15)) * 16 + (row >> 4)
    allowed = (key_place >= first) & (key_place <= query_place)
    return bent, jnp.where(allowed, SOFTCAP * bent, MASKED)


def block_probs(queries, keys, first, b):
    pieces = [
        block_scores(queries, keys[kb], first, b, kb) for kb in range(max(0, b - 2), b + 1)
    ]
    peak = functools.reduce(
        jnp.maximum, [jnp.max(capped, axis=-1, keepdims=True) for _, capped in pieces]
    )
    exps = [jnp.exp(capped - peak) for _, capped in pieces]
    total = functools.reduce(jnp.add, [jnp.sum(e, axis=-1, keepdims=True) for e in exps])
    return [bent for bent, _ in pieces], [e / total for e in exps]


def dot(left, right, left_dim, right_dim):
    return lax.dot_general(
        left, right, (((left_dim,), (right_dim,)), ((), ())), preferred_element_type=F32
    )


def attend_kernel(
    qkv, first, cosine, sine, attended, q_rot, k_rot, v_all,
    rq, rkv, held, send, recv_q, recv_kv, send_back, recv_back, local,
):
    y, zh, core, t = here()
    me = rank(y, zh, core)
    half = lax.rem(t, 2)
    other = t + 1 - 2 * half
    owner = (y < 3) & (core == 0)
    units = [(m, w) for m in range(2) for w in range(3)]
    barrier = pltpu.get_barrier_semaphore()

    def signal(dp, tensor):
        pl.semaphore_signal(barrier, inc=1, device_id=(dp, tensor), device_id_type=MESH)

    @pl.when(owner)
    def _():
        def each(d, _):
            pl.when(d != me)(lambda: signal(d, t))
            signal(d, other)
            return 0

        lax.fori_loop(0, 16, each, 0)

    for m, w in units:
        pl.when(unit_owner(m, w) != me)(functools.partial(signal, unit_owner(m, w), t))

    @pl.when(owner)
    def _():
        pl.semaphore_wait(barrier, 26)

    @pl.when(jnp.logical_not(owner))
    def _():
        pl.semaphore_wait(barrier, 12)

    def to_owner(u, m, w, start):
        o = unit_owner(m, w)
        q_src, kv_src = qkv.at[w, m, :, pl.ds(0, HD)], qkv.at[w, m, :, pl.ds(HD, HD)]
        across = remote(kv_src, rkv.at[half, me], send.at[u, 2], recv_kv.at[half, me], o, other)
        away = [
            remote(q_src, rq.at[me], send.at[u, 0], recv_q.at[me], o, t),
            remote(kv_src, rkv.at[half, me], send.at[u, 1], recv_kv.at[half, me], o, t),
        ]
        near = [
            pltpu.make_async_copy(q_src, rq.at[me], local.at[0]),
            pltpu.make_async_copy(kv_src, rkv.at[half, me], local.at[1]),
        ]

        @pl.when(o != me)
        def _():
            for copy in away:
                copy.start() if start else copy.wait_send()

        @pl.when(o == me)
        def _():
            for copy in near:
                copy.start() if start else copy.wait()

        across.start() if start else across.wait_send()

    for u, (m, w) in enumerate(units):
        to_owner(u, m, w, True)
    for u, (m, w) in enumerate(units):
        to_owner(u, m, w, False)

    @pl.when(owner)
    def _():
        def each(d, _):
            @pl.when(d != me)
            def _():
                remote(rq.at[d], rq.at[d], send.at[0, 0], recv_q.at[d], me, other).wait_recv()
                remote(
                    rkv.at[half, d], rkv.at[half, d], send.at[0, 0], recv_kv.at[half, d], me, other
                ).wait_recv()

            remote(
                rkv.at[1 - half, d], rkv.at[1 - half, d], send.at[0, 0], recv_kv.at[1 - half, d], me, other
            ).wait_recv()
            return 0

        lax.fori_loop(0, 16, each, 0)
        for b in range(4):
            rows = slice(16 * b, 16 * b + 16)
            c, s = cosine[b], sine[b]
            q = rq[:, rows, :].reshape(256, HD).astype(F32)
            q_rot[b] = rotate(q, c, s).astype(B16)
            k = jnp.concatenate(
                [rkv[i, :, rows, : HD // 2].reshape(256, HD // 2) for i in range(2)], -1
            )
            k_rot[b] = rotate(k.astype(F32), c, s).astype(B16)
            v_all[b] = jnp.concatenate(
                [rkv[i, :, rows, HD // 2 :].reshape(256, HD // 2) for i in range(2)], -1
            )
        for b in range(4):
            keys = {kb: k_rot[kb] for kb in range(max(0, b - 2), b + 1)}
            _, probs = block_probs(q_rot[b], keys, first[b], b)
            out = sum(
                dot(p.astype(B16), v_all[kb], 1, 0) for p, kb in zip(probs, sorted(keys))
            )
            held[:, 16 * b : 16 * b + 16, :] = out.astype(B16).reshape(16, 16, HD)

        def hand_back(d, start):
            @pl.when(d != me)
            def _():
                copy = remote(
                    held.at[d], attended.at[y, zh], send_back.at[d], recv_back.at[zh * 3 + y], d, t
                )
                copy.start() if start else copy.wait_send()

            @pl.when(d == me)
            def _():
                copy = pltpu.make_async_copy(held.at[d], attended.at[y, zh], local.at[0])
                copy.start() if start else copy.wait()

        lax.fori_loop(0, 16, lambda d, _: (hand_back(d, True), 0)[1], 0)
        lax.fori_loop(0, 16, lambda d, _: (hand_back(d, False), 0)[1], 0)

    for u, (m, w) in enumerate(units):

        @pl.when(unit_owner(m, w) != me)
        def _():
            ref = attended.at[w, m]
            remote(ref, ref, send.at[0, 0], recv_back.at[u], me, other).wait_recv()


def attend(qkv, first, cosine, sine):
    return pl.pallas_call(
        attend_kernel,
        name="attend",
        out_shape=[struct((3, 2, 64, HD), B16)] + [struct((4, 256, HD), B16)] * 3,
        in_specs=any_space(1) + vmem_space(3),
        out_specs=any_space(1) + vmem_space(3),
        scratch_shapes=[
            pltpu.VMEM((16, 64, HD), B16),
            pltpu.VMEM((2, 16, 64, HD), B16),
            pltpu.VMEM((16, 64, HD), B16),
            pltpu.SemaphoreType.DMA((6, 3)),
            pltpu.SemaphoreType.DMA((16,)),
            pltpu.SemaphoreType.DMA((2, 16)),
            pltpu.SemaphoreType.DMA((16,)),
            pltpu.SemaphoreType.DMA((6,)),
            pltpu.SemaphoreType.DMA((2,)),
        ],
        compiler_params=params(3),
    )(qkv, first, cosine, sine)


def attend_back_kernel(
    d_attended, first, cosine, sine, q_rot, k_rot, v_all, d_query, d_kv,
    rdo, held_q, held_kv, acc_k, acc_v, send, recv, send_q, send_kv, recv_q, recv_kv, local,
):
    y, zh, core, t = here()
    me = rank(y, zh, core)
    half = lax.rem(t, 2)
    other = t + 1 - 2 * half
    owner = (y < 3) & (core == 0)
    units = [(m, w) for m in range(2) for w in range(3)]
    barrier = pltpu.get_barrier_semaphore()

    def signal(dp, tensor):
        pl.semaphore_signal(barrier, inc=1, device_id=(dp, tensor), device_id_type=MESH)

    @pl.when(owner)
    def _():
        def each(d, _):
            pl.when(d != me)(lambda: signal(d, t))
            return 0

        lax.fori_loop(0, 16, each, 0)

    for m, w in units:
        pl.when(unit_owner(m, w) != me)(functools.partial(signal, unit_owner(m, w), t))
        signal(unit_owner(m, w), other)

    @pl.when(owner)
    def _():
        pl.semaphore_wait(barrier, 36)

    @pl.when(jnp.logical_not(owner))
    def _():
        pl.semaphore_wait(barrier, 6)

    def to_owner(u, m, w, start):
        o = unit_owner(m, w)
        src = d_attended.at[w, m]

        @pl.when(o != me)
        def _():
            copy = remote(src, rdo.at[me], send.at[u], recv.at[me], o, t)
            copy.start() if start else copy.wait_send()

        @pl.when(o == me)
        def _():
            copy = pltpu.make_async_copy(src, rdo.at[me], local.at[0])
            copy.start() if start else copy.wait()

    for u, (m, w) in enumerate(units):
        to_owner(u, m, w, True)
    for u, (m, w) in enumerate(units):
        to_owner(u, m, w, False)

    @pl.when(owner)
    def _():
        def each(d, _):
            @pl.when(d != me)
            def _():
                remote(rdo.at[d], rdo.at[d], send.at[0], recv.at[d], me, other).wait_recv()

            return 0

        lax.fori_loop(0, 16, each, 0)
        acc_k[...] = jnp.zeros_like(acc_k)
        acc_v[...] = jnp.zeros_like(acc_v)
        for b in range(4):
            rows = slice(16 * b, 16 * b + 16)
            blocks = list(range(max(0, b - 2), b + 1))
            queries = q_rot[b]
            keys = {kb: k_rot[kb] for kb in blocks}
            upstream = rdo[:, rows, :].reshape(256, HD)
            bents, probs = block_probs(queries, keys, first[b], b)
            d_probs = [dot(upstream, v_all[kb], 1, 1) for kb in blocks]
            centre = sum(
                jnp.sum(p * dp, axis=-1, keepdims=True) for p, dp in zip(probs, d_probs)
            )
            d_q = jnp.zeros((256, HD), F32)
            for kb, bent, p, dp in zip(blocks, bents, probs, d_probs):
                d_scores = (p * (dp - centre) * (1.0 - bent * bent)).astype(B16)
                d_q = d_q + dot(d_scores, keys[kb], 1, 0)
                acc_k[kb] += dot(d_scores, queries, 0, 0)
                acc_v[kb] += dot(p.astype(B16), upstream, 0, 0)
            d_q = unrotate(d_q * 0.0625, cosine[b], sine[b])
            held_q[:, rows, :] = d_q.astype(B16).reshape(16, 16, HD)
        for b in range(4):
            rows = slice(16 * b, 16 * b + 16)
            d_k = unrotate(acc_k[b] * 0.0625, cosine[b], sine[b]).astype(B16)
            d_v = acc_v[b].astype(B16)
            for i in range(2):
                cols = slice(128 * i, 128 * i + 128)
                held_kv[i, :, rows, :128] = d_k[:, cols].reshape(16, 16, 128)
                held_kv[i, :, rows, 128:] = d_v[:, cols].reshape(16, 16, 128)

        def hand_back(d, start):
            u = zh * 3 + y
            across = remote(
                held_kv.at[1 - half, d], d_kv.at[half, y, zh], send_kv.at[1, d], recv_kv.at[half, u], d, other
            )
            across.start() if start else across.wait_send()

            @pl.when(d != me)
            def _():
                for copy in (
                    remote(held_q.at[d], d_query.at[y, zh], send_q.at[d], recv_q.at[u], d, t),
                    remote(
                        held_kv.at[half, d], d_kv.at[half, y, zh], send_kv.at[0, d], recv_kv.at[half, u], d, t
                    ),
                ):
                    copy.start() if start else copy.wait_send()

            @pl.when(d == me)
            def _():
                for copy in (
                    pltpu.make_async_copy(held_q.at[d], d_query.at[y, zh], local.at[0]),
                    pltpu.make_async_copy(held_kv.at[half, d], d_kv.at[half, y, zh], local.at[1]),
                ):
                    copy.start() if start else copy.wait()

        lax.fori_loop(0, 16, lambda d, _: (hand_back(d, True), 0)[1], 0)
        lax.fori_loop(0, 16, lambda d, _: (hand_back(d, False), 0)[1], 0)

    for u, (m, w) in enumerate(units):

        @pl.when(unit_owner(m, w) != me)
        def _():
            ref = d_query.at[w, m]
            remote(ref, ref, send.at[0], recv_q.at[u], me, other).wait_recv()
            ref = d_kv.at[half, w, m]
            remote(ref, ref, send.at[0], recv_kv.at[half, u], me, other).wait_recv()

        ref = d_kv.at[1 - half, w, m]
        remote(ref, ref, send.at[0], recv_kv.at[1 - half, u], me, other).wait_recv()


def attend_back(d_attended, first, cosine, sine, q_rot, k_rot, v_all):
    return pl.pallas_call(
        attend_back_kernel,
        name="attend_back",
        out_shape=[struct((3, 2, 64, HD), B16), struct((2, 3, 2, 64, HD), B16)],
        in_specs=any_space(1) + vmem_space(6),
        out_specs=any_space(2),
        scratch_shapes=[
            pltpu.VMEM((16, 64, HD), B16),
            pltpu.VMEM((16, 64, HD), B16),
            pltpu.VMEM((2, 16, 64, HD), B16),
            pltpu.VMEM((4, 256, HD), F32),
            pltpu.VMEM((4, 256, HD), F32),
            pltpu.SemaphoreType.DMA((6,)),
            pltpu.SemaphoreType.DMA((16,)),
            pltpu.SemaphoreType.DMA((16,)),
            pltpu.SemaphoreType.DMA((2, 16)),
            pltpu.SemaphoreType.DMA((6,)),
            pltpu.SemaphoreType.DMA((2, 6)),
            pltpu.SemaphoreType.DMA((2,)),
        ],
        compiler_params=params(4),
    )(d_attended, first, cosine, sine, q_rot, k_rot, v_all)


def level(codes, width):
    if width == 0:
        return codes
    stride = (1, 16, 64)[width]
    return jnp.floor(codes * B16(1.0 / stride)) * B16(stride) + B16(stride // 2)


def gelu_parts(value):
    slope = 0.7978845608028654
    inner = jnp.tanh(slope * (value + 0.044715 * value * value * value))
    grown = 0.5 * value * (1.0 + inner)
    rate = 0.5 * (1.0 + inner) + 0.5 * value * (1.0 - inner * inner) * slope * (
        1.0 + 3 * 0.044715 * value * value
    )
    return grown, rate


def body(
    tokens,
    cotangent,
    segments,
    codes_query,
    codes_key,
    codes_value,
    codes_out,
    codes_gate,
    codes_up,
    codes_down,
    query_column_scale,
    key_column_scale,
    value_column_scale,
    output_column_scale,
    gate_column_scale,
    up_column_scale,
    down_column_scale,
    gain_first,
    gain_second,
    gain_third,
    gain_fourth,
):
    widths = range(3)
    z_hi = lax.rem(lax.div(lax.axis_index("dp"), 2), 2)
    tokens = tokens.reshape(ROWS, WIDE)
    cotangent = cotangent.reshape(3, ROWS, WIDE)
    gains = jnp.stack([gain_first, gain_second, gain_third, gain_fourth])
    w_qkv, w_out, w_gu, w_down = (
        gathered.reshape(WIDE, -1)
        for gathered in gather_weights(
            [
                jnp.concatenate([codes_query, codes_key, codes_value], 1).astype(B16),
                codes_out.astype(B16).T,
                jnp.concatenate([codes_gate, codes_up], 1).astype(B16),
                codes_down.astype(B16).T,
            ]
        )
    )
    scale_qkv = jnp.concatenate([query_column_scale, key_column_scale, value_column_scale])
    scale_gu = jnp.concatenate([gate_column_scale, up_column_scale])

    documents = lax.dynamic_index_in_dim(segments, z_hi, 0, False)
    starts = jnp.sum((documents[None, :] < documents[:, None]).astype(jnp.int32), axis=1)
    place = jnp.arange(1024, dtype=jnp.int32)

    def blocked(rows):
        return rows.reshape(4, 16, 16).transpose(0, 2, 1).reshape(4, 256)

    first = blocked(starts)[:, :, None]
    expo = jnp.arange(HD // 2, dtype=F32) * (2.0 / HD)
    angle = blocked(place - starts).astype(F32)[:, :, None] * jnp.power(ROPE_BASE, -expo)
    cosine, sine = jnp.cos(angle), jnp.sin(angle)

    inputs = tokens.astype(F32)
    normed_input = (inputs * inverse_rms(inputs) * (1.0 + gain_first)).astype(B16)
    qkv_pre = jnp.stack([dot(normed_input, level(w_qkv, w), 1, 0) * scale_qkv for w in widths])
    attended, q_rot, k_rot, v_all = attend(
        qkv_pre.astype(B16).reshape(3, 2, 64, 2 * HD), first, cosine, sine
    )
    attended = attended.reshape(3, ROWS, HD)
    branch_part = jnp.stack(
        [dot(attended[w], level(w_out, w), 1, 1) * output_column_scale for w in widths]
    ).astype(B16)
    normed_middle, branch, middle = tensor_call(
        middle_kernel,
        "middle",
        5,
        3,
        1,
        (branch_part, tokens[None], gains),
        any_space(2) + vmem_space(1),
        [struct((3, ROWS, WIDE), B16)] + [struct((3, SLICE, WIDE), F32)] * 2,
        any_space(1) + vmem_space(2),
        [pltpu.VMEM((3, SLICE, WIDE), B16)],
    )
    gu_pre = jnp.stack([dot(normed_middle[w], level(w_gu, w), 1, 0) * scale_gu for w in widths])
    half = gu_pre.shape[-1] // 2
    gate_pre, up_pre = gu_pre[..., :half], gu_pre[..., half:]
    grown, rate = gelu_parts(gate_pre)
    hidden = (grown * up_pre).astype(B16)
    feed_part = jnp.stack(
        [dot(hidden[w], level(w_down, w), 1, 1) * down_column_scale for w in widths]
    ).astype(B16)
    d_feed, results, feed_sums = tensor_call(
        feed_kernel,
        "feed",
        6,
        3,
        3,
        (feed_part, cotangent, middle, gains),
        any_space(2) + vmem_space(2),
        [struct((3, ROWS, WIDE), B16)] * 2 + [struct((8, WIDE), F32)],
        any_space(2) + vmem_space(1),
        [pltpu.VMEM((3, SLICE, WIDE), B16)] * 2,
    )

    d_feed_scaled = (d_feed.astype(F32) * down_column_scale).astype(B16)
    d_hidden = jnp.stack([dot(d_feed_scaled[w], level(w_down, w), 1, 0) for w in widths])
    d_gu = jnp.concatenate([d_hidden * up_pre * rate, d_hidden * grown], -1)
    d_gu_low = d_gu.astype(B16)
    gu_sums = jnp.sum(d_gu_low.astype(F32) * gu_pre, axis=(0, 1)) / scale_gu
    d_gu_scaled = (d_gu * scale_gu).astype(B16)
    d_middle_part = jnp.stack([dot(d_gu_scaled[w], level(w_gu, w), 1, 1) for w in widths]).astype(
        B16
    )
    d_branch, d_middle, branch_sums = tensor_call(
        branch_kernel,
        "branch",
        7,
        3,
        3,
        (d_middle_part, cotangent, middle, branch, gains),
        any_space(2) + vmem_space(3),
        [struct((3, ROWS, WIDE), B16), struct((1, SLICE, WIDE), F32), struct((8, WIDE), F32)],
        any_space(1) + vmem_space(2),
        [pltpu.VMEM((3, SLICE, WIDE), B16)],
    )
    d_branch_scaled = (d_branch.astype(F32) * output_column_scale).astype(B16)
    d_attended = jnp.stack([dot(d_branch_scaled[w], level(w_out, w), 1, 0) for w in widths]).astype(
        B16
    )
    d_query, d_kv = attend_back(
        d_attended.reshape(3, 2, 64, HD), first, cosine, sine, q_rot, k_rot, v_all
    )
    d_kv = (d_kv[0].astype(F32) + d_kv[1].astype(F32)).astype(B16)
    d_qkv = jnp.concatenate([d_query, d_kv], -1).reshape(3, ROWS, 2 * HD).astype(F32)
    qkv_sums = jnp.sum(d_qkv * qkv_pre, axis=(0, 1)) / scale_qkv
    d_qkv_scaled = (d_qkv * scale_qkv).astype(B16)
    d_input_part = sum(dot(d_qkv_scaled[w], level(w_qkv, w), 1, 1) for w in widths).astype(B16)
    input_gradient, input_sums = tensor_call(
        input_kernel,
        "input",
        8,
        1,
        1,
        (d_input_part[None], tokens[None], d_middle, gains),
        any_space(2) + vmem_space(2),
        [struct((1, ROWS, WIDE), F32), struct((8, WIDE), F32)],
        any_space(1) + vmem_space(1),
        [pltpu.VMEM((1, SLICE, WIDE), F32)],
    )
    flat = (3 * ROWS, -1)
    parts = (
        dot(normed_input, jnp.sum(d_qkv, axis=0).astype(B16), 0, 0).astype(B16),
        dot(d_branch.reshape(flat), attended.reshape(flat), 0, 0).astype(B16),
        dot(normed_middle.reshape(flat), d_gu_low.reshape(flat), 0, 0).astype(B16),
        dot(d_feed.reshape(flat), hidden.reshape(flat), 0, 0).astype(B16),
    )
    g_qkv, g_out, g_gu, g_down = scatter_gradients(parts)

    rows = jnp.stack(
        [
            input_sums[0],
            branch_sums[1],
            branch_sums[0],
            feed_sums[0],
            branch_sums[2] / output_column_scale,
            feed_sums[1] / down_column_scale,
        ]
    )
    rows = lax.psum(rows, ("dp", "tensor"))
    rows = lax.dynamic_slice_in_dim(rows, lax.axis_index("dp") * SHARD, SHARD, 1)
    columns = lax.psum(jnp.concatenate([qkv_sums, gu_sums]), "dp")
    return (
        results.reshape(3, 2, 64, 1, WIDE),
        input_gradient.reshape(2, 64, 1, WIDE),
        g_qkv[:, :256],
        g_qkv[:, 256:384],
        g_qkv[:, 384:],
        g_out.T,
        g_gu[:, :half],
        g_gu[:, half:],
        g_down.T,
        columns[:256],
        columns[256:384],
        columns[384:512],
        rows[4],
        columns[512 : 512 + half],
        columns[512 + half :],
        rows[5],
        rows[0],
        rows[1],
        rows[2],
        rows[3],
    )


def solution(mesh):
    matrix, turned = P("dp", "tensor"), P("tensor", "dp")
    columns, whole, shard = P("tensor"), P(), P("dp")
    in_specs = (
        P(None, None, "dp", None),
        P(None, None, None, "dp", None),
        whole,
        *(matrix, matrix, matrix, turned, matrix, matrix, turned),
        *(columns, columns, columns, whole, columns, columns, whole),
        *(whole, whole, whole, whole),
    )
    out_specs = (
        P(None, None, None, "dp", None),
        P(None, None, "dp", None),
        *(matrix, matrix, matrix, turned, matrix, matrix, turned),
        *(columns, columns, columns, shard, columns, columns, shard),
        *(shard, shard, shard, shard),
    )
    return jax.shard_map(body, mesh=mesh, in_specs=in_specs, out_specs=out_specs, check_vma=False)
```

time: 1830 us -> 742 us (0.41)
  waiting for transfers between devices: 1010 us -> 0 us
  Pallas kernels: 0 us -> 457 us
  other arithmetic: 262 us -> 38.9 us
  matrix products: 267 us -> 60.1 us
  blocking collectives: 202 us -> 141 us
    pallas_call x0 -> x8, Pallas kernels: none -> 457 us  [the longest x4 207 us: tensor_call(): pl.pallas_call(kernel, name=name, out_shape=outs, in_specs=in_specs, out_...]
    all_gather x9 -> x0, waiting for transfers between devices: 300 us -> none  [the longest x2 89.5 us: body(): lax.all_gather(value_here, 'dp', axis=1, tiled=True)]
    psum x4 -> x0, waiting for transfers between devices: 276 us -> none  [the longest x1 93.1 us: body(): d_normed_middle = lax.psum(d_normed_middle, 'tensor')]
    reduce_scatter x7 -> x0, waiting for transfers between devices: 245 us -> none  [the longest x1 87 us: body(): lax.psum_scatter(totals[4].astype(jnp.bfloat16), 'dp', scatter_dimension=...]
    dot_general x54 -> x28, matrix products: 267 us -> 60.1 us  [dot(): lax.dot_general(left, right, (((left_dim,), (right_dim,)), ((), ())), pre...]
    unnamed x26 -> x0, waiting for transfers between devices: 173 us -> none
    reduce_sum x22 -> x5, other arithmetic: 123 us -> 2.76 us  [the longest x1 1.04 us: body(): jnp.sum(d_qkv, axis=0).astype(B16)]
    another operation x12 -> x11, other arithmetic: 77.1 us -> 5.94 us  [the longest x1 1.4 us: body(): jnp.stack([dot(attended[w], level(w_out, w), 1, 1) * output_column_scale...]
  transfers between devices with their start and end apart: 31 -> 0, of which waited for: 22 -> 0; matrix products, arithmetic and copies ran while one was open for 24% -> 0% of each run, Pallas kernels for 0% -> 0%
where the time goes in v1:
time: 742 us; the launch traced here: 735 us
  Pallas kernels  457 us (62%)
  blocking collectives  141 us (19%)
  matrix products  60.1 us (8%)
  other arithmetic  38.9 us (5%)
  local copies, waits for them, and re-layouts  35.6 us (5%)
    pallas_call x4, Pallas kernels, tensor_call(): pl.pallas_call(kernel, name=name, out_shape=outs, in_specs=in_specs, out_...  207 us
    pallas_call x1, Pallas kernels, gather_weights(): pl.pallas_call(functools.partial(gather_kernel, count), name='gather_weig...  108 us
    pallas_call x1, Pallas kernels, scatter_gradients(): pl.pallas_call(functools.partial(scatter_kernel, count), name='scatter_gr...  84.7 us
    psum x1, blocking collectives, body(): rows = lax.psum(rows, ('dp', 'tensor'))  72.7 us
    psum x1, blocking collectives, body(): columns = lax.psum(jnp.concatenate([qkv_sums, gu_sums]), 'dp')  68 us
    dot_general x28, matrix products, dot(): lax.dot_general(left, right, (((left_dim,), (right_dim,)), ((), ())), pre...  60.1 us
    pallas_call x1, Pallas kernels, attend_back(): pl.pallas_call(attend_back_kernel, name='attend_back', out_shape=[struct(...  29.1 us
    pallas_call x1, Pallas kernels, attend(): pl.pallas_call(attend_kernel, name='attend', out_shape=[struct((3, 2, 64,...  28.8 us

profile of v1, /device:TPU:0, one launch (start us, length us, event | category | flops | bytes accessed | tf_op | source)
XLA Modules:
  0.0 734.9 jit_solution(12595743008832908722)
XLA Ops:
  2.2 3.0 multiply_sine_fusion
  5.3 1.1 broadcast_in_dim_reshape.9.first
  6.6 0.9 pad_maximum_fusion.7.refs_2_
  7.5 0.8 convert_bitcast_fusion.refs_3_
  9.7 107.7 %gather_weights.1 = (bf16[16,144,512]{2,1,0:T(8,128)(2,1)}, bf16[16,144,256]{2,1,0:T(8,128)(2,1)}, bf16[16,144,2304]{2,1,0:T(8,128)(2,1)}, bf16[16,144,1152]{2,1,0:T(8,128)(2,1)}) custom-call(bf16[144,512]{1,0:T(8,128)(2,1)} %pad_maximum_fusion.10.refs_0_, bf16[144,256]{1,0:T(8,128)(2,1)} %convert_bitcast_fusion.1.refs_1_, ...), custom_call_target="tpu_custom_call" | custom-call | tf_op jit(solution)/shard_map/gather_weights/pallas_call | solution.py:142
  117.4 3.9 multiply_add_fusion.6
  121.9 2.4 convolution_multiply_fusion.10
  124.8 1.2 copy-done.9
  126.5 0.8 fusion.42.qkv
  127.3 28.8 %attend.1 = (bf16[3,2,64,256]{3,2,1,0:T(8,128)(2,1)}, bf16[4,256,256]{2,1,0:T(8,128)(2,1)}, bf16[4,256,256]{2,1,0:T(8,128)(2,1)}, bf16[4,256,256]{2,1,0:T(8,128)(2,1)}) custom-call(bf16[3,2,64,512]{3,2,1,0:T(8,128)(2,1)} %fusion.42.qkv, s32[4,256,1]{2,1,0:T(8,128)} %broadcast_in_dim_reshape.9.first, f32[4,256,128]{2,1,0:T(8,128)} %get-tuple-element.190.cosine, ...), custom_call_target="tpu_custom_call" | custom-call | tf_op jit(solution)/shard_map/attend/pallas_call | solution.py:654
  156.1 0.9 fusion.52
  157.6 0.8 multiply_add_fusion.8
  159.9 1.4 pad_maximum_fusion.2.part
  162.0 56.6 %middle.1 = (bf16[3,128,2304]{2,1,0:T(8,128)(2,1)}, f32[3,16,2304]{2,1,0:T(8,128)}, f32[3,16,2304]{2,1,0:T(8,128)}) custom-call(bf16[3,128,2304]{2,1,0:T(8,128)(2,1)} %pad_maximum_fusion.2.part, bf16[1,128,2304]{2,1,0:T(8,128)(2,1)} %bitcast.232, f32[4,2304]{1,0:T(4,128)} %pad_maximum_fusion.11.gains), custom_call_target="tpu_custom_call" | custom-call | tf_op jit(solution)/shard_map/middle/pallas_call | solution.py:461
  218.8 5.9 fusion.1
  225.4 7.6 %multiply_add_fusion.1 = (bf16[16,144,2304]{2,1,0:T(8,128)(2,1)S(1)}, bf16[16,144,2304]{2,1,0:T(8,128)(2,1)S(1)}) fusion(bf16[16,144,2304]{2,1,0:T(8,128)(2,1)S(1)} %bitcast.194), kind=kLoop, calls=%fused_computation.4 | loop fusion | flops 90243072 | bytes 31850496 | tf_op jit(solution)/shard_map/add | solution.py:839
  233.0 1.6 fusion.2
  234.6 3.4 copy-done.3
  238.0 3.2 copy-done.2
  241.2 1.6 fusion.3
  244.4 1.3 copy-done.7
  245.7 1.6 fusion.20
  247.3 3.9 multiply_add_fusion.3
  251.2 1.6 fusion.19
  252.8 0.8 copy-done.4
  253.6 1.6 fusion.18
  255.2 1.4 pad_maximum_fusion.3.part
  256.6 73.2 %feed.1 = (bf16[3,128,2304]{2,1,0:T(8,128)(2,1)}, bf16[3,128,2304]{2,1,0:T(8,128)(2,1)}, f32[8,2304]{1,0:T(8,128)}) custom-call(bf16[3,128,2304]{2,1,0:T(8,128)(2,1)} %pad_maximum_fusion.3.part, bf16[3,128,2304]{2,1,0:T(8,128)(2,1)} %bitcast.234, f32[3,16,2304]{2,1,0:T(8,128)} %get-tuple-element.51.middle, f32[4,2304]{1,0:T(4,128)} %pad_maximum_fusion.11.gains), custom_call_target="tpu_custom_call" | custom-call | tf_op jit(solution)/shard_map/feed/pallas_call | solution.py:461
  329.8 1.9 multiply_convert_fusion.2
  331.7 1.0 convolution_bitcast_fusion.3
  332.8 0.9 convolution_bitcast_fusion.2
  334.5 1.0 convolution_bitcast_fusion.1
  335.6 1.3 fusion.27
  337.4 0.8 multiply_reduce_fusion
  338.7 1.4 slice-done.4
  340.5 3.5 fusion.12
  344.1 7.7 %fusion.13 = bf16[1,128,2304]{2,1,0:T(8,128)(2,1)S(1)} fusion(bf16[2304,2304]{1,0:T(8,128)(2,1)} %bitcast.203, bf16[3,128,2304]{2,1,0:T(8,128)(2,1)S(1)} %get-tuple-element.157), kind=kOutput, calls=%fused_computation.42 | convolution fusion | flops 1359249408 | bytes 11796480 | tf_op jit(solution)/shard_map/dot_general | solution.py:523
  351.8 3.5 fusion.14
  355.3 1.4 pad_maximum_fusion.5.part
  356.7 51.0 %branch.1 = (bf16[3,128,2304]{2,1,0:T(8,128)(2,1)}, f32[1,16,2304]{2,1,0:T(8,128)}, f32[8,2304]{1,0:T(8,128)}) custom-call(bf16[3,128,2304]{2,1,0:T(8,128)(2,1)} %pad_maximum_fusion.5.part, bf16[3,128,2304]{2,1,0:T(8,128)(2,1)} %bitcast.235, f32[3,16,2304]{2,1,0:T(8,128)} %get-tuple-element.51.middle, f32[3,16,2304]{2,1,0:T(8,128)} %get-tuple-element.54.branch, ...), custom_call_target="tpu_custom_call" | custom-call | tf_op jit(solution)/shard_map/branch/pallas_call | solution.py:461
  407.7 1.2 slice_reduce_fusion
  408.9 1.8 multiply_convert_fusion
  410.8 1.1 copy-done.19
  414.4 29.1 %attend_back.1 = (bf16[3,2,64,256]{3,2,1,0:T(8,128)(2,1)}, bf16[2,3,2,64,256]{4,3,2,1,0:T(8,128)(2,1)}) custom-call(bf16[3,2,64,256]{3,2,1,0:T(8,128)(2,1)} %pad_maximum_fusion.9.d_attended, s32[4,256,1]{2,1,0:T(8,128)} %broadcast_in_dim_reshape.9.first, f32[4,256,128]{2,1,0:T(8,128)} %get-tuple-element.190.cosine, f32[4,256,128]{2,1,0:T(8,128)} %get-tuple-element.189.sine, ...), custom_call_target="tpu_custom_call" | custom-call | tf_op jit(solution)/shard_map/attend_back/pallas_call | solution.py:811
  443.5 1.2 fusion.46
  444.7 1.0 fusion.44
  445.9 0.9 fusion.47
  446.8 0.8 copy-done.13
  447.5 0.9 convolution_add_fusion.1
  448.4 0.8 copy-done.12
  449.2 1.7 fusion.11.part
  450.9 26.3 %input.1 = (f32[1,128,2304]{2,1,0:T(8,128)}, f32[8,2304]{1,0:T(8,128)}) custom-call(bf16[1,128,2304]{2,1,0:T(8,128)(2,1)} %fusion.11.part, bf16[1,128,2304]{2,1,0:T(8,128)(2,1)} %bitcast.233, f32[1,16,2304]{2,1,0:T(8,128)} %get-tuple-element.61.d_middle, f32[4,2304]{1,0:T(4,128)} %pad_maximum_fusion.11.gains), custom_call_target="tpu_custom_call" | custom-call | tf_op jit(solution)/shard_map/input/pallas_call | solution.py:461
  477.2 0.9 slice.177
  478.2 72.7 %psum.15 = f32[6,2304]{1,0:T(8,128)S(1)} all-reduce(f32[6,2304]{1,0:T(8,128)S(1)} %stack.146), channel_id=1, replica_groups=mesh['dp'=16,'tensor'=8] {'dp','tensor'}, use_global_device_ids=true, to_apply=%region_6.7 | all-reduce | flops 13824 | bytes 110592 | tf_op jit(solution)/shard_map/psum | solution.py:1013
  551.7 68.0 %psum.14 = f32[2816]{0:T(1024)S(1)} all-reduce(f32[2816]{0:T(1024)S(1)} %pad_maximum_fusion.12), channel_id=1, replica_groups=mesh['dp'=16,'tensor'=8] {'dp'}, use_global_device_ids=true, to_apply=%region_5.6 | all-reduce | flops 2816 | bytes 22528 | tf_op jit(solution)/shard_map/psum | solution.py:1015
  621.4 7.1 fusion
  628.5 8.3 %bitcast_convert_fusion = bf16[2304,2304]{1,0:T(8,128)(2,1)} fusion(bf16[3,128,2304]{2,1,0:T(8,128)(2,1)S(1)} %copy-done.30, f32[3,128,1152]{2,1,0:T(8,128)S(1)} %copy-done.28, f32[3,128,1152]{2,1,0:T(8,128)S(1)} %copy-done.26), kind=kOutput, calls=%fused_computation | convolution fusion | flops 4085710848 | bytes 15925248 | tf_op jit(solution)/shard_map/dot_general | solution.py:523
  636.8 1.8 convolution_convert_fusion.1
  638.7 2.2 convolution_convert_fusion
  640.9 84.7 %scatter_gradients.1 = (f32[144,512]{1,0:T(8,128)}, f32[144,256]{1,0:T(8,128)}, f32[144,2304]{1,0:T(8,128)}, f32[144,1152]{1,0:T(8,128)}) custom-call(bf16[8,2,144,512]{3,2,1,0:T(8,128)(2,1)} %bitcast.231, bf16[8,2,144,256]{3,2,1,0:T(8,128)(2,1)} %bitcast.248, bf16[8,2,144,2304]{3,2,1,0:T(8,128)(2,1)} %bitcast.224, bf16[8,2,144,1152]{3,2,1,0:T(8,128)(2,1)} %bitcast.236), custom_call_target="tpu_custom_call" | custom-call | tf_op jit(solution)/shard_map/scatter_gradients/pallas_call | solution.py:272
  725.6 2.5 fusion.50
  729.5 2.2 copy.67
  731.7 1.2 copy.78
  733.6 0.8 copy.80
  (206 shorter events, 19.3 us)
Async XLA Ops:
  0.7 5.7 copy-start.39
  0.7 5.8 copy-start.40
  6.5 1.8 copy-start.47
  6.5 1.8 copy-start.50
  6.5 1.8 copy-start.51
  6.5 2.5 copy-start.48
  117.4 4.0 copy-start.59
  117.4 4.0 copy-start.60
  117.4 4.0 copy-start.61
  117.4 4.0 copy-start.52
  117.4 4.0 copy-start.24
  121.3 3.0 copy-start.11
  124.3 1.7 copy-start.9
  126.5 30.6 %copy-start.33 = (f32[128,512]{1,0:T(8,128)}, f32[128,512]{1,0:T(8,128)S(1)}, u32[]{:S(2)}) copy-start(f32[128,512]{1,0:T(8,128)S(1)} %convolution_multiply_fusion.11) | copy-start | bytes 786436
  126.5 30.6 %copy-start.18 = (bf16[16,144,256]{2,1,0:T(8,128)(2,1)S(1)}, bf16[16,144,256]{2,1,0:T(8,128)(2,1)}, u32[]{:S(2)}) copy-start(bf16[16,144,256]{2,1,0:T(8,128)(2,1)} %get-tuple-element.47) | copy-start | bytes 3538948
  126.5 30.6 %copy-start.43 = (f32[2304]{0:T(1024)S(1)}, f32[2304]{0:T(1024)}, u32[]{:S(2)}) copy-start(f32[2304]{0:T(1024)} %param.34) | copy-start | bytes 27652
  159.9 1.4 copy-start.54
  159.9 1.5 copy-start.55
  159.9 1.5 copy-start.56
  161.3 57.4 %copy-start.57 = (f32[1152]{0:T(1024)S(1)}, f32[1152]{0:T(1024)}, u32[]{:S(2)}) copy-start(f32[1152]{0:T(1024)} %param.35) | copy-start | bytes 13828
  161.3 57.4 %copy-start.58 = (f32[1152]{0:T(1024)S(1)}, f32[1152]{0:T(1024)}, u32[]{:S(2)}) copy-start(f32[1152]{0:T(1024)} %param.36) | copy-start | bytes 13828
  162.0 62.7 %slice-start = ((s8[10616832]{0:T(1024)(128)(4,1)}), s8[2228224]{0:T(1024)(128)(4,1)S(1)}, s32[]{:S(2)}) async-start(s8[10616832]{0:T(1024)(128)(4,1)} %bitcast.193), calls=%async_computation | async-start | bytes 4456448
  218.7 5.9 slice-start.1
  218.7 6.7 slice-start.2
  225.4 17.4 %copy-start.14 = (f32[1,128,2304]{2,1,0:T(8,128)}, f32[1,128,2304]{2,1,0:T(8,128)S(1)}, u32[]{:S(2)}) copy-start(f32[1,128,2304]{2,1,0:T(8,128)S(1)} %fusion.1) | copy-start | bytes 3538948
  225.4 7.6 %copy-start.29 = (bf16[3,128,2304]{2,1,0:T(8,128)(2,1)S(1)}, bf16[3,128,2304]{2,1,0:T(8,128)(2,1)}, u32[]{:S(2)}) copy-start(bf16[3,128,2304]{2,1,0:T(8,128)(2,1)} %get-tuple-element.48) | copy-start | bytes 5308420
  233.0 5.1 copy-start.3
  233.0 8.2 %copy-start.2 = (bf16[16,144,2304]{2,1,0:T(8,128)(2,1)}, bf16[16,144,2304]{2,1,0:T(8,128)(2,1)S(1)}, u32[]{:S(2)}) copy-start(bf16[16,144,2304]{2,1,0:T(8,128)(2,1)S(1)} %get-tuple-element.151) | copy-start | bytes 31850500
  233.0 12.7 %slice-start.9 = ((s8[5308416]{0:T(1024)(128)(4,1)}), s8[4194304]{0:T(1024)(128)(4,1)S(1)}, s32[]{:S(2)}) async-start(s8[5308416]{0:T(1024)(128)(4,1)} %bitcast.204), calls=%async_computation.9 | async-start | bytes 8388608
  241.2 4.5 slice-start.10
  243.8 1.9 copy-start.7
  243.8 1.9 copy-start.44
  245.7 7.1 copy-start.31
  251.2 2.4 copy-start.4
  251.2 4.0 copy-start.5
  329.8 3.0 copy-start.6
  329.8 4.3 slice-start.11
  331.7 2.8 slice-start.12
  332.8 2.8 copy-start.8
  334.5 4.2 slice-start.3
  335.6 1.7 copy-start.17
  335.6 4.5 slice-start.4
  336.9 1.8 copy-start.27
  337.3 3.2 slice-start.5
  340.5 11.2 %slice-start.6 = ((s8[10616832]{0:T(1024)(128)(4,1)}), s8[4194304]{0:T(1024)(128)(4,1)S(1)}, s32[]{:S(2)}) async-start(s8[10616832]{0:T(1024)(128)(4,1)} %bitcast.199), calls=%async_computation.6 | async-start | bytes 8388608
  340.5 11.2 %slice-start.7 = ((s8[10616832]{0:T(1024)(128)(4,1)}), s8[2228224]{0:T(1024)(128)(4,1)S(1)}, s32[]{:S(2)}) async-start(s8[10616832]{0:T(1024)(128)(4,1)} %bitcast.199), calls=%async_computation.7 | async-start | bytes 4456448
  344.0 7.7 %slice-start.8 = ((s8[10616832]{0:T(1024)(128)(4,1)}), s8[4194304]{0:T(1024)(128)(4,1)S(1)}, s32[]{:S(2)}) async-start(s8[10616832]{0:T(1024)(128)(4,1)} %bitcast.199), calls=%async_computation.8 | async-start | bytes 8388608
  410.8 1.5 copy-start.23
  443.5 2.4 copy-start.10
  445.9 1.7 copy-start.13
  447.5 1.7 copy-start.12
  450.9 100.7 %copy-start.34 = (f32[128,512]{1,0:T(8,128)S(1)}, f32[128,512]{1,0:T(8,128)}, u32[]{:S(2)}) copy-start(f32[128,512]{1,0:T(8,128)} %copy-done.33) | copy-start | bytes 786436
  450.9 100.7 %copy-start.38 = (bf16[3,2,64,256]{3,2,1,0:T(8,128)(2,1)S(1)}, bf16[3,2,64,256]{3,2,1,0:T(8,128)(2,1)}, u32[]{:S(2)}) copy-start(bf16[3,2,64,256]{3,2,1,0:T(8,128)(2,1)} %get-tuple-element.59) | copy-start | bytes 589828
  450.9 170.5 %copy-start.32 = (bf16[3,128,1152]{2,1,0:T(8,128)(2,1)S(1)}, bf16[3,128,1152]{2,1,0:T(8,128)(2,1)}, u32[]{:S(2)}) copy-start(bf16[3,128,1152]{2,1,0:T(8,128)(2,1)} %copy-done.31) | copy-start | bytes 2654212
  621.4 7.1 copy-start.26
  621.4 7.1 copy-start.28
  621.4 7.1 copy-start.30
  628.5 8.4 %copy-start.36 = (bf16[3,128,2304]{2,1,0:T(8,128)(2,1)S(1)}, bf16[3,128,2304]{2,1,0:T(8,128)(2,1)}, u32[]{:S(2)}) copy-start(bf16[3,128,2304]{2,1,0:T(8,128)(2,1)} %get-tuple-element.55) | copy-start | bytes 5308420
  628.5 8.4 %copy-start.46 = (bf16[3,2,64,256]{3,2,1,0:T(8,128)(2,1)S(1)}, bf16[3,2,64,256]{3,2,1,0:T(8,128)(2,1)}, u32[]{:S(2)}) copy-start(bf16[3,2,64,256]{3,2,1,0:T(8,128)(2,1)} %get-tuple-element.46) | copy-start | bytes 589828
  725.5 2.6 copy-start.45
  725.6 3.9 copy-start.37
  728.1 3.6 copy-start.35
  731.7 2.7 copy-start.1
  731.7 1.9 copy-start.42
  (11 other events, 13.2 us)

commit v2 on v1

--- a/solution.py
+++ b/solution.py
@@ -22,6 +22,7 @@
 TENSOR = 8
 ROWS = 128
 SLICE = ROWS // TENSOR
+EXTRA = 384
 VMEM_BYTES = 56 * 2**20
 
 
@@ -45,6 +46,10 @@
     for device in devices:
         pl.semaphore_signal(barrier, inc=1, device_id=device, device_id_type=MESH)
     pl.semaphore_wait(barrier, len(devices))
+
+
+def struct(shape, dtype):
+    return jax.ShapeDtypeStruct(shape, dtype)
 
 
 def any_space(count):
@@ -154,18 +159,26 @@
     )(*shards)
 
 
-def scatter_kernel(count, *refs):
-    parts, outs = refs[:count], refs[count : 2 * count]
+def finish_kernel(count, *refs):
+    parts, refs = refs[:count], refs[count:]
+    (part, tokens, d_middle, gains, final, sums, columns), refs = refs[:7], refs[7:]
+    outs, refs = refs[:count], refs[count:]
+    (results, gradient, totals), refs = refs[:3], refs[3:]
     own, sibs, yrecv, zrecv, ylast, zlast = (
-        refs[(2 + i) * count : (3 + i) * count] for i in range(6)
-    )
-    send, recv, local = refs[8 * count :]
+        refs[i * count : (i + 1) * count] for i in range(6)
+    )
+    refs = refs[6 * count :]
+    held, mine, block, vectors, from_t, from_sib, from_y, from_z = refs[:8]
+    send, recv, local, send_t, recv_t, local_t, send_v, recv_v = refs[8:]
     y, zh, core, t = here()
-    sib, zz = rank(y, zh, 1 - core), rank(y, 1 - zh, core)
+    me, sib, zz = rank(y, zh, core), rank(y, zh, 1 - core), rank(y, 1 - zh, core)
     ahead = [lax.rem(y + dy, 4) for dy in (1, 2, 3)]
     fore = [rank(place, zh, core) for place in ahead]
-    greet([(sib, t), (zz, t)] + [(dp, t) for dp in fore])
-    started = []
+    peers = tensor_peers()
+    greet([(sib, t), (zz, t)] + [(dp, t) for dp in fore] + [(me, peer) for peer in peers[1:]])
+    started = scatter_rows(part, held, send_t.at[0], recv_t.at[0], local_t.at[0])
+    input_copies = list(started)
+    finish_results = spread_rows(final, results, send_t.at[1], recv_t.at[1], local_t.at[1])
 
     def push(k, slot, src, dst, dp):
         copy = remote(src, dst, send.at[k, slot], recv.at[k, slot], dp, t)
@@ -179,11 +192,28 @@
     for k in range(count):
         for i, place in enumerate(order):
             pair = pl.ds(place * 2, 2)
-            back = lax.rem(y + 4 - (i + 1), 4)
             push(k, i, parts[k].at[pair, 1 - core], sibs[k].at[pair], sib)
             pltpu.make_async_copy(
                 parts[k].at[pair, core], own[k].at[pair], local.at[k, i]
             ).start()
+
+    load = load_rows(tokens, mine, local_t.at[2])
+    load.wait()
+    upstream = summed(held, input_copies)
+    signal = mine[...].astype(F32)
+    inverse = inverse_rms(signal)
+    normed = signal * inverse
+    block[...] = d_middle[...] + norm_back(normed, inverse, gains[0:1], upstream)
+    finish_input = spread_rows(block, gradient, send_t.at[2], recv_t.at[2], local_t.at[3])
+    from_t[t] = jnp.concatenate(
+        [over_rows(upstream * normed), sums[...], jnp.zeros((2, WIDE), F32)], 0
+    )
+    vector_copies = []
+    for k in range(1, TENSOR):
+        copy = remote(from_t.at[t], from_t.at[t], send_t.at[3, k], recv_t.at[3, k], me, peers[k])
+        copy.start()
+        vector_copies.append(copy)
+
     for k in range(count):
         for i, place in enumerate(order):
             pair = pl.ds(place * 2, 2)
@@ -206,6 +236,20 @@
             push(
                 k, 7 + i, own[k].at[place * 2 + 1 - zh, pl.ds(LOW, HIGH)], zrecv[k].at[place], zz
             )
+    for k in range(1, TENSOR):
+        source = from_t.at[peers[TENSOR - k]]
+        remote(source, source, send_t.at[3, k], recv_t.at[3, k], me, peers[k]).wait_recv()
+    vectors[:, :WIDE] = functools.reduce(jnp.add, [from_t[i] for i in range(TENSOR)])
+    vectors[:, WIDE:] = columns[...]
+    copy = remote(vectors, from_sib, send_v.at[0], recv_v.at[0], sib, t)
+    copy.start()
+    copy.wait()
+    from_y[y] = vectors[...] + from_sib[...]
+    for i in range(3):
+        copy = remote(from_y.at[y], from_y.at[y], send_v.at[1 + i], recv_v.at[1 + i], fore[i], t)
+        copy.start()
+        vector_copies.append(copy)
+
     for k in range(count):
         for i, place in enumerate(order):
             arrive(k, 7 + i, zrecv[k].at[place])
@@ -235,6 +279,12 @@
 
         lax.fori_loop(0, 2 * LOW // 16, pool, 0)
         push(k, 14, own[k].at[y * 2 + 1 - zh, pl.ds(0, LOW)], zlast[k], zz)
+    for i in range(3):
+        source = from_y.at[lax.rem(y + 3 - i, 4)]
+        remote(source, source, send_v.at[1 + i], recv_v.at[1 + i], fore[i], t).wait_recv()
+    totals[...] = functools.reduce(jnp.add, [from_y[i] for i in range(4)])
+    vectors_z = remote(totals, from_z, send_v.at[4], recv_v.at[4], zz, t)
+    vectors_z.start()
     for k in range(count):
         arrive(k, 14, zlast[k])
 
@@ -256,11 +306,15 @@
             return 0
 
         lax.fori_loop(0, HIGH // 16, end_high, 0)
-    for copy in started:
+    vectors_z.wait()
+    totals[...] = totals[...] + from_z[...]
+    finish_results()
+    finish_input()
+    for copy in started + vector_copies:
         copy.wait_send()
 
 
-def scatter_gradients(parts):
+def finish_layer(parts, *others):
     count = len(parts)
     columns = [part.shape[-1] for part in parts]
     scratch = [pltpu.VMEM((8, SHARD, c), B16) for c in columns]
@@ -270,19 +324,37 @@
     scratch += [pltpu.VMEM((3, HIGH, c), B16) for c in columns]
     scratch += [pltpu.VMEM((LOW, c), B16) for c in columns]
     return pl.pallas_call(
-        functools.partial(scatter_kernel, count),
-        name="scatter_gradients",
-        out_shape=[jax.ShapeDtypeStruct((SHARD, c), F32) for c in columns],
-        in_specs=any_space(count),
-        out_specs=vmem_space(count),
+        functools.partial(finish_kernel, count),
+        name="finish_layer",
+        out_shape=[struct((SHARD, c), F32) for c in columns]
+        + [
+            struct((3, ROWS, WIDE), B16),
+            struct((1, ROWS, WIDE), F32),
+            struct((8, WIDE + EXTRA), F32),
+        ],
+        in_specs=any_space(count + 2) + vmem_space(5),
+        out_specs=vmem_space(count) + any_space(2) + vmem_space(1),
         scratch_shapes=scratch
         + [
+            pltpu.VMEM((TENSOR, 1, SLICE, WIDE), B16),
+            pltpu.VMEM((1, SLICE, WIDE), B16),
+            pltpu.VMEM((1, SLICE, WIDE), F32),
+            pltpu.VMEM((8, WIDE + EXTRA), F32),
+            pltpu.VMEM((TENSOR, 8, WIDE), F32),
+            pltpu.VMEM((8, WIDE + EXTRA), F32),
+            pltpu.VMEM((4, 8, WIDE + EXTRA), F32),
+            pltpu.VMEM((8, WIDE + EXTRA), F32),
             pltpu.SemaphoreType.DMA((count, 15)),
             pltpu.SemaphoreType.DMA((count, 15)),
             pltpu.SemaphoreType.DMA((count, 4)),
+            pltpu.SemaphoreType.DMA((4, TENSOR)),
+            pltpu.SemaphoreType.DMA((4, TENSOR)),
+            pltpu.SemaphoreType.DMA((4,)),
+            pltpu.SemaphoreType.DMA((5,)),
+            pltpu.SemaphoreType.DMA((5,)),
         ],
         compiler_params=params(2),
-    )(*[part.reshape(8, 2, SHARD, part.shape[-1]) for part in parts])
+    )(*[part.reshape(8, 2, SHARD, part.shape[-1]) for part in parts], *others)
 
 
 def row_block(index):
@@ -386,7 +458,7 @@
 
 
 def feed_kernel(
-    part, cotangent, middle, gains, d_feed, results, sums, held, mine, block, final, send, recv, local
+    part, cotangent, middle, gains, d_feed, final, sums, held, mine, block, send, recv, local
 ):
     greet_tensor()
     copies = scatter_rows(part, held, send.at[0], recv.at[0], local.at[0])
@@ -400,13 +472,11 @@
     block[...] = lowered
     finish = spread_rows(block, d_feed, send.at[1], recv.at[1], local.at[2])
     final[...] = (middle[...] + normed * (1.0 + gains[3:4])).astype(B16)
-    finish_results = spread_rows(final, results, send.at[2], recv.at[2], local.at[3])
     sums[0:1] = over_rows(upstream * normed)
     sums[1:2] = over_rows(lowered.astype(F32) * signal)
     for copy in copies:
         copy.wait_send()
     finish()
-    finish_results()
 
 
 def branch_kernel(
@@ -436,25 +506,6 @@
     finish()
 
 
-def input_kernel(
-    part, tokens, d_middle, gains, gradient, sums, held, mine, block, send, recv, local
-):
-    greet_tensor()
-    copies = scatter_rows(part, held, send.at[0], recv.at[0], local.at[0])
-    load = load_rows(tokens, mine, local.at[1])
-    load.wait()
-    upstream = summed(held, copies)
-    signal = mine[...].astype(F32)
-    inverse = inverse_rms(signal)
-    normed = signal * inverse
-    block[...] = d_middle[...] + norm_back(normed, inverse, gains[0:1], upstream)
-    finish = spread_rows(block, gradient, send.at[1], recv.at[1], local.at[2])
-    sums[0:1] = over_rows(upstream * normed)
-    for copy in copies:
-        copy.wait_send()
-    finish()
-
-
 def tensor_call(
     kernel, name, collective_id, depth, loaded, operands, in_specs, outs, out_specs, blocks
 ):
@@ -476,10 +527,6 @@
         ],
         compiler_params=params(collective_id),
     )(*operands)
-
-
-def struct(shape, dtype):
-    return jax.ShapeDtypeStruct(shape, dtype)
 
 
 def unit_owner(micro, width):
@@ -933,7 +980,7 @@
     feed_part = jnp.stack(
         [dot(hidden[w], level(w_down, w), 1, 1) * down_column_scale for w in widths]
     ).astype(B16)
-    d_feed, results, feed_sums = tensor_call(
+    d_feed, final, feed_sums = tensor_call(
         feed_kernel,
         "feed",
         6,
@@ -941,9 +988,9 @@
         3,
         (feed_part, cotangent, middle, gains),
         any_space(2) + vmem_space(2),
-        [struct((3, ROWS, WIDE), B16)] * 2 + [struct((8, WIDE), F32)],
-        any_space(2) + vmem_space(1),
-        [pltpu.VMEM((3, SLICE, WIDE), B16)] * 2,
+        [struct((3, ROWS, WIDE), B16), struct((3, SLICE, WIDE), B16), struct((8, WIDE), F32)],
+        any_space(1) + vmem_space(2),
+        [pltpu.VMEM((3, SLICE, WIDE), B16)],
     )
 
     d_feed_scaled = (d_feed.astype(F32) * down_column_scale).astype(B16)
@@ -979,18 +1026,6 @@
     qkv_sums = jnp.sum(d_qkv * qkv_pre, axis=(0, 1)) / scale_qkv
     d_qkv_scaled = (d_qkv * scale_qkv).astype(B16)
     d_input_part = sum(dot(d_qkv_scaled[w], level(w_qkv, w), 1, 1) for w in widths).astype(B16)
-    input_gradient, input_sums = tensor_call(
-        input_kernel,
-        "input",
-        8,
-        1,
-        1,
-        (d_input_part[None], tokens[None], d_middle, gains),
-        any_space(2) + vmem_space(2),
-        [struct((1, ROWS, WIDE), F32), struct((8, WIDE), F32)],
-        any_space(1) + vmem_space(1),
-        [pltpu.VMEM((1, SLICE, WIDE), F32)],
-    )
     flat = (3 * ROWS, -1)
     parts = (
         dot(normed_input, jnp.sum(d_qkv, axis=0).astype(B16), 0, 0).astype(B16),
@@ -998,21 +1033,21 @@
         dot(normed_middle.reshape(flat), d_gu_low.reshape(flat), 0, 0).astype(B16),
         dot(d_feed.reshape(flat), hidden.reshape(flat), 0, 0).astype(B16),
     )
-    g_qkv, g_out, g_gu, g_down = scatter_gradients(parts)
-
-    rows = jnp.stack(
+    sums = jnp.concatenate(
         [
-            input_sums[0],
-            branch_sums[1],
-            branch_sums[0],
-            feed_sums[0],
-            branch_sums[2] / output_column_scale,
-            feed_sums[1] / down_column_scale,
+            branch_sums[1:2],
+            branch_sums[0:1],
+            feed_sums[0:1],
+            branch_sums[2:3] / output_column_scale,
+            feed_sums[1:2] / down_column_scale,
         ]
     )
-    rows = lax.psum(rows, ("dp", "tensor"))
-    rows = lax.dynamic_slice_in_dim(rows, lax.axis_index("dp") * SHARD, SHARD, 1)
-    columns = lax.psum(jnp.concatenate([qkv_sums, gu_sums]), "dp")
+    columns = jnp.pad(jnp.concatenate([qkv_sums, gu_sums]), (0, 8 * EXTRA - 2816))
+    g_qkv, g_out, g_gu, g_down, results, input_gradient, sums = finish_layer(
+        parts, d_input_part[None], tokens[None], d_middle, gains, final, sums, columns.reshape(8, EXTRA)
+    )
+    rows = lax.dynamic_slice_in_dim(sums[:, :WIDE], lax.axis_index("dp") * SHARD, SHARD, 1)
+    columns = sums[:, WIDE:].reshape(-1)
     return (
         results.reshape(3, 2, 64, 1, WIDE),
         input_gradient.reshape(2, 64, 1, WIDE),
@@ -1028,7 +1063,7 @@
         columns[384:512],
         rows[4],
         columns[512 : 512 + half],
-        columns[512 + half :],
+        columns[512 + half : 512 + 2 * half],
         rows[5],
         rows[0],
         rows[1],

time: 742 us -> 598 us (0.81)
  blocking collectives: 141 us -> 0 us
    psum x2 -> x0, blocking collectives: 141 us -> none  [the longest x1 72.7 us: body(): rows = lax.psum(rows, ('dp', 'tensor'))]
    pallas_call x4 -> x3, Pallas kernels: 207 us -> 162 us  [tensor_call(): pl.pallas_call(kernel, name=name, out_shape=outs, in_specs=in_specs, out_...]
    pallas_call x1, Pallas kernels: 84.7 us -> 129 us  [finish_layer(): pl.pallas_call(functools.partial(finish_kernel, count), name='finish_laye...]
    unnamed x157 -> x161, local copies, waits for them, and re-layouts: 24.7 us -> 24.8 us
where the time goes in v2:
time: 598 us; the launch traced here: 589 us
  Pallas kernels  453 us (76%)
  matrix products  57.9 us (10%)
  other arithmetic  41 us (7%)
  local copies, waits for them, and re-layouts  34.9 us (6%)
    pallas_call x3, Pallas kernels, tensor_call(): pl.pallas_call(kernel, name=name, out_shape=outs, in_specs=in_specs, out_...  162 us
    pallas_call x1, Pallas kernels, finish_layer(): pl.pallas_call(functools.partial(finish_kernel, count), name='finish_laye...  129 us
    pallas_call x1, Pallas kernels, gather_weights(): pl.pallas_call(functools.partial(gather_kernel, count), name='gather_weig...  108 us
    dot_general x28, matrix products, dot(): lax.dot_general(left, right, (((left_dim,), (right_dim,)), ((), ())), pre...  57.9 us
    pallas_call x1, Pallas kernels, attend(): pl.pallas_call(attend_kernel, name='attend', out_shape=[struct((3, 2, 64,...  28.8 us
    pallas_call x1, Pallas kernels, attend_back(): pl.pallas_call(attend_back_kernel, name='attend_back', out_shape=[struct(...  25.7 us
    unnamed x161, local copies, waits for them, and re-layouts  24.8 us
    add x4, other arithmetic, level(): return jnp.floor(codes * B16(1.0 / stride)) * B16(stride) + B16(stride // 2)  16.3 us

profile of v2, /device:TPU:0, one launch (start us, length us, event | category | flops | bytes accessed | tf_op | source)
XLA Modules:
  0.0 588.5 jit_solution(12469661334244362833)
XLA Ops:
  2.2 3.1 multiply_sine_fusion
  5.3 1.1 broadcast_in_dim_reshape.9.first
  6.6 0.9 pad_maximum_fusion.7.refs_2_
  7.5 0.8 convert_bitcast_fusion.refs_3_
  9.7 107.7 %gather_weights.1 = (bf16[16,144,512]{2,1,0:T(8,128)(2,1)}, bf16[16,144,256]{2,1,0:T(8,128)(2,1)}, bf16[16,144,2304]{2,1,0:T(8,128)(2,1)}, bf16[16,144,1152]{2,1,0:T(8,128)(2,1)}) custom-call(bf16[144,512]{1,0:T(8,128)(2,1)} %pad_maximum_fusion.10.refs_0_, bf16[144,256]{1,0:T(8,128)(2,1)} %convert_bitcast_fusion.1.refs_1_, ...), custom_call_target="tpu_custom_call" | custom-call | tf_op jit(solution)/shard_map/gather_weights/pallas_call | solution.py:147
  117.5 3.9 multiply_add_fusion.6
  121.9 2.4 convolution_multiply_fusion.10
  124.9 1.2 copy-done.9
  126.5 0.8 fusion.42.qkv
  127.3 28.8 %attend.1 = (bf16[3,2,64,256]{3,2,1,0:T(8,128)(2,1)}, bf16[4,256,256]{2,1,0:T(8,128)(2,1)}, bf16[4,256,256]{2,1,0:T(8,128)(2,1)}, bf16[4,256,256]{2,1,0:T(8,128)(2,1)}) custom-call(bf16[3,2,64,512]{3,2,1,0:T(8,128)(2,1)} %fusion.42.qkv, s32[4,256,1]{2,1,0:T(8,128)} %broadcast_in_dim_reshape.9.first, f32[4,256,128]{2,1,0:T(8,128)} %get-tuple-element.192.cosine, ...), custom_call_target="tpu_custom_call" | custom-call | tf_op jit(solution)/shard_map/attend/pallas_call | solution.py:701
  156.2 0.9 fusion.52
  157.6 0.8 multiply_add_fusion.8
  159.9 1.4 pad_maximum_fusion.2.part
  162.1 56.8 %middle.1 = (bf16[3,128,2304]{2,1,0:T(8,128)(2,1)}, f32[3,16,2304]{2,1,0:T(8,128)}, f32[3,16,2304]{2,1,0:T(8,128)}) custom-call(bf16[3,128,2304]{2,1,0:T(8,128)(2,1)} %pad_maximum_fusion.2.part, bf16[1,128,2304]{2,1,0:T(8,128)(2,1)} %bitcast.232, f32[4,2304]{1,0:T(4,128)} %pad_maximum_fusion.11.gains.refs_7_), custom_call_target="tpu_custom_call" | custom-call | tf_op jit(solution)/shard_map/middle/pallas_call | solution.py:512
  219.0 5.9 %fusion.1 = f32[1,128,2304]{2,1,0:T(8,128)S(1)} fusion(bf16[2304,2304]{1,0:T(8,128)(2,1)} %bitcast.192, f32[2304]{0:T(1024)S(1)} %constant_dynamic-update-slice_fusion.4, bf16[3,128,2304]{2,1,0:T(8,128)(2,1)} %get-tuple-element.49), kind=kOutput, calls=%fused_computation.21 | convolution fusion | flops 1359249408 | bytes 12395520 | tf_op jit(solution)/shard_map/dot_general | solution.py:570
  224.9 0.7 slice-done.2
  225.6 7.6 %multiply_add_fusion.1 = (bf16[16,144,2304]{2,1,0:T(8,128)(2,1)S(1)}, bf16[16,144,2304]{2,1,0:T(8,128)(2,1)S(1)}) fusion(bf16[16,144,2304]{2,1,0:T(8,128)(2,1)S(1)} %bitcast.194), kind=kLoop, calls=%fused_computation.4 | loop fusion | flops 90243072 | bytes 31850496 | tf_op jit(solution)/shard_map/add | solution.py:886
  233.2 1.6 fusion.2
  234.8 3.4 copy-done.3
  238.3 3.2 copy-done.2
  241.5 1.6 fusion.3
  243.3 0.7 copy-done.16
  244.7 1.3 copy-done.7
  246.0 1.6 fusion.20
  247.5 3.9 multiply_add_fusion.3
  251.5 1.6 fusion.19
  253.0 0.8 copy-done.4
  253.9 1.6 fusion.18
  255.4 1.4 pad_maximum_fusion.3.part
  256.8 51.1 %feed.1 = (bf16[3,128,2304]{2,1,0:T(8,128)(2,1)}, bf16[3,16,2304]{2,1,0:T(8,128)(2,1)}, f32[8,2304]{1,0:T(8,128)}) custom-call(bf16[3,128,2304]{2,1,0:T(8,128)(2,1)} %pad_maximum_fusion.3.part, bf16[3,128,2304]{2,1,0:T(8,128)(2,1)} %bitcast.234, f32[3,16,2304]{2,1,0:T(8,128)} %get-tuple-element.52.middle, f32[4,2304]{1,0:T(4,128)} %pad_maximum_fusion.11.gains.refs_7_), custom_call_target="tpu_custom_call" | custom-call | tf_op jit(solution)/shard_map/feed/pallas_call | solution.py:512
  308.0 1.9 multiply_convert_fusion.2
  309.9 1.0 convolution_bitcast_fusion.3
  311.0 0.9 convolution_bitcast_fusion.2
  312.7 0.9 convolution_bitcast_fusion.1
  313.8 1.3 fusion.27
  315.5 0.8 multiply_reduce_fusion
  316.9 1.4 slice-done.4
  318.7 3.5 fusion.12
  322.3 7.7 %fusion.13 = bf16[1,128,2304]{2,1,0:T(8,128)(2,1)S(1)} fusion(bf16[2304,2304]{1,0:T(8,128)(2,1)} %bitcast.203, bf16[3,128,2304]{2,1,0:T(8,128)(2,1)S(1)} %get-tuple-element.159), kind=kOutput, calls=%fused_computation.42 | convolution fusion | flops 1359249408 | bytes 11796480 | tf_op jit(solution)/shard_map/dot_general | solution.py:570
  330.0 3.5 fusion.14
  333.5 1.4 pad_maximum_fusion.5.part
  334.9 53.8 %branch.1 = (bf16[3,128,2304]{2,1,0:T(8,128)(2,1)}, f32[1,16,2304]{2,1,0:T(8,128)}, f32[8,2304]{1,0:T(8,128)}) custom-call(bf16[3,128,2304]{2,1,0:T(8,128)(2,1)} %pad_maximum_fusion.5.part, bf16[3,128,2304]{2,1,0:T(8,128)(2,1)} %bitcast.235, f32[3,16,2304]{2,1,0:T(8,128)} %get-tuple-element.52.middle, f32[3,16,2304]{2,1,0:T(8,128)} %get-tuple-element.54.branch, ...), custom_call_target="tpu_custom_call" | custom-call | tf_op jit(solution)/shard_map/branch/pallas_call | solution.py:512
  388.7 1.8 multiply_convert_fusion
  390.6 1.1 copy-done.19
  394.2 25.7 %attend_back.1 = (bf16[3,2,64,256]{3,2,1,0:T(8,128)(2,1)}, bf16[2,3,2,64,256]{4,3,2,1,0:T(8,128)(2,1)}) custom-call(bf16[3,2,64,256]{3,2,1,0:T(8,128)(2,1)} %pad_maximum_fusion.9.d_attended, s32[4,256,1]{2,1,0:T(8,128)} %broadcast_in_dim_reshape.9.first, f32[4,256,128]{2,1,0:T(8,128)} %get-tuple-element.192.cosine, f32[4,256,128]{2,1,0:T(8,128)} %get-tuple-element.191.sine, ...), custom_call_target="tpu_custom_call" | custom-call | tf_op jit(solution)/shard_map/attend_back/pallas_call | solution.py:858
  419.9 1.1 fusion.46
  421.0 1.2 multiply_reduce_fusion.1
  422.9 1.1 reshape_divide_fusion
  423.9 0.7 concatenate.36.refs_9_
  424.6 1.1 fusion.44
  425.9 0.9 fusion.47
  426.8 0.8 copy-done.13
  427.6 0.9 convolution_add_fusion.1
  428.5 0.8 copy-done.12
  429.2 1.7 fusion.11.refs_4_
  431.0 4.8 fusion
  435.9 8.3 %bitcast_convert_fusion = bf16[2304,2304]{1,0:T(8,128)(2,1)} fusion(bf16[3,128,2304]{2,1,0:T(8,128)(2,1)S(1)} %copy-done.30, f32[3,128,1152]{2,1,0:T(8,128)S(1)} %copy-done.28, f32[3,128,1152]{2,1,0:T(8,128)S(1)} %copy-done.26), kind=kOutput, calls=%fused_computation | convolution fusion | flops 4085710848 | bytes 15925248 | tf_op jit(solution)/shard_map/dot_general | solution.py:570
  444.2 1.8 convolution_convert_fusion.1
  446.0 2.2 convolution_convert_fusion
  448.2 128.6 %finish_layer.1 = (f32[144,512]{1,0:T(8,128)}, f32[144,256]{1,0:T(8,128)}, f32[144,2304]{1,0:T(8,128)}, f32[144,1152]{1,0:T(8,128)}, bf16[3,128,2304]{2,1,0:T(8,...) custom-call(bf16[8,2,144,512]{3,2,1,0:T(8,128)(2,1)} %bitcast.231, bf16[8,2,144,256]{3,2,1,0:T(8,128)(2,1)} %bitcast.248, ...), custom_call_target="tpu_custom_call" | custom-call | tf_op jit(solution)/shard_map/finish_layer/pallas_call | solution.py:326
  576.9 2.5 fusion.50
  579.4 2.2 copy.67
  585.4 1.2 copy.78
  587.3 0.8 copy.80
  (206 shorter events, 18.3 us)
Async XLA Ops:
  0.7 5.8 copy-start.40
  0.7 5.8 copy-start.41
  6.5 1.8 copy-start.48
  6.5 1.8 copy-start.52
  6.5 1.8 copy-start.53
  6.6 2.5 copy-start.49
  117.4 4.0 copy-start.61
  117.4 4.0 copy-start.62
  117.4 4.0 copy-start.63
  117.4 4.0 copy-start.54
  117.4 4.0 copy-start.24
  121.4 3.0 copy-start.11
  124.4 1.7 copy-start.9
  126.5 30.6 %copy-start.33 = (f32[128,512]{1,0:T(8,128)}, f32[128,512]{1,0:T(8,128)S(1)}, u32[]{:S(2)}) copy-start(f32[128,512]{1,0:T(8,128)S(1)} %convolution_multiply_fusion.11) | copy-start | bytes 786436
  126.5 30.6 %copy-start.18 = (bf16[16,144,256]{2,1,0:T(8,128)(2,1)S(1)}, bf16[16,144,256]{2,1,0:T(8,128)(2,1)}, u32[]{:S(2)}) copy-start(bf16[16,144,256]{2,1,0:T(8,128)(2,1)} %get-tuple-element.48) | copy-start | bytes 3538948
  126.5 30.6 %copy-start.44 = (f32[2304]{0:T(1024)S(1)}, f32[2304]{0:T(1024)}, u32[]{:S(2)}) copy-start(f32[2304]{0:T(1024)} %param.34) | copy-start | bytes 27652
  159.9 1.5 copy-start.57
  159.9 1.5 copy-start.58
  161.3 57.6 %copy-start.59 = (f32[1152]{0:T(1024)S(1)}, f32[1152]{0:T(1024)}, u32[]{:S(2)}) copy-start(f32[1152]{0:T(1024)} %param.35) | copy-start | bytes 13828
  161.3 57.6 %copy-start.60 = (f32[1152]{0:T(1024)S(1)}, f32[1152]{0:T(1024)}, u32[]{:S(2)}) copy-start(f32[1152]{0:T(1024)} %param.36) | copy-start | bytes 13828
  162.1 62.8 %slice-start = ((s8[10616832]{0:T(1024)(128)(4,1)}), s8[2228224]{0:T(1024)(128)(4,1)S(1)}, s32[]{:S(2)}) async-start(s8[10616832]{0:T(1024)(128)(4,1)} %bitcast.193), calls=%async_computation | async-start | bytes 4456448
  219.0 5.9 %slice-start.1 = ((s8[10616832]{0:T(1024)(128)(4,1)}), s8[4194304]{0:T(1024)(128)(4,1)S(1)}, s32[]{:S(2)}) async-start(s8[10616832]{0:T(1024)(128)(4,1)} %bitcast.193), calls=%async_computation.1 | async-start | bytes 8388608
  219.0 6.7 %slice-start.2 = ((s8[10616832]{0:T(1024)(128)(4,1)}), s8[4194304]{0:T(1024)(128)(4,1)S(1)}, s32[]{:S(2)}) async-start(s8[10616832]{0:T(1024)(128)(4,1)} %bitcast.193), calls=%async_computation.2 | async-start | bytes 8388608
  225.6 17.4 %copy-start.14 = (f32[1,128,2304]{2,1,0:T(8,128)}, f32[1,128,2304]{2,1,0:T(8,128)S(1)}, u32[]{:S(2)}) copy-start(f32[1,128,2304]{2,1,0:T(8,128)S(1)} %fusion.1) | copy-start | bytes 3538948
  225.6 7.6 %copy-start.29 = (bf16[3,128,2304]{2,1,0:T(8,128)(2,1)S(1)}, bf16[3,128,2304]{2,1,0:T(8,128)(2,1)}, u32[]{:S(2)}) copy-start(bf16[3,128,2304]{2,1,0:T(8,128)(2,1)} %get-tuple-element.49) | copy-start | bytes 5308420
  233.2 5.1 copy-start.3
  233.2 8.2 %copy-start.2 = (bf16[16,144,2304]{2,1,0:T(8,128)(2,1)}, bf16[16,144,2304]{2,1,0:T(8,128)(2,1)S(1)}, u32[]{:S(2)}) copy-start(bf16[16,144,2304]{2,1,0:T(8,128)(2,1)S(1)} %get-tuple-element.153) | copy-start | bytes 31850500
  233.2 12.7 %slice-start.9 = ((s8[5308416]{0:T(1024)(128)(4,1)}), s8[4194304]{0:T(1024)(128)(4,1)S(1)}, s32[]{:S(2)}) async-start(s8[5308416]{0:T(1024)(128)(4,1)} %bitcast.204), calls=%async_computation.9 | async-start | bytes 8388608
  241.5 4.5 slice-start.10
  244.1 1.9 copy-start.7
  244.1 1.9 copy-start.45
  245.9 7.1 %copy-start.31 = (bf16[3,128,1152]{2,1,0:T(8,128)(2,1)}, bf16[3,128,1152]{2,1,0:T(8,128)(2,1)S(1)}, u32[]{:S(2)}) copy-start(bf16[3,128,1152]{2,1,0:T(8,128)(2,1)S(1)} %multiply_convert_fusion.3) | copy-start | bytes 2654212
  251.4 2.4 copy-start.4
  251.5 4.0 copy-start.5
  307.9 3.0 copy-start.6
  308.0 4.3 slice-start.11
  309.9 2.8 slice-start.12
  311.0 2.8 copy-start.8
  312.7 4.2 slice-start.3
  313.8 1.7 copy-start.17
  313.8 4.5 slice-start.4
  315.1 1.8 copy-start.27
  315.5 3.2 slice-start.5
  318.7 11.2 %slice-start.6 = ((s8[10616832]{0:T(1024)(128)(4,1)}), s8[4194304]{0:T(1024)(128)(4,1)S(1)}, s32[]{:S(2)}) async-start(s8[10616832]{0:T(1024)(128)(4,1)} %bitcast.199), calls=%async_computation.6 | async-start | bytes 8388608
  318.7 11.2 %slice-start.7 = ((s8[10616832]{0:T(1024)(128)(4,1)}), s8[2228224]{0:T(1024)(128)(4,1)S(1)}, s32[]{:S(2)}) async-start(s8[10616832]{0:T(1024)(128)(4,1)} %bitcast.199), calls=%async_computation.7 | async-start | bytes 4456448
  322.2 7.7 %slice-start.8 = ((s8[10616832]{0:T(1024)(128)(4,1)}), s8[4194304]{0:T(1024)(128)(4,1)S(1)}, s32[]{:S(2)}) async-start(s8[10616832]{0:T(1024)(128)(4,1)} %bitcast.199), calls=%async_computation.8 | async-start | bytes 8388608
  390.6 1.5 copy-start.23
  394.2 26.8 %copy-start.34 = (f32[128,512]{1,0:T(8,128)S(1)}, f32[128,512]{1,0:T(8,128)}, u32[]{:S(2)}) copy-start(f32[128,512]{1,0:T(8,128)} %copy-done.33) | copy-start | bytes 786436
  421.0 4.9 copy-start.10
  425.9 1.7 copy-start.13
  427.6 1.7 copy-start.12
  429.2 1.7 copy-start.32
  429.2 1.8 copy-start.37
  431.0 4.9 copy-start.26
  431.0 4.9 copy-start.28
  431.0 4.9 copy-start.30
  435.8 8.3 %copy-start.38 = (bf16[3,128,2304]{2,1,0:T(8,128)(2,1)S(1)}, bf16[3,128,2304]{2,1,0:T(8,128)(2,1)}, u32[]{:S(2)}) copy-start(bf16[3,128,2304]{2,1,0:T(8,128)(2,1)} %get-tuple-element.55) | copy-start | bytes 5308420
  435.8 8.3 %copy-start.47 = (bf16[3,2,64,256]{3,2,1,0:T(8,128)(2,1)S(1)}, bf16[3,2,64,256]{3,2,1,0:T(8,128)(2,1)}, u32[]{:S(2)}) copy-start(bf16[3,2,64,256]{3,2,1,0:T(8,128)(2,1)} %get-tuple-element.47) | copy-start | bytes 589828
  576.9 2.5 copy-start.39
  579.4 2.2 copy-start.46
  579.4 3.6 copy-start.51
  579.4 6.0 %copy-start.35 = (bf16[3,128,2304]{2,1,0:T(8,128)(2,1)S(1)}, bf16[3,128,2304]{2,1,0:T(8,128)(2,1)}, u32[]{:S(2)}) copy-start(bf16[3,128,2304]{2,1,0:T(8,128)(2,1)} %get-tuple-element.65) | copy-start | bytes 5308420
  584.8 3.3 copy-start.1
  585.4 1.9 copy-start.43
  (13 other events, 15.9 us)

commit v3 on v1

v3 whole, which is shorter than its diff:
```python
import functools

import jax
import jax.numpy as jnp
from jax import lax
from jax.experimental import pallas as pl
from jax.experimental.pallas import tpu as pltpu
from jax.sharding import PartitionSpec as P

MESH = pl.DeviceIdType.MESH
F32 = jnp.float32
B16 = jnp.bfloat16
EPSILON = 1e-06
SOFTCAP = 50.0
ROPE_BASE = 10000.0
MASKED = -1e30
HD = 256
WIDE = 2304
SHARD = 144
LOW = 64
HIGH = SHARD - LOW
TENSOR = 8
ROWS = 128
SLICE = ROWS // TENSOR
EXTRA = 384
VMEM_BYTES = 63 * 2**20


def here():
    dp = lax.axis_index("dp")
    return lax.div(dp, 4), lax.rem(lax.div(dp, 2), 2), lax.rem(dp, 2), lax.axis_index("tensor")


def rank(y, z_hi, core):
    return (y * 2 + z_hi) * 2 + core


def remote(src, dst, send, recv, dp, tensor):
    return pltpu.make_async_remote_copy(
        src, dst, send, recv, device_id=(dp, tensor), device_id_type=MESH
    )


def greet(devices):
    barrier = pltpu.get_barrier_semaphore()
    for device in devices:
        pl.semaphore_signal(barrier, inc=1, device_id=device, device_id_type=MESH)
    pl.semaphore_wait(barrier, len(devices))


def struct(shape, dtype):
    return jax.ShapeDtypeStruct(shape, dtype)


def any_space(count):
    return [pl.BlockSpec(memory_space=pl.ANY)] * count


def vmem_space(count):
    return [pl.BlockSpec(memory_space=pltpu.VMEM)] * count


def params(collective_id):
    return pltpu.CompilerParams(
        collective_id=collective_id, has_side_effects=True, vmem_limit_bytes=VMEM_BYTES
    )


class Gather:
    def __init__(self, src, out, send, recv, local):
        self.src, self.out, self.send, self.recv, self.local = src, out, send, recv, local
        self.y, self.zh, self.core, self.t = here()
        y, zh, core = self.y, self.zh, self.core
        self.me, self.sib, self.zz = rank(y, zh, core), rank(y, zh, 1 - core), rank(y, 1 - zh, core)
        self.fore = [rank(lax.rem(y + dy, 4), zh, core) for dy in (1, 2, 3)]
        self.behind = [lax.rem(y + 4 - dy, 4) for dy in (1, 2, 3)]
        self.low, self.high = pl.ds(0, LOW), pl.ds(LOW, HIGH)
        self.started = []

    def push(self, slot, src, dst, dp):
        copy = remote(src, dst, self.send.at[slot], self.recv.at[slot], dp, self.t)
        copy.start()
        self.started.append(copy)

    def arrive(self, slot, ref):
        remote(ref, ref, self.send.at[slot], self.recv.at[slot], self.sib, self.t).wait_recv()

    def start(self):
        src, mine = self.src, self.out.at[self.me]
        self.mine = pltpu.make_async_copy(src, mine, self.local)
        self.mine.start()
        low, high = self.low, self.high
        self.push(0, src.at[low], self.out.at[self.me, low], self.zz)
        for i in range(3):
            self.push(4 + i, src.at[high], self.out.at[self.me, high], self.fore[i])
        for i in range(3):
            self.push(1 + i, src.at[low], self.out.at[self.me, low], self.fore[i])
        self.push(7, src.at[high], self.out.at[self.me, high], self.zz)
        self.push(14, src, mine, self.sib)

    def over_y(self):
        block = self.out.at[self.zz, self.low]
        self.arrive(0, block)
        for i in range(3):
            self.push(8 + i, block, block, self.fore[i])
        self.push(15, block, block, self.sib)

    def over_z(self):
        for i in range(3):
            block = self.out.at[rank(self.behind[i], self.zh, self.core), self.high]
            self.arrive(4 + i, block)
            self.push(11 + i, block, block, self.zz)
            self.push(16 + i, block, block, self.sib)

    def near(self):
        for i in range(3):
            block = self.out.at[rank(self.behind[i], self.zh, self.core), self.low]
            self.arrive(1 + i, block)
            self.push(19 + i, block, block, self.sib)
        block = self.out.at[self.zz, self.high]
        self.arrive(7, block)
        self.push(22, block, block, self.sib)

    def far(self):
        for i in range(3):
            dp = rank(self.behind[i], 1 - self.zh, self.core)
            for slot, rows in ((0, self.low), (3, self.high)):
                block = self.out.at[dp, rows]
                self.arrive(8 + slot + i, block)
                self.push(23 + slot + i, block, block, self.sib)

    def end(self):
        out, low, high, other = self.out, self.low, self.high, 1 - self.core
        self.arrive(14, out.at[self.sib])
        far = rank(self.y, 1 - self.zh, other)
        self.arrive(15, out.at[far, low])
        self.arrive(22, out.at[far, high])
        for i in range(3):
            near, far = (rank(self.behind[i], zh, other) for zh in (self.zh, 1 - self.zh))
            self.arrive(16 + i, out.at[near, high])
            self.arrive(19 + i, out.at[near, low])
            self.arrive(23 + i, out.at[far, low])
            self.arrive(26 + i, out.at[far, high])
        self.mine.wait()

    def drain(self):
        for copy in self.started:
            copy.wait_send()


class Rows:
    def __init__(self, part, held_x, held_z, stage, block, out, sems, own=None):
        self.own = own
        self.part, self.held_x, self.held_z, self.stage = part, held_x, held_z, stage
        self.block, self.out = block, out
        self.send, self.recv, self.local = sems
        self.dp, self.t = lax.axis_index("dp"), lax.axis_index("tensor")
        self.zl, self.x = lax.div(self.t, 4), lax.rem(self.t, 4)
        self.ahead = [lax.rem(self.x + k, 4) for k in (1, 2, 3)]
        self.behind = [lax.rem(self.x + 4 - k, 4) for k in (1, 2, 3)]
        self.x_peers = [self.zl * 4 + x for x in self.ahead]
        self.z_peer = (1 - self.zl) * 4 + self.x
        self.started = []

    def peers(self):
        return [(self.dp, t) for t in self.x_peers + [self.z_peer]]

    def push(self, w, slot, src, dst, t):
        copy = remote(src, dst, self.send.at[w, slot], self.recv.at[w, slot], self.dp, t)
        copy.start()
        self.started.append(copy)

    def arrive(self, w, slot, ref):
        remote(
            ref, ref, self.send.at[w, slot], self.recv.at[w, slot], self.dp, self.z_peer
        ).wait_recv()

    def scatter_x(self, w):
        for k in range(3):
            self.push(w, 1 + k, self.part.at[w, :, self.ahead[k]], self.held_x.at[w, k], self.x_peers[k])

    def summed_x(self, w, zl):
        total = (self.part[w, zl, self.x] if self.own is None else self.own[w, zl]).astype(F32)
        for k in range(3):
            total = total + self.held_x[w, k, zl].astype(F32)
        return total

    def scatter_z(self, w):
        for k in range(3):
            self.arrive(w, 1 + k, self.held_x.at[w, k])
        self.stage[w] = self.summed_x(w, 1 - self.zl).astype(B16)
        self.push(w, 0, self.stage.at[w], self.held_z.at[w], self.z_peer)

    def total(self, w):
        self.arrive(w, 0, self.held_z.at[w])
        return self.summed_x(w, self.zl) + self.held_z[w].astype(F32)

    def spread(self, w):
        block, mine = self.block.at[w], self.out.at[w, self.zl, self.x]
        self.push(w, 4, block, mine, self.z_peer)
        for k in range(3):
            self.push(w, 5 + k, block, mine, self.x_peers[k])
        pltpu.make_async_copy(block, mine, self.local.at[w]).start()

    def forward(self, w):
        block = self.out.at[w, 1 - self.zl, self.x]
        self.arrive(w, 4, block)
        for k in range(3):
            self.push(w, 8 + k, block, block, self.x_peers[k])

    def end(self, w):
        for k in range(3):
            self.arrive(w, 5 + k, self.out.at[w, self.zl, self.behind[k]])
            self.arrive(w, 8 + k, self.out.at[w, 1 - self.zl, self.behind[k]])
        pltpu.make_async_copy(
            self.block.at[w], self.out.at[w, self.zl, self.x], self.local.at[w]
        ).wait()

    def drain(self):
        for copy in self.started:
            copy.wait_send()


def rows_scratch(depth):
    return [
        pltpu.VMEM((depth, 3, 2, SLICE, WIDE), B16),
        pltpu.VMEM((depth, SLICE, WIDE), B16),
        pltpu.VMEM((depth, SLICE, WIDE), B16),
        pltpu.VMEM((depth, SLICE, WIDE), B16),
        pltpu.SemaphoreType.DMA((depth, 11)),
        pltpu.SemaphoreType.DMA((depth, 11)),
        pltpu.SemaphoreType.DMA((depth,)),
    ]


class Reduce:
    def __init__(self, columns, away, own, sibs, yrecv, zrecv, ylast, zlast, out, send, recv):
        self.columns, self.away, self.own, self.sibs = columns, away, own, sibs
        self.yrecv, self.zrecv, self.ylast, self.zlast, self.out = yrecv, zrecv, ylast, zlast, out
        self.send, self.recv = send, recv
        self.y, self.zh, self.core, self.t = here()
        y, zh, core = self.y, self.zh, self.core
        self.sib, self.zz = rank(y, zh, 1 - core), rank(y, 1 - zh, core)
        self.ahead = [lax.rem(y + dy, 4) for dy in (1, 2, 3)]
        self.fore = [rank(place, zh, core) for place in self.ahead]
        self.started = []

    def push(self, slot, src, dst, dp):
        copy = remote(src, dst, self.send.at[slot], self.recv.at[slot], dp, self.t)
        copy.start()
        self.started.append(copy)

    def arrive(self, slot, ref):
        remote(ref, ref, self.send.at[slot], self.recv.at[slot], self.sib, self.t).wait_recv()

    def store(self, first, count, cols, block):
        block = block.astype(B16).reshape(count, 2, SHARD, block.shape[-1])
        even = self.core == 0
        chips = pl.ds(first, count)
        self.own[chips, :, cols] = jnp.where(even, block[:, 0], block[:, 1])
        self.away[chips, :, cols] = jnp.where(even, block[:, 1], block[:, 0])

    def to_sibling(self, place):
        pair = pl.ds(place * 2, 2)
        return remote(
            self.away.at[pair, :, pl.ds(0, self.columns)],
            self.sibs.at[pair],
            self.send.at[place],
            self.recv.at[place],
            self.sib,
            self.t,
        )

    def product(self, turned, right, left_columns=0):
        def step(place, _):
            rows = pl.ds(pl.multiple_of(place * 4 * SHARD, 16), 4 * SHARD)
            for i in range(self.columns // 384):
                block = dot(turned[rows], right[:, left_columns + 384 * i : left_columns + 384 * (i + 1)], 1, 0)
                self.store(place * 2, 2, slice(384 * i, 384 * (i + 1)), block)
            self.to_sibling(place).start()
            return 0

        lax.fori_loop(0, 4, step, 0)

    def product_whole(self, left, right):
        for i in range(self.columns // HD):
            cols = slice(HD * i, HD * i + HD)
            self.store(0, 8, cols, dot(left, right[:, cols], 0, 0))
        for place in range(4):
            self.to_sibling(place).start()

    def sent_away(self):
        for place in range(4):
            self.to_sibling(place).wait_send()

    def add(self):
        own, sibs = self.own, self.sibs
        for i, place in enumerate(self.ahead + [self.y]):
            pair = pl.ds(place * 2, 2)
            self.arrive(place, sibs.at[pair])

            def step(step, _, place=place):
                chip = place * 2 + lax.div(step, SHARD // 16)
                rows = pl.ds(pl.multiple_of(lax.rem(step, SHARD // 16) * 16, 16), 16)
                own[chip, rows] = (
                    own[chip, rows].astype(F32) + sibs[chip, rows].astype(F32)
                ).astype(B16)
                return 0

            lax.fori_loop(0, 2 * SHARD // 16, step, 0)
            self.push(
                7 + i, own.at[place * 2 + 1 - self.zh, pl.ds(LOW, HIGH)], self.zrecv.at[place], self.zz
            )
            if i < 3:
                self.push(4 + i, own.at[pair, pl.ds(0, LOW)], self.yrecv.at[i], self.fore[i])

    def merge(self):
        own, zrecv = self.own, self.zrecv
        for i, place in enumerate(self.ahead + [self.y]):
            self.arrive(7 + i, zrecv.at[place])

            def step(step, _, place=place):
                rows = pl.ds(pl.multiple_of(step * 16, 16), 16)
                mine = pl.ds(pl.multiple_of(step * 16 + LOW, 16), 16)
                zrecv[place, rows] = (
                    zrecv[place, rows].astype(F32) + own[place * 2 + self.zh, mine].astype(F32)
                ).astype(B16)
                return 0

            lax.fori_loop(0, HIGH // 16, step, 0)
            if i < 3:
                self.push(11 + i, zrecv.at[place], self.ylast.at[i], self.fore[i])

    def pool(self):
        for i in range(3):
            self.arrive(4 + i, self.yrecv.at[i])

        def step(step, _):
            chip = lax.div(step, LOW // 16)
            rows = pl.ds(pl.multiple_of(lax.rem(step, LOW // 16) * 16, 16), 16)
            total = self.own[self.y * 2 + chip, rows].astype(F32)
            for i in range(3):
                total = total + self.yrecv[i, chip, rows].astype(F32)
            self.own[self.y * 2 + chip, rows] = total.astype(B16)
            return 0

        lax.fori_loop(0, 2 * LOW // 16, step, 0)
        self.push(14, self.own.at[self.y * 2 + 1 - self.zh, pl.ds(0, LOW)], self.zlast, self.zz)

    def end(self):
        self.arrive(14, self.zlast)

        def low(step, _):
            rows = pl.ds(pl.multiple_of(step * 16, 16), 16)
            self.out[rows] = self.own[self.y * 2 + self.zh, rows].astype(F32) + self.zlast[
                rows
            ].astype(F32)
            return 0

        lax.fori_loop(0, LOW // 16, low, 0)
        for i in range(3):
            self.arrive(11 + i, self.ylast.at[i])

        def high(step, _):
            rows = pl.ds(pl.multiple_of(step * 16, 16), 16)
            total = self.zrecv[self.y, rows].astype(F32)
            for i in range(3):
                total = total + self.ylast[i, rows].astype(F32)
            self.out[pl.ds(pl.multiple_of(step * 16 + LOW, 16), 16)] = total
            return 0

        lax.fori_loop(0, HIGH // 16, high, 0)

    def drain(self):
        for copy in self.started:
            copy.wait_send()


def reduce_scratch(columns):
    return [
        pltpu.VMEM((8, SHARD, columns), B16),
        pltpu.VMEM((8, SHARD, columns), B16),
        pltpu.VMEM((3, 2, LOW, columns), B16),
        pltpu.VMEM((4, HIGH, columns), B16),
        pltpu.VMEM((3, HIGH, columns), B16),
        pltpu.VMEM((LOW, columns), B16),
        pltpu.SemaphoreType.DMA((15,)),
        pltpu.SemaphoreType.DMA((15,)),
    ]


def row_block(index):
    return pl.ds(pl.multiple_of(index * SLICE, SLICE), SLICE)


def tensor_peers():
    t = lax.axis_index("tensor")
    return [lax.rem(t + k, TENSOR) for k in range(TENSOR)]


def greet_tensor():
    dp = lax.axis_index("dp")
    greet([(dp, peer) for peer in tensor_peers()[1:]])


def scatter_rows(part, held, send, recv, local):
    dp = lax.axis_index("dp")
    peers = tensor_peers()
    copies = []
    for k in range(1, TENSOR):
        copy = remote(
            part.at[:, row_block(peers[k])], held.at[k], send.at[k], recv.at[k], dp, peers[k]
        )
        copy.start()
        copies.append(copy)
    mine = pltpu.make_async_copy(part.at[:, row_block(peers[0])], held.at[0], local)
    mine.start()
    mine.wait()
    return copies


def summed(held, copies):
    total = held[0].astype(F32)
    for k in range(1, TENSOR):
        copies[k - 1].wait_recv()
        total = total + held[k].astype(F32)
    return total


def spread_rows(block, whole, send, recv, local):
    dp = lax.axis_index("dp")
    peers = tensor_peers()
    here_rows = whole.at[:, row_block(peers[0])]
    copies = []
    for k in range(1, TENSOR):
        copy = remote(block, here_rows, send.at[k], recv.at[k], dp, peers[k])
        copy.start()
        copies.append(copy)
    mine = pltpu.make_async_copy(block, here_rows, local)
    mine.start()

    def finish():
        mine.wait()
        for k in range(1, TENSOR):
            source = whole.at[:, row_block(peers[TENSOR - k])]
            remote(source, source, send.at[k], recv.at[k], dp, peers[k]).wait_recv()
        for copy in copies:
            copy.wait_send()

    return finish


def inverse_rms(signal):
    return lax.rsqrt(jnp.mean(signal * signal, axis=-1, keepdims=True) + EPSILON)


def norm_back(normed, inverse, gain, upstream):
    inner = upstream * (1.0 + gain)
    return inverse * (inner - normed * jnp.mean(inner * normed, axis=-1, keepdims=True))


def over_rows(term):
    return jnp.sum(term, axis=(0, 1))[None]


def load_rows(whole, block, local):
    copy = pltpu.make_async_copy(
        whole.at[:, row_block(lax.axis_index("tensor"))], block, local
    )
    copy.start()
    return copy


def feed_kernel(
    part, cotangent, middle, gains, d_feed, final, sums, held, mine, block, send, recv, local
):
    greet_tensor()
    copies = scatter_rows(part, held, send.at[0], recv.at[0], local.at[0])
    load = load_rows(cotangent, mine, local.at[1])
    load.wait()
    signal = summed(held, copies)
    inverse = inverse_rms(signal)
    normed = signal * inverse
    upstream = mine[...].astype(F32)
    lowered = norm_back(normed, inverse, gains[3:4], upstream).astype(B16)
    block[...] = lowered
    finish = spread_rows(block, d_feed, send.at[1], recv.at[1], local.at[2])
    final[...] = (middle[...] + normed * (1.0 + gains[3:4])).astype(B16)
    sums[0:1] = over_rows(upstream * normed)
    sums[1:2] = over_rows(lowered.astype(F32) * signal)
    for copy in copies:
        copy.wait_send()
    finish()


def tensor_call(
    kernel, name, collective_id, depth, loaded, operands, in_specs, outs, out_specs, blocks
):
    return pl.pallas_call(
        kernel,
        name=name,
        out_shape=outs,
        in_specs=in_specs,
        out_specs=out_specs,
        scratch_shapes=[
            pltpu.VMEM((TENSOR, depth, SLICE, WIDE), B16),
            pltpu.VMEM((loaded, SLICE, WIDE), B16),
        ]
        + blocks
        + [
            pltpu.SemaphoreType.DMA((3, TENSOR)),
            pltpu.SemaphoreType.DMA((3, TENSOR)),
            pltpu.SemaphoreType.DMA((4,)),
        ],
        compiler_params=params(collective_id),
    )(*operands)


def unit_owner(micro, width):
    return rank(width, micro, 0)


def rotate(signal, cosine, sine):
    former, latter = signal[:, : HD // 2], signal[:, HD // 2 :]
    return jnp.concatenate([former * cosine - latter * sine, latter * cosine + former * sine], -1)


def unrotate(signal, cosine, sine):
    former, latter = signal[:, : HD // 2], signal[:, HD // 2 :]
    return jnp.concatenate([former * cosine + latter * sine, latter * cosine - former * sine], -1)


def block_scores(queries, keys, first, b, kb):
    scores = lax.dot_general(queries, keys, (((1,), (1,)), ((), ())), preferred_element_type=F32)
    bent = jnp.tanh(scores * (0.0625 / SOFTCAP))
    lane = lax.broadcasted_iota(jnp.int32, (256, 256), 1)
    row = lax.broadcasted_iota(jnp.int32, (256, 256), 0)
    key_place = (16 * kb + (lane & 15)) * 16 + (lane >> 4)
    query_place = (16 * b + (row & 15)) * 16 + (row >> 4)
    allowed = (key_place >= first) & (key_place <= query_place)
    return bent, jnp.where(allowed, SOFTCAP * bent, MASKED)


def block_probs(queries, keys, first, b):
    pieces = [
        block_scores(queries, keys[kb], first, b, kb) for kb in range(max(0, b - 2), b + 1)
    ]
    peak = functools.reduce(
        jnp.maximum, [jnp.max(capped, axis=-1, keepdims=True) for _, capped in pieces]
    )
    exps = [jnp.exp(capped - peak) for _, capped in pieces]
    total = functools.reduce(jnp.add, [jnp.sum(e, axis=-1, keepdims=True) for e in exps])
    return [bent for bent, _ in pieces], [e / total for e in exps]


def dot(left, right, left_dim, right_dim):
    return lax.dot_general(
        left, right, (((left_dim,), (right_dim,)), ((), ())), preferred_element_type=F32
    )


def front_kernel(*refs):
    shards, refs = refs[:4], refs[4:]
    (tokens, gains, scale_qkv, scale_out, first, cosine, sine), refs = refs[:7], refs[7:]
    (w_qkv, w_out, w_gu, w_down, normed_middle), refs = refs[:5], refs[5:]
    (attended, normed_input, qkv_pre, q_rot, k_rot, v_all, branch, middle), refs = refs[:8], refs[8:]
    (wq, wo, low, rq, rkv, held, att, part), refs = refs[:8], refs[8:]
    (held_x, held_z, stage, block, *row_sems), refs = refs[:7], refs[7:]
    (send_g, recv_g, local_g, send, recv_q, recv_kv, send_back, recv_back, local) = refs
    y, zh, core, t = here()
    me = rank(y, zh, core)
    half = lax.rem(t, 2)
    other = t + 1 - 2 * half
    owner = (y < 3) & (core == 0)
    units = [(m, w) for m in range(2) for w in range(3)]
    gathers = [
        Gather(src, out, send_g.at[k], recv_g.at[k], local_g.at[k])
        for k, (src, out) in enumerate(zip(shards, (wq, wo, w_gu, w_down)))
    ]
    g_qkv, g_out, g_gu, g_down = gathers
    rows = Rows(part, held_x, held_z, stage, block, normed_middle, row_sems)
    barrier = pltpu.get_barrier_semaphore()

    def signal(dp, tensor):
        pl.semaphore_signal(barrier, inc=1, device_id=(dp, tensor), device_id_type=MESH)

    plane = [(g_qkv.sib, t), (g_qkv.zz, t)] + [(dp, t) for dp in g_qkv.fore] + rows.peers()
    for device in plane:
        signal(*device)

    @pl.when(owner)
    def _():
        def each(d, _):
            pl.when(d != me)(lambda: signal(d, t))
            signal(d, other)
            return 0

        lax.fori_loop(0, 16, each, 0)

    for m, w in units:
        pl.when(unit_owner(m, w) != me)(functools.partial(signal, unit_owner(m, w), t))

    @pl.when(owner)
    def _():
        pl.semaphore_wait(barrier, len(plane) + 26)

    @pl.when(jnp.logical_not(owner))
    def _():
        pl.semaphore_wait(barrier, len(plane) + 12)

    g_qkv.start()
    g_out.start()
    inputs = tokens[...].astype(F32)
    normed_input[...] = (inputs * inverse_rms(inputs) * (1.0 + gains[0:1])).astype(B16)
    for gather in (g_qkv, g_out):
        gather.over_y()
        gather.over_z()
    for gather in (g_qkv, g_out):
        gather.near()
        gather.far()
    g_qkv.end()

    for i in range(2):
        cols = slice(HD * i, HD * i + HD)
        codes = wq[:, :, cols].reshape(WIDE, HD)
        for w in range(3):
            product = dot(normed_input[...], level(codes, w), 1, 0) * scale_qkv[:, cols]
            qkv_pre[w, :, cols] = product
            low[w, :, :, cols] = product.astype(B16).reshape(2, 64, HD)

    def to_owner(u, m, w, start):
        o = unit_owner(m, w)
        q_src, kv_src = low.at[w, m, :, pl.ds(0, HD)], low.at[w, m, :, pl.ds(HD, HD)]
        across = remote(kv_src, rkv.at[half, me], send.at[u, 2], recv_kv.at[half, me], o, other)
        away = [
            remote(q_src, rq.at[me], send.at[u, 0], recv_q.at[me], o, t),
            remote(kv_src, rkv.at[half, me], send.at[u, 1], recv_kv.at[half, me], o, t),
        ]
        near = [
            pltpu.make_async_copy(q_src, rq.at[me], local.at[0]),
            pltpu.make_async_copy(kv_src, rkv.at[half, me], local.at[1]),
        ]

        @pl.when(o != me)
        def _():
            for copy in away:
                copy.start() if start else copy.wait_send()

        @pl.when(o == me)
        def _():
            for copy in near:
                copy.start() if start else copy.wait()

        across.start() if start else across.wait_send()

    for u, (m, w) in enumerate(units):
        to_owner(u, m, w, True)

    @pl.when(owner)
    def _():
        for u, (m, w) in enumerate(units):

            @pl.when(unit_owner(m, w) == me)
            def _():
                for i in range(2):
                    ref = (rq.at[me], rkv.at[half, me])[i]
                    pltpu.make_async_copy(ref, ref, local.at[i]).wait()

        def each(d, _):
            @pl.when(d != me)
            def _():
                remote(rq.at[d], rq.at[d], send.at[0, 0], recv_q.at[d], me, other).wait_recv()
                remote(
                    rkv.at[half, d], rkv.at[half, d], send.at[0, 0], recv_kv.at[half, d], me, other
                ).wait_recv()

            remote(
                rkv.at[1 - half, d], rkv.at[1 - half, d], send.at[0, 0], recv_kv.at[1 - half, d], me, other
            ).wait_recv()
            return 0

        lax.fori_loop(0, 16, each, 0)
        for b in range(4):
            rows_b = slice(16 * b, 16 * b + 16)
            c, s = cosine[b], sine[b]
            q = rq[:, rows_b, :].reshape(256, HD).astype(F32)
            q_rot[b] = rotate(q, c, s).astype(B16)
            k = jnp.concatenate(
                [rkv[i, :, rows_b, : HD // 2].reshape(256, HD // 2) for i in range(2)], -1
            )
            k_rot[b] = rotate(k.astype(F32), c, s).astype(B16)
            v_all[b] = jnp.concatenate(
                [rkv[i, :, rows_b, HD // 2 :].reshape(256, HD // 2) for i in range(2)], -1
            )
        for b in range(4):
            keys = {kb: k_rot[kb] for kb in range(max(0, b - 2), b + 1)}
            _, probs = block_probs(q_rot[b], keys, first[b], b)
            out = sum(
                dot(p.astype(B16), v_all[kb], 1, 0) for p, kb in zip(probs, sorted(keys))
            )
            held[:, 16 * b : 16 * b + 16, :] = out.astype(B16).reshape(16, 16, HD)

        def hand_back(d, start):
            @pl.when(d != me)
            def _():
                copy = remote(
                    held.at[d], att.at[y, zh], send_back.at[d], recv_back.at[zh * 3 + y], d, t
                )
                copy.start() if start else copy.wait_send()

            @pl.when(d == me)
            def _():
                copy = pltpu.make_async_copy(held.at[d], att.at[y, zh], local.at[0])
                copy.start() if start else copy.wait()

        lax.fori_loop(0, 16, lambda d, _: (hand_back(d, True), 0)[1], 0)
        lax.fori_loop(0, 16, lambda d, _: (hand_back(d, False), 0)[1], 0)

    g_gu.start()
    g_down.start()
    g_out.end()
    for u, (m, w) in enumerate(units):

        @pl.when(unit_owner(m, w) != me)
        def _():
            ref = att.at[w, m]
            remote(ref, ref, send.at[0, 0], recv_back.at[u], me, other).wait_recv()

    codes = wo[...].reshape(WIDE, HD)
    for w in range(3):
        product = dot(att[w].reshape(ROWS, HD), level(codes, w), 1, 1) * scale_out[...]
        part[w] = product.astype(B16).reshape(2, 4, SLICE, WIDE)
        rows.scatter_x(w)
    attended[...] = att[...]
    keep = [
        pltpu.make_async_copy(src, dst, local.at[i])
        for i, (src, dst) in enumerate(((wq, w_qkv), (wo, w_out)))
    ]
    for copy in keep:
        copy.start()
    g_gu.over_y()
    g_down.over_y()
    g_gu.over_z()
    g_down.over_z()
    for w in range(3):
        rows.scatter_z(w)
    mine = tokens[pl.ds(pl.multiple_of(t * SLICE, SLICE), SLICE)].astype(F32)
    for w in range(3):
        signal_w = rows.total(w)
        branch[w] = signal_w
        total = mine + signal_w * inverse_rms(signal_w) * (1.0 + gains[1:2])
        middle[w] = total
        block[w] = (total * inverse_rms(total) * (1.0 + gains[2:3])).astype(B16)
        rows.spread(w)
    for gather in (g_gu, g_down):
        gather.near()
    for w in range(3):
        rows.forward(w)
    for gather in (g_gu, g_down):
        gather.far()
    for w in range(3):
        rows.end(w)
    for gather in (g_gu, g_down):
        gather.end()
    for copy in keep:
        copy.wait()
    for u, (m, w) in enumerate(units):
        o = unit_owner(m, w)

        @pl.when(o != me)
        def _():
            for slot, src in enumerate((low.at[w, m, :, pl.ds(0, HD)], low.at[w, m, :, pl.ds(HD, HD)])):
                remote(src, src, send.at[u, slot], recv_q.at[0], o, t).wait_send()

        src = low.at[w, m, :, pl.ds(HD, HD)]
        remote(src, src, send.at[u, 2], recv_q.at[0], o, other).wait_send()
    rows.drain()
    for gather in gathers:
        gather.drain()


def front(shards, tokens, gains, scale_qkv, scale_out, first, cosine, sine):
    return pl.pallas_call(
        front_kernel,
        name="front",
        out_shape=[struct((16,) + shard.shape, B16) for shard in shards]
        + [
            struct((3, 2, 4, SLICE, WIDE), B16),
            struct((3, 2, 64, HD), B16),
            struct((ROWS, WIDE), B16),
            struct((3, ROWS, 2 * HD), F32),
        ]
        + [struct((4, 256, HD), B16)] * 3
        + [struct((3, SLICE, WIDE), F32)] * 2,
        in_specs=any_space(4) + vmem_space(7),
        out_specs=any_space(5) + vmem_space(8),
        scratch_shapes=[
            pltpu.VMEM((16, SHARD, 2 * HD), B16),
            pltpu.VMEM((16, SHARD, HD), B16),
            pltpu.VMEM((3, 2, 64, 2 * HD), B16),
            pltpu.VMEM((16, 64, HD), B16),
            pltpu.VMEM((2, 16, 64, HD), B16),
            pltpu.VMEM((16, 64, HD), B16),
            pltpu.VMEM((3, 2, 64, HD), B16),
            pltpu.VMEM((3, 2, 4, SLICE, WIDE), B16),
        ]
        + rows_scratch(3)
        + [
            pltpu.SemaphoreType.DMA((4, 29)),
            pltpu.SemaphoreType.DMA((4, 29)),
            pltpu.SemaphoreType.DMA((4,)),
            pltpu.SemaphoreType.DMA((6, 3)),
            pltpu.SemaphoreType.DMA((16,)),
            pltpu.SemaphoreType.DMA((2, 16)),
            pltpu.SemaphoreType.DMA((16,)),
            pltpu.SemaphoreType.DMA((6,)),
            pltpu.SemaphoreType.DMA((2,)),
        ],
        compiler_params=params(3),
    )(*shards, tokens, gains, scale_qkv[None], scale_out[None], first, cosine, sine)


GRADIENTS = (1152, 1152, 1152, HD, 2 * HD)


def back_kernel(*refs):
    (part, cotangent), refs = refs[:2], refs[2:]
    (turned_middle, turned_feed, d_gu, hidden, middle, branch, final, feed_sums, gu_sums), refs = refs[:9], refs[9:]
    (w_out, w_qkv, scale_out, scale_down, scale_qkv, gains, tokens, attended, normed_input), refs = refs[:9], refs[9:]
    (qkv_pre, first, cosine, sine, q_rot, k_rot, v_all), refs = refs[:7], refs[7:]
    (results, gradient, totals), refs = refs[:3], refs[3:]
    outs, refs = refs[:5], refs[5:]
    aways, refs = refs[:2], refs[2:]
    reduces = []
    for k, columns in enumerate(GRADIENTS):
        held, refs = refs[:8], refs[8:]
        away = aways[k % 2]
        reduces.append(Reduce(columns, away, *held[:6], outs[k], *held[6:]))
    g_gate, g_up, g_down, g_out, g_qkv = reduces
    (own_part, cot, d_branch), refs = refs[:3], refs[3:]
    (held_x, held_z, stage, block, *row_sems), refs = refs[:7], refs[7:]
    (part_in, held_x1, held_z1, stage1, _, *row_sems1), refs = refs[:8], refs[8:]
    (result_sems, block1), refs = (refs[:3], refs[3]), refs[4:]
    (vec_x, vec_z, vec_sib, vec_y, vec_zz, vec, send_v, recv_v), refs = refs[:8], refs[8:]
    (datt, rdo, held_q, held_kv, acc_k, acc_v, d_query, d_kv), refs = refs[:8], refs[8:]
    send, recv, send_q, send_kv, recv_q, recv_kv, local = refs
    y, zh, core, t = here()
    me = rank(y, zh, core)
    half = lax.rem(t, 2)
    other = t + 1 - 2 * half
    owner = (y < 3) & (core == 0)
    units = [(m, w) for m in range(2) for w in range(3)]
    rows = Rows(part, held_x, held_z, stage, block, d_branch, row_sems, own_part)
    rows_in = Rows(part_in, held_x1, held_z1, stage1, block1, gradient, row_sems1)
    rows_out = Rows(None, None, None, None, final, results, result_sems)
    barrier = pltpu.get_barrier_semaphore()

    def signal(dp, tensor):
        pl.semaphore_signal(barrier, inc=1, device_id=(dp, tensor), device_id_type=MESH)

    plane = [(g_gate.sib, t), (g_gate.zz, t)] + [(dp, t) for dp in g_gate.fore] + rows.peers()
    for device in plane:
        signal(*device)

    @pl.when(owner)
    def _():
        def each(d, _):
            pl.when(d != me)(lambda: signal(d, t))
            return 0

        lax.fori_loop(0, 16, each, 0)

    for m, w in units:
        pl.when(unit_owner(m, w) != me)(functools.partial(signal, unit_owner(m, w), t))
        signal(unit_owner(m, w), other)

    @pl.when(owner)
    def _():
        pl.semaphore_wait(barrier, len(plane) + 36)

    @pl.when(jnp.logical_not(owner))
    def _():
        pl.semaphore_wait(barrier, len(plane) + 6)

    for w in range(3):
        rows.scatter_x(w)
    loads = [
        pltpu.make_async_copy(part.at[:, :, rows.x], own_part, local.at[0]),
        pltpu.make_async_copy(cotangent.at[:, rows.zl, rows.x], cot, local.at[1]),
    ]
    for copy in loads:
        copy.start()
    g_gate.product(turned_middle, d_gu)
    for copy in loads:
        copy.wait()
    rows.scatter_z(0)
    g_up.product(turned_middle, d_gu, 1152)
    rows.scatter_z(1)
    g_gate.sent_away()
    g_down.product(turned_feed, hidden)
    rows.scatter_z(2)
    d_middle = jnp.zeros((SLICE, WIDE), F32)
    sums = [jnp.zeros((1, WIDE), F32)] * 3
    for w in range(3):
        upstream = rows.total(w)
        signal_w = middle[w]
        inverse = inverse_rms(signal_w)
        normed = signal_w * inverse
        d_signal = cot[w].astype(F32) + norm_back(normed, inverse, gains[2:3], upstream)
        lower = branch[w]
        inverse_lower = inverse_rms(lower)
        normed_lower = lower * inverse_lower
        lowered = norm_back(normed_lower, inverse_lower, gains[1:2], d_signal).astype(B16)
        block[w] = lowered
        rows.spread(w)
        d_middle = d_middle + d_signal
        terms = (d_signal * normed_lower, upstream * normed, lowered.astype(F32) * lower)
        sums = [old + jnp.sum(new, axis=0, keepdims=True) for old, new in zip(sums, terms)]
        if w == 0:
            g_gate.add()
    g_up.add()
    vec[1:2] = sums[0]
    vec[2:3] = sums[1]
    vec[3:4] = feed_sums[0:1]
    vec[4:5] = sums[2] / scale_out[...]
    vec[5:6] = feed_sums[1:2] / scale_down[...]

    codes = w_out[...].reshape(WIDE, HD)

    def to_owner(u, m, w, start):
        o = unit_owner(m, w)
        src = datt.at[w, m]

        @pl.when(o != me)
        def _():
            copy = remote(src, rdo.at[me], send.at[u], recv.at[me], o, t)
            copy.start() if start else copy.wait_send()

        @pl.when(o == me)
        def _():
            copy = pltpu.make_async_copy(src, rdo.at[me], local.at[0])
            copy.start() if start else copy.wait()

    for w in range(3):
        rows.forward(w)
    for w in range(3):
        rows.end(w)
        scaled = (d_branch[w].reshape(ROWS, WIDE).astype(F32) * scale_out[...]).astype(B16)
        datt[w] = dot(scaled, level(codes, w), 1, 0).astype(B16).reshape(2, 64, HD)
        for m in range(2):
            to_owner(m * 3 + w, m, w, True)
    for u, (m, w) in enumerate(units):
        to_owner(u, m, w, False)

    @pl.when(owner)
    def _():
        def each(d, _):
            @pl.when(d != me)
            def _():
                remote(rdo.at[d], rdo.at[d], send.at[0], recv.at[d], me, other).wait_recv()

            return 0

        lax.fori_loop(0, 16, each, 0)
        acc_k[...] = jnp.zeros_like(acc_k)
        acc_v[...] = jnp.zeros_like(acc_v)
        for b in range(4):
            rows_b = slice(16 * b, 16 * b + 16)
            blocks = list(range(max(0, b - 2), b + 1))
            queries = q_rot[b]
            keys = {kb: k_rot[kb] for kb in blocks}
            upstream = rdo[:, rows_b, :].reshape(256, HD)
            bents, probs = block_probs(queries, keys, first[b], b)
            d_probs = [dot(upstream, v_all[kb], 1, 1) for kb in blocks]
            centre = sum(
                jnp.sum(p * dp, axis=-1, keepdims=True) for p, dp in zip(probs, d_probs)
            )
            d_q = jnp.zeros((256, HD), F32)
            for kb, bent, p, dp in zip(blocks, bents, probs, d_probs):
                d_scores = (p * (dp - centre) * (1.0 - bent * bent)).astype(B16)
                d_q = d_q + dot(d_scores, keys[kb], 1, 0)
                acc_k[kb] += dot(d_scores, queries, 0, 0)
                acc_v[kb] += dot(p.astype(B16), upstream, 0, 0)
            d_q = unrotate(d_q * 0.0625, cosine[b], sine[b])
            held_q[:, rows_b, :] = d_q.astype(B16).reshape(16, 16, HD)
        for b in range(4):
            rows_b = slice(16 * b, 16 * b + 16)
            d_k = unrotate(acc_k[b] * 0.0625, cosine[b], sine[b]).astype(B16)
            d_v = acc_v[b].astype(B16)
            for i in range(2):
                cols = slice(128 * i, 128 * i + 128)
                held_kv[i, :, rows_b, :128] = d_k[:, cols].reshape(16, 16, 128)
                held_kv[i, :, rows_b, 128:] = d_v[:, cols].reshape(16, 16, 128)

    def hand_back(d, start):
        u = zh * 3 + y
        across = remote(
            held_kv.at[1 - half, d], d_kv.at[half, y, zh], send_kv.at[1, d], recv_kv.at[half, u], d, other
        )
        across.start() if start else across.wait_send()

        @pl.when(d != me)
        def _():
            for copy in (
                remote(held_q.at[d], d_query.at[y, zh], send_q.at[d], recv_q.at[u], d, t),
                remote(
                    held_kv.at[half, d], d_kv.at[half, y, zh], send_kv.at[0, d], recv_kv.at[half, u], d, t
                ),
            ):
                copy.start() if start else copy.wait_send()

        @pl.when(d == me)
        def _():
            for copy in (
                pltpu.make_async_copy(held_q.at[d], d_query.at[y, zh], local.at[0]),
                pltpu.make_async_copy(held_kv.at[half, d], d_kv.at[half, y, zh], local.at[1]),
            ):
                copy.start() if start else copy.wait()

    @pl.when(owner)
    def _():
        lax.fori_loop(0, 16, lambda d, _: (hand_back(d, True), 0)[1], 0)
        lax.fori_loop(0, 16, lambda d, _: (hand_back(d, False), 0)[1], 0)

    g_up.sent_away()
    g_out.product_whole(d_branch[...].reshape(3 * ROWS, WIDE), attended[...])
    g_down.add()
    g_gate.merge()
    g_gate.pool()
    for u, (m, w) in enumerate(units):

        @pl.when(unit_owner(m, w) != me)
        def _():
            ref = d_query.at[w, m]
            remote(ref, ref, send.at[0], recv_q.at[u], me, other).wait_recv()
            ref = d_kv.at[half, w, m]
            remote(ref, ref, send.at[0], recv_kv.at[half, u], me, other).wait_recv()

        ref = d_kv.at[1 - half, w, m]
        remote(ref, ref, send.at[0], recv_kv.at[1 - half, u], me, other).wait_recv()

    codes = w_qkv[...].reshape(WIDE, 2 * HD)
    d_input = jnp.zeros((ROWS, WIDE), F32)
    qkv_sums = jnp.zeros((1, 2 * HD), F32)
    d_qkv_all = jnp.zeros((ROWS, 2 * HD), F32)
    for w in range(3):
        both = (d_kv[0, w].astype(F32) + d_kv[1, w].astype(F32)).astype(B16).astype(F32)
        d_qkv = jnp.concatenate([d_query[w].astype(F32), both], -1).reshape(ROWS, 2 * HD)
        qkv_sums = qkv_sums + jnp.sum(d_qkv * qkv_pre[w], axis=0, keepdims=True)
        d_qkv_all = d_qkv_all + d_qkv
        scaled = (d_qkv * scale_qkv[...]).astype(B16)
        d_input = d_input + dot(scaled, level(codes, w), 1, 1)
    part_in[0] = d_input.astype(B16).reshape(2, 4, SLICE, WIDE)
    rows_in.scatter_x(0)
    g_down.sent_away()
    g_qkv.product_whole(normed_input[...], d_qkv_all.astype(B16))
    g_out.add()
    g_up.merge()
    g_up.pool()
    rows_in.scatter_z(0)
    g_qkv.add()

    upstream = rows_in.total(0)
    signal_in = tokens[pl.ds(pl.multiple_of(t * SLICE, SLICE), SLICE)].astype(F32)
    inverse = inverse_rms(signal_in)
    normed = signal_in * inverse
    block1[0] = d_middle + norm_back(normed, inverse, gains[0:1], upstream)
    rows_in.spread(0)

    vec[0:1] = jnp.sum(upstream * normed, axis=0, keepdims=True)
    vec[6:8] = jnp.zeros((2, WIDE), F32)
    x = rows.x
    copies = []

    def exchange(slot, src, dst, dp, tensor):
        copy = remote(src, dst, send_v.at[slot], recv_v.at[slot], dp, tensor)
        copy.start()
        copies.append(copy)

    def exchanged(slot, ref):
        remote(ref, ref, send_v.at[slot], recv_v.at[slot], me, other).wait_recv()

    vec_x[x] = vec[...]
    for k in range(3):
        exchange(k, vec_x.at[x], vec_x.at[x], me, rows.x_peers[k])
    g_down.merge()
    g_down.pool()
    g_gate.end()
    for k in range(3):
        exchanged(k, vec_x.at[rows.behind[k]])
    vec[...] = functools.reduce(jnp.add, [vec_x[i] for i in range(4)])
    exchange(3, vec, vec_z, me, rows.z_peer)
    rows_in.forward(0)
    for w in range(3):
        rows_out.spread(w)
    g_out.merge()
    g_out.pool()
    exchanged(3, vec_z)
    copies[3].wait_send()
    vec[0:6] = vec[0:6] + vec_z[0:6]
    vec[6:7] = gu_sums[...]
    vec[7:8, : 2 * HD] = qkv_sums / scale_qkv[...]
    exchange(4, vec, vec_sib, g_gate.sib, t)
    g_qkv.merge()
    g_qkv.pool()
    for w in range(3):
        rows_out.forward(w)
    exchanged(4, vec_sib)
    vec_y[y] = vec[...] + vec_sib[...]
    for i in range(3):
        exchange(5 + i, vec_y.at[y], vec_y.at[y], g_gate.fore[i], t)
    g_up.end()
    g_down.end()
    for i in range(3):
        exchanged(5 + i, vec_y.at[lax.rem(y + 3 - i, 4)])
    copies[4].wait_send()
    vec[...] = functools.reduce(jnp.add, [vec_y[i] for i in range(4)])
    exchange(8, vec, vec_zz, g_gate.zz, t)
    g_out.end()
    g_qkv.end()
    exchanged(8, vec_zz)
    totals[...] = vec[...] + vec_zz[...]
    rows_in.end(0)
    for w in range(3):
        rows_out.end(w)
    g_out.sent_away()
    g_qkv.sent_away()
    for k in (0, 1, 2, 5, 6, 7, 8):
        copies[k].wait_send()
    for part_of in (rows, rows_in, rows_out, *reduces):
        part_of.drain()


def back(hbm, vmem):
    def vec():
        return pltpu.VMEM((8, WIDE), F32)

    scratch = [pltpu.VMEM((8, SHARD, 1152), B16)] * 2
    for columns in GRADIENTS:
        scratch += reduce_scratch(columns)
    scratch += [
        pltpu.VMEM((3, 2, SLICE, WIDE), B16),
        pltpu.VMEM((3, SLICE, WIDE), B16),
        pltpu.VMEM((3, 2, 4, SLICE, WIDE), B16),
    ]
    scratch += rows_scratch(3)
    scratch += [pltpu.VMEM((1, 2, 4, SLICE, WIDE), B16)] + rows_scratch(1)
    scratch += rows_scratch(3)[4:] + [pltpu.VMEM((1, SLICE, WIDE), F32)]
    scratch += [pltpu.VMEM((4, 8, WIDE), F32), vec(), vec(), pltpu.VMEM((4, 8, WIDE), F32), vec(), vec()]
    scratch += [pltpu.SemaphoreType.DMA((9,))] * 2
    scratch += [
        pltpu.VMEM((3, 2, 64, HD), B16),
        pltpu.VMEM((16, 64, HD), B16),
        pltpu.VMEM((16, 64, HD), B16),
        pltpu.VMEM((2, 16, 64, HD), B16),
        pltpu.VMEM((4, 256, HD), F32),
        pltpu.VMEM((4, 256, HD), F32),
        pltpu.VMEM((3, 2, 64, HD), B16),
        pltpu.VMEM((2, 3, 2, 64, HD), B16),
        pltpu.SemaphoreType.DMA((6,)),
        pltpu.SemaphoreType.DMA((16,)),
        pltpu.SemaphoreType.DMA((16,)),
        pltpu.SemaphoreType.DMA((2, 16)),
        pltpu.SemaphoreType.DMA((6,)),
        pltpu.SemaphoreType.DMA((2, 6)),
        pltpu.SemaphoreType.DMA((2,)),
    ]
    return pl.pallas_call(
        back_kernel,
        name="back",
        out_shape=[
            struct((3, 2, 4, SLICE, WIDE), B16),
            struct((1, 2, 4, SLICE, WIDE), F32),
            struct((8, WIDE), F32),
        ]
        + [struct((SHARD, columns), F32) for columns in GRADIENTS],
        in_specs=any_space(len(hbm)) + vmem_space(len(vmem)),
        out_specs=any_space(2) + vmem_space(6),
        scratch_shapes=scratch,
        compiler_params=params(4),
    )(*hbm, *vmem)


def level(codes, width):
    if width == 0:
        return codes
    stride = (1, 16, 64)[width]
    return jnp.floor(codes * B16(1.0 / stride)) * B16(stride) + B16(stride // 2)


def gelu_parts(value):
    slope = 0.7978845608028654
    inner = jnp.tanh(slope * (value + 0.044715 * value * value * value))
    grown = 0.5 * value * (1.0 + inner)
    rate = 0.5 * (1.0 + inner) + 0.5 * value * (1.0 - inner * inner) * slope * (
        1.0 + 3 * 0.044715 * value * value
    )
    return grown, rate


def body(
    tokens,
    cotangent,
    segments,
    codes_query,
    codes_key,
    codes_value,
    codes_out,
    codes_gate,
    codes_up,
    codes_down,
    query_column_scale,
    key_column_scale,
    value_column_scale,
    output_column_scale,
    gate_column_scale,
    up_column_scale,
    down_column_scale,
    gain_first,
    gain_second,
    gain_third,
    gain_fourth,
):
    widths = range(3)
    z_hi = lax.rem(lax.div(lax.axis_index("dp"), 2), 2)
    tokens = tokens.reshape(ROWS, WIDE)
    cotangent = cotangent.reshape(3, ROWS, WIDE)
    gains = jnp.stack([gain_first, gain_second, gain_third, gain_fourth])
    shards = [
        jnp.concatenate([codes_query, codes_key, codes_value], 1).astype(B16),
        codes_out.astype(B16).T,
        jnp.concatenate([codes_gate, codes_up], 1).astype(B16),
        codes_down.astype(B16).T,
    ]
    scale_qkv = jnp.concatenate([query_column_scale, key_column_scale, value_column_scale])
    scale_gu = jnp.concatenate([gate_column_scale, up_column_scale])

    documents = lax.dynamic_index_in_dim(segments, z_hi, 0, False)
    starts = jnp.sum((documents[None, :] < documents[:, None]).astype(jnp.int32), axis=1)
    place = jnp.arange(1024, dtype=jnp.int32)

    def blocked(rows):
        return rows.reshape(4, 16, 16).transpose(0, 2, 1).reshape(4, 256)

    first = blocked(starts)[:, :, None]
    expo = jnp.arange(HD // 2, dtype=F32) * (2.0 / HD)
    angle = blocked(place - starts).astype(F32)[:, :, None] * jnp.power(ROPE_BASE, -expo)
    cosine, sine = jnp.cos(angle), jnp.sin(angle)

    *weights, normed_middle, attended, normed_input, qkv_pre, q_rot, k_rot, v_all, branch, middle = front(
        shards, tokens, gains, scale_qkv, output_column_scale, first, cosine, sine
    )
    w_qkv, w_out, w_gu, w_down = (gathered.reshape(WIDE, -1) for gathered in weights)
    attended = attended.reshape(3, ROWS, HD)
    normed_middle = normed_middle.reshape(3, ROWS, WIDE)
    gu_pre = jnp.stack([dot(normed_middle[w], level(w_gu, w), 1, 0) * scale_gu for w in widths])
    half = gu_pre.shape[-1] // 2
    gate_pre, up_pre = gu_pre[..., :half], gu_pre[..., half:]
    grown, rate = gelu_parts(gate_pre)
    hidden = (grown * up_pre).astype(B16)
    feed_part = jnp.stack(
        [dot(hidden[w], level(w_down, w), 1, 1) * down_column_scale for w in widths]
    ).astype(B16)
    d_feed, final, feed_sums = tensor_call(
        feed_kernel,
        "feed",
        6,
        3,
        3,
        (feed_part, cotangent, middle, gains),
        any_space(2) + vmem_space(2),
        [struct((3, ROWS, WIDE), B16), struct((3, SLICE, WIDE), B16), struct((8, WIDE), F32)],
        any_space(1) + vmem_space(2),
        [pltpu.VMEM((3, SLICE, WIDE), B16)],
    )

    d_feed_scaled = (d_feed.astype(F32) * down_column_scale).astype(B16)
    d_hidden = jnp.stack([dot(d_feed_scaled[w], level(w_down, w), 1, 0) for w in widths])
    d_gu = jnp.concatenate([d_hidden * up_pre * rate, d_hidden * grown], -1)
    d_gu_low = d_gu.astype(B16)
    gu_sums = jnp.sum(d_gu_low.astype(F32) * gu_pre, axis=(0, 1)) / scale_gu
    d_gu_scaled = (d_gu * scale_gu).astype(B16)
    d_middle_part = jnp.stack([dot(d_gu_scaled[w], level(w_gu, w), 1, 1) for w in widths]).astype(
        B16
    )
    flat = (3 * ROWS, -1)
    grid = (3, 2, 4, SLICE, WIDE)
    results, input_gradient, totals, g_gate, g_up, g_down, g_out, g_qkv = back(
        [d_middle_part.reshape(grid), cotangent.reshape(grid)],
        [
            normed_middle.reshape(flat).T,
            d_feed.reshape(flat).T,
            d_gu_low.reshape(flat),
            hidden.reshape(flat),
            middle,
            branch,
            final,
            feed_sums,
            gu_sums[None],
            weights[1],
            weights[0],
            output_column_scale[None],
            down_column_scale[None],
            scale_qkv[None],
            gains,
            tokens,
            attended.reshape(flat),
            normed_input,
            qkv_pre,
            first,
            cosine,
            sine,
            q_rot,
            k_rot,
            v_all,
        ],
    )
    rows = lax.dynamic_slice_in_dim(totals, lax.axis_index("dp") * SHARD, SHARD, 1)
    return (
        results.reshape(3, 2, 64, 1, WIDE),
        input_gradient.reshape(2, 64, 1, WIDE),
        g_qkv[:, :256],
        g_qkv[:, 256:384],
        g_qkv[:, 384:],
        g_out.T,
        g_gate,
        g_up,
        g_down.T,
        totals[7, :256],
        totals[7, 256:384],
        totals[7, 384:512],
        rows[4],
        totals[6, :half],
        totals[6, half:],
        rows[5],
        rows[0],
        rows[1],
        rows[2],
        rows[3],
    )


def solution(mesh):
    matrix, turned = P("dp", "tensor"), P("tensor", "dp")
    columns, whole, shard = P("tensor"), P(), P("dp")
    in_specs = (
        P(None, None, "dp", None),
        P(None, None, None, "dp", None),
        whole,
        *(matrix, matrix, matrix, turned, matrix, matrix, turned),
        *(columns, columns, columns, whole, columns, columns, whole),
        *(whole, whole, whole, whole),
    )
    out_specs = (
        P(None, None, None, "dp", None),
        P(None, None, "dp", None),
        *(matrix, matrix, matrix, turned, matrix, matrix, turned),
        *(columns, columns, columns, shard, columns, columns, shard),
        *(shard, shard, shard, shard),
    )
    return jax.shard_map(body, mesh=mesh, in_specs=in_specs, out_specs=out_specs, check_vma=False)
```

time: 742 us -> 451 us (0.61)
  blocking collectives: 141 us -> 0 us
  Pallas kernels: 457 us -> 340 us
  matrix products: 60.1 us -> 34.3 us
  other arithmetic: 38.9 us -> 28.9 us
    pallas_call x4 -> x1, Pallas kernels: 207 us -> 49.7 us  [tensor_call(): pl.pallas_call(kernel, name=name, out_shape=outs, in_specs=in_specs, out_...]
    psum x2 -> x0, blocking collectives: 141 us -> none  [the longest x1 72.7 us: body(): rows = lax.psum(rows, ('dp', 'tensor'))]
    pallas_call x4 -> x2, Pallas kernels: 250 us -> 290 us  [the longest x1 168 us: back(): pl.pallas_call(back_kernel, name='back', out_shape=[struct((3, 2, 4, SLIC...]
    dot_general x28 -> x12, matrix products: 60.1 us -> 34.3 us  [dot(): lax.dot_general(left, right, (((left_dim,), (right_dim,)), ((), ())), pre...]
    add x4 -> x2, other arithmetic: 16.2 us -> 11.3 us  [level(): return jnp.floor(codes * B16(1.0 / stride)) * B16(stride) + B16(stride // 2)]
    unnamed x157 -> x119, local copies, waits for them, and re-layouts: 24.7 us -> 21.6 us
where the time goes in v3:
time: 451 us; the launch traced here: 443 us
  Pallas kernels  340 us (75%)
  local copies, waits for them, and re-layouts  38.1 us (8%)
  matrix products  34.3 us (8%)
  other arithmetic  28.9 us (6%)
    pallas_call x1, Pallas kernels, back(): pl.pallas_call(back_kernel, name='back', out_shape=[struct((3, 2, 4, SLIC...  168 us
    pallas_call x1, Pallas kernels, front(): pl.pallas_call(front_kernel, name='front', out_shape=[struct((16,) + shar...  122 us
    pallas_call x1, Pallas kernels, tensor_call(): pl.pallas_call(kernel, name=name, out_shape=outs, in_specs=in_specs, out_...  49.7 us
    dot_general x12, matrix products, dot(): lax.dot_general(left, right, (((left_dim,), (right_dim,)), ((), ())), pre...  34.3 us
    unnamed x119, local copies, waits for them, and re-layouts  21.6 us
    add x2, other arithmetic, level(): return jnp.floor(codes * B16(1.0 / stride)) * B16(stride) + B16(stride // 2)  11.3 us

profile of v3, /device:TPU:0, one launch (start us, length us, event | category | flops | bytes accessed | tf_op | source)
XLA Modules:
  0.0 442.7 jit_solution(6124802955665483890)
XLA Ops:
  0.8 0.6 copy-done
  1.4 0.6 convert_reduce_fusion
  2.2 3.1 multiply_sine_fusion
  5.3 1.1 broadcast_in_dim_reshape.4.refs_8_.refs_21_
  6.5 0.7 pad_maximum_fusion.8.refs_5_.gains.refs_16_
  7.2 0.6 broadcast_in_dim.7.refs_7_.refs_13_
  7.8 0.6 pad_maximum_fusion.9
  8.5 0.9 pad_maximum_fusion.6.refs_2_
  9.4 0.8 convert_bitcast_fusion.refs_3_
  10.3 0.7 pad_maximum_fusion.7.refs_0_
  10.9 0.6 convert_bitcast_fusion.1.refs_1_
  11.6 122.0 %front.1 = (bf16[16,144,512]{2,1,0:T(8,128)(2,1)}, bf16[16,144,256]{2,1,0:T(8,128)(2,1)}, bf16[16,144,2304]{2,1,0:T(8,128)(2,1)}, bf16[16,144,1152]{2,1,0:T(8,12...) custom-call(bf16[144,512]{1,0:T(8,128)(2,1)} %pad_maximum_fusion.7.r, ...), custom_call_target="tpu_custom_call" | custom-call | tf_op jit(solution)/shard_map/front/pallas_call | solution.py:783
  133.6 2.5 fusion.25
  136.2 5.9 %fusion = f32[1,128,2304]{2,1,0:T(8,128)S(1)} fusion(bf16[128,2304]{1,0:T(8,128)(2,1)} %bitcast.152, bf16[2304,2304]{1,0:T(8,128)(2,1)} %bitcast.121, f32[2304]{0:T(1024)S(1)} %constant_dynamic-update-slice_fusion), kind=kOutput, calls=%fused_computation.11 | convolution fusion | flops 1359249408 | bytes 12395520 | tf_op jit(solution)/shard_map/dot_general | solution.py:557
  142.1 0.7 slice-done.2
  142.8 7.5 %multiply_add_fusion.1 = (bf16[16,144,2304]{2,1,0:T(8,128)(2,1)S(1)}, bf16[16,144,2304]{2,1,0:T(8,128)(2,1)S(1)}) fusion(bf16[16,144,2304]{2,1,0:T(8,128)(2,1)S(1)} %bitcast.123), kind=kLoop, calls=%fused_computation.1 | loop fusion | flops 90243072 | bytes 31850496 | tf_op jit(solution)/shard_map/add | solution.py:1188
  150.3 1.6 fusion.1
  151.9 2.3 copy-done.3
  154.3 3.2 copy-done.2
  157.4 1.6 fusion.2
  159.1 0.3 pad_maximum_fusion
  159.4 0.7 copy-done.13
  160.1 0.6 multiply_convert_fusion.2
  160.7 1.1 copy-done.7
  161.8 1.6 fusion.11
  163.4 3.8 multiply_add_fusion.3
  167.2 1.6 fusion.10
  168.8 0.7 copy-done.4
  169.5 1.6 fusion.9
  171.2 1.4 pad_maximum_fusion.2.part
  172.6 49.7 %feed.1 = (bf16[3,128,2304]{2,1,0:T(8,128)(2,1)}, bf16[3,16,2304]{2,1,0:T(8,128)(2,1)}, f32[8,2304]{1,0:T(8,128)}) custom-call(bf16[3,128,2304]{2,1,0:T(8,128)(2,1)} %pad_maximum_fusion.2.part, bf16[3,128,2304]{2,1,0:T(8,128)(2,1)} %bitcast.144, f32[3,16,2304]{2,1,0:T(8,128)} %get-tuple-element.47.middle.refs_6_, ...), custom_call_target="tpu_custom_call" | custom-call | tf_op jit(solution)/shard_map/feed/pallas_call | solution.py:499
  222.3 1.9 multiply_convert_fusion.1
  224.3 3.9 convolution_bitcast_fusion.2
  228.2 0.9 convolution_bitcast_fusion.1
  229.2 0.9 convolution_bitcast_fusion
  230.2 1.1 copy-done.8
  231.2 1.4 fusion.20
  232.6 1.3 pad_maximum_fusion.5.refs_4_
  234.0 1.2 copy-done.10
  235.1 0.4 copy-done.12
  235.5 0.4 copy-done.14
  235.9 0.7 multiply_reduce_fusion
  236.7 0.9 slice-done.5
  237.6 3.5 fusion.6
  241.1 7.7 %fusion.7 = bf16[1,2,4,16,2304]{4,3,2,1,0:T(8,128)(2,1)S(1)} fusion(bf16[2,4,16,2304]{3,2,1,0:T(8,128)(2,1)S(1)} %bitcast.156, bf16[2304,2304,1,1]{1,0,3,2:T(8,128)(2,1)} %bitcast.132), kind=kOutput, calls=%fused_computation.26 | convolution fusion | flops 1359249408 | bytes 11796480 | tf_op jit(solution)/shard_map/dot_general | solution.py:557
  248.8 3.5 fusion.8
  252.4 1.4 pad_maximum_fusion.4.refs_0_
  253.8 0.6 maximum_divide_fusion.refs_10_
  254.5 2.2 copy.64
  256.7 2.2 copy.63
  258.9 0.6 broadcast_in_dim.8.refs_14_
  259.5 168.1 %back.1 = (bf16[3,2,4,16,2304]{4,3,2,1,0:T(8,128)(2,1)}, f32[1,2,4,16,2304]{4,3,2,1,0:T(8,128)}, f32[8,2304]{1,0:T(8,128)}, f32[144,1152]{1,0:T(8,128)}, f32[144...) custom-call(bf16[3,2,4,16,2304]{4,3,2,1,0:T(8,128)(2,1)} %pad_maximum_fusion.4.refs_0_, ...), custom_call_target="tpu_custom_call" | custom-call | tf_op jit(solution)/shard_map/back/pallas_call | solution.py:1168
  427.6 3.6 copy.67
  431.3 0.7 fusion.26
  431.9 0.7 slice.101
  432.6 1.6 fusion.27
  434.2 1.4 slice_reduce_fusion
  435.6 1.2 slice_bitcast_fusion.12
  436.8 1.3 slice.104
  438.1 1.2 copy.78
  439.3 0.7 copy.79
  440.0 0.8 copy.80
  440.8 0.8 copy.81
  441.7 0.8 copy.82
  (127 shorter events, 1.0 us)
Async XLA Ops:
  0.7 0.7 copy-start
  0.7 5.8 %copy-start.35 = (f32[2304]{0:T(1024)S(1)}, f32[2304]{0:T(1024)}, u32[]{:S(2)}) copy-start(f32[2304]{0:T(1024)} %param.38) | copy-start | bytes 27652
  0.7 5.8 %copy-start.36 = (f32[2304]{0:T(1024)S(1)}, f32[2304]{0:T(1024)}, u32[]{:S(2)}) copy-start(f32[2304]{0:T(1024)} %param.39) | copy-start | bytes 27652
  0.7 5.8 %copy-start.37 = (f32[2304]{0:T(1024)S(1)}, f32[2304]{0:T(1024)}, u32[]{:S(2)}) copy-start(f32[2304]{0:T(1024)} %param.40) | copy-start | bytes 27652
  0.7 5.8 %copy-start.38 = (f32[2304]{0:T(1024)S(1)}, f32[2304]{0:T(1024)}, u32[]{:S(2)}) copy-start(f32[2304]{0:T(1024)} %param.41) | copy-start | bytes 27652
  0.7 6.5 %copy-start.39 = (f32[2304]{0:T(1024)S(1)}, f32[2304]{0:T(1024)}, u32[]{:S(2)}) copy-start(f32[2304]{0:T(1024)} %param.34) | copy-start | bytes 27652
  0.7 7.1 %copy-start.40 = (f32[256]{0:T(256)S(1)}, f32[256]{0:T(256)}, u32[]{:S(2)}) copy-start(f32[256]{0:T(256)} %param.31) | copy-start | bytes 3076
  0.7 7.1 %copy-start.42 = (f32[128]{0:T(128)S(1)}, f32[128]{0:T(128)}, u32[]{:S(2)}) copy-start(f32[128]{0:T(128)} %param.32) | copy-start | bytes 1540
  0.7 7.1 %copy-start.41 = (f32[128]{0:T(128)S(1)}, f32[128]{0:T(128)}, u32[]{:S(2)}) copy-start(f32[128]{0:T(128)} %param.33) | copy-start | bytes 1540
  0.8 7.6 %copy-start.19 = (s32[144,1152]{1,0:T(8,128)S(1)}, s32[144,1152]{1,0:T(8,128)}, u32[]{:S(2)}) copy-start(s32[144,1152]{1,0:T(8,128)} %param.28) | copy-start | bytes 1990660
  0.8 7.7 %copy-start.20 = (s32[144,1152]{1,0:T(8,128)S(1)}, s32[144,1152]{1,0:T(8,128)}, u32[]{:S(2)}) copy-start(s32[144,1152]{1,0:T(8,128)} %param.29) | copy-start | bytes 1990660
  6.4 3.0 copy-start.21
  8.4 1.8 copy-start.28
  8.5 1.8 copy-start.31
  8.5 1.8 copy-start.32
  8.5 2.4 copy-start.29
  133.6 2.6 copy-start.33
  133.6 2.6 copy-start.34
  133.6 8.5 %slice-start = ((s8[10616832]{0:T(1024)(128)(4,1)}), s8[2228224]{0:T(1024)(128)(4,1)S(1)}, s32[]{:S(2)}) async-start(s8[10616832]{0:T(1024)(128)(4,1)} %bitcast.122), calls=%async_computation | async-start | bytes 4456448
  136.1 5.9 %slice-start.1 = ((s8[10616832]{0:T(1024)(128)(4,1)}), s8[4194304]{0:T(1024)(128)(4,1)S(1)}, s32[]{:S(2)}) async-start(s8[10616832]{0:T(1024)(128)(4,1)} %bitcast.122), calls=%async_computation.1 | async-start | bytes 8388608
  136.2 6.7 %slice-start.2 = ((s8[10616832]{0:T(1024)(128)(4,1)}), s8[4194304]{0:T(1024)(128)(4,1)S(1)}, s32[]{:S(2)}) async-start(s8[10616832]{0:T(1024)(128)(4,1)} %bitcast.122), calls=%async_computation.2 | async-start | bytes 8388608
  142.8 16.2 %copy-start.9 = (f32[1,128,2304]{2,1,0:T(8,128)}, f32[1,128,2304]{2,1,0:T(8,128)S(1)}, u32[]{:S(2)}) copy-start(f32[1,128,2304]{2,1,0:T(8,128)S(1)} %fusion) | copy-start | bytes 3538948
  150.3 3.9 copy-start.3
  150.3 7.1 %copy-start.2 = (bf16[16,144,2304]{2,1,0:T(8,128)(2,1)}, bf16[16,144,2304]{2,1,0:T(8,128)(2,1)S(1)}, u32[]{:S(2)}) copy-start(bf16[16,144,2304]{2,1,0:T(8,128)(2,1)S(1)} %get-tuple-element.155) | copy-start | bytes 31850500
  150.3 11.5 %slice-start.9 = ((s8[5308416]{0:T(1024)(128)(4,1)}), s8[1114112]{0:T(1024)(128)(4,1)S(1)}, s32[]{:S(2)}) async-start(s8[5308416]{0:T(1024)(128)(4,1)} %bitcast.134), calls=%async_computation.9 | async-start | bytes 2228224
  154.3 4.8 %copy-start.11 = (f32[1,128,2304]{2,1,0:T(8,128)}, f32[1,128,2304]{2,1,0:T(8,128)S(1)}, u32[]{:S(2)}) copy-start(f32[1,128,2304]{2,1,0:T(8,128)S(1)} %fusion.1) | copy-start | bytes 3538948
  157.4 4.4 slice-start.10
  159.0 1.0 copy-start.13
  160.1 1.7 copy-start.7
  160.1 1.8 copy-start.25
  161.8 7.0 %copy-start.15 = (bf16[3,128,1152]{2,1,0:T(8,128)(2,1)}, bf16[3,128,1152]{2,1,0:T(8,128)(2,1)S(1)}, u32[]{:S(2)}) copy-start(bf16[3,128,1152]{2,1,0:T(8,128)(2,1)S(1)} %multiply_convert_fusion.2) | copy-start | bytes 2654212
  167.2 2.3 copy-start.4
  167.2 4.0 copy-start.5
  222.3 5.9 %copy-start.6 = (bf16[16,144,1152]{2,1,0:T(8,128)(2,1)S(1)}, bf16[16,144,1152]{2,1,0:T(8,128)(2,1)}, u32[]{:S(2)}) copy-start(bf16[16,144,1152]{2,1,0:T(8,128)(2,1)} %copy-done.5) | copy-start | bytes 15925252
  222.3 6.8 %slice-start.11 = ((s8[5308416]{0:T(1024)(128)(4,1)}), s8[1114112]{0:T(1024)(128)(4,1)S(1)}, s32[]{:S(2)}) async-start(s8[5308416]{0:T(1024)(128)(4,1)} %bitcast.138), calls=%async_computation.11 | async-start | bytes 2228224
  224.3 4.9 %slice-start.12 = ((s8[5308416]{0:T(1024)(128)(4,1)}), s8[4194304]{0:T(1024)(128)(4,1)S(1)}, s32[]{:S(2)}) async-start(s8[5308416]{0:T(1024)(128)(4,1)} %bitcast.138), calls=%async_computation.12 | async-start | bytes 8388608
  229.2 2.0 copy-start.8
  231.2 5.5 %slice-start.3 = ((s8[10616832]{0:T(1024)(128)(4,1)}), s8[4194304]{0:T(1024)(128)(4,1)S(1)}, s32[]{:S(2)}) async-start(s8[10616832]{0:T(1024)(128)(4,1)} %bitcast.124), calls=%async_computation.3 | async-start | bytes 8388608
  231.2 5.5 %slice-start.4 = ((s8[10616832]{0:T(1024)(128)(4,1)}), s8[4194304]{0:T(1024)(128)(4,1)S(1)}, s32[]{:S(2)}) async-start(s8[10616832]{0:T(1024)(128)(4,1)} %bitcast.124), calls=%async_computation.4 | async-start | bytes 8388608
  232.6 2.5 copy-start.10
  232.6 2.9 copy-start.12
  232.6 3.2 copy-start.14
  235.9 1.8 slice-start.5
  237.6 11.2 %slice-start.6 = ((s8[10616832]{0:T(1024)(128)(4,1)}), s8[4194304]{0:T(1024)(128)(4,1)S(1)}, s32[]{:S(2)}) async-start(s8[10616832]{0:T(1024)(128)(4,1)} %bitcast.128), calls=%async_computation.6 | async-start | bytes 8388608
  237.6 11.2 %slice-start.7 = ((s8[10616832]{0:T(1024)(128)(4,1)}), s8[2228224]{0:T(1024)(128)(4,1)S(1)}, s32[]{:S(2)}) async-start(s8[10616832]{0:T(1024)(128)(4,1)} %bitcast.128), calls=%async_computation.7 | async-start | bytes 4456448
  241.1 7.7 %slice-start.8 = ((s8[10616832]{0:T(1024)(128)(4,1)}), s8[4194304]{0:T(1024)(128)(4,1)S(1)}, s32[]{:S(2)}) async-start(s8[10616832]{0:T(1024)(128)(4,1)} %bitcast.128), calls=%async_computation.8 | async-start | bytes 8388608
  252.4 2.1 copy-start.17
  254.5 2.2 copy-start.16
  256.7 2.2 copy-start.26
  427.6 3.7 copy-start.27
  427.6 10.5 %copy-start.18 = (bf16[3,2,4,16,2304]{4,3,2,1,0:T(8,128)(2,1)S(1)}, bf16[3,2,4,16,2304]{4,3,2,1,0:T(8,128)(2,1)}, u32[]{:S(2)}) copy-start(bf16[3,2,4,16,2304]{4,3,2,1,0:T(8,128)(2,1)} %get-tuple-element.60) | copy-start | bytes 5308420
  438.1 1.2 copy-start.30
  438.1 1.9 copy-start.24
  438.1 2.7 copy-start.23
  439.3 2.4 copy-start.22
  439.3 3.2 copy-start.1

commit v4 on v3

--- a/solution.py
+++ b/solution.py
@@ -16,13 +16,14 @@
 MASKED = -1e30
 HD = 256
 WIDE = 2304
+FF = 1152
+STRIDES = (1, 16, 64)
 SHARD = 144
 LOW = 64
 HIGH = SHARD - LOW
 TENSOR = 8
 ROWS = 128
 SLICE = ROWS // TENSOR
-EXTRA = 384
 VMEM_BYTES = 63 * 2**20
 
 
@@ -389,67 +390,6 @@
     ]
 
 
-def row_block(index):
-    return pl.ds(pl.multiple_of(index * SLICE, SLICE), SLICE)
-
-
-def tensor_peers():
-    t = lax.axis_index("tensor")
-    return [lax.rem(t + k, TENSOR) for k in range(TENSOR)]
-
-
-def greet_tensor():
-    dp = lax.axis_index("dp")
-    greet([(dp, peer) for peer in tensor_peers()[1:]])
-
-
-def scatter_rows(part, held, send, recv, local):
-    dp = lax.axis_index("dp")
-    peers = tensor_peers()
-    copies = []
-    for k in range(1, TENSOR):
-        copy = remote(
-            part.at[:, row_block(peers[k])], held.at[k], send.at[k], recv.at[k], dp, peers[k]
-        )
-        copy.start()
-        copies.append(copy)
-    mine = pltpu.make_async_copy(part.at[:, row_block(peers[0])], held.at[0], local)
-    mine.start()
-    mine.wait()
-    return copies
-
-
-def summed(held, copies):
-    total = held[0].astype(F32)
-    for k in range(1, TENSOR):
-        copies[k - 1].wait_recv()
-        total = total + held[k].astype(F32)
-    return total
-
-
-def spread_rows(block, whole, send, recv, local):
-    dp = lax.axis_index("dp")
-    peers = tensor_peers()
-    here_rows = whole.at[:, row_block(peers[0])]
-    copies = []
-    for k in range(1, TENSOR):
-        copy = remote(block, here_rows, send.at[k], recv.at[k], dp, peers[k])
-        copy.start()
-        copies.append(copy)
-    mine = pltpu.make_async_copy(block, here_rows, local)
-    mine.start()
-
-    def finish():
-        mine.wait()
-        for k in range(1, TENSOR):
-            source = whole.at[:, row_block(peers[TENSOR - k])]
-            remote(source, source, send.at[k], recv.at[k], dp, peers[k]).wait_recv()
-        for copy in copies:
-            copy.wait_send()
-
-    return finish
-
-
 def inverse_rms(signal):
     return lax.rsqrt(jnp.mean(signal * signal, axis=-1, keepdims=True) + EPSILON)
 
@@ -459,61 +399,176 @@
     return inverse * (inner - normed * jnp.mean(inner * normed, axis=-1, keepdims=True))
 
 
-def over_rows(term):
-    return jnp.sum(term, axis=(0, 1))[None]
-
-
-def load_rows(whole, block, local):
-    copy = pltpu.make_async_copy(
-        whole.at[:, row_block(lax.axis_index("tensor"))], block, local
-    )
-    copy.start()
-    return copy
+def half_level(codes, width):
+    return codes if width == 0 else jnp.floor(codes * B16(1.0 / STRIDES[width]))
+
+
+def offset(left, width):
+    return 0.0 if width == 0 else 0.5 * jnp.sum(left.astype(F32), axis=-1, keepdims=True)
 
 
 def feed_kernel(
-    part, cotangent, middle, gains, d_feed, final, sums, held, mine, block, send, recv, local
+    normed_middle, w_gu, w_down, cotangent, scale_gu, scale_down, middle, gains,
+    d_part, turned_middle, turned_feed, d_gu_low, hidden, final, sums, gu_sums,
+    nm, wg, wd, gu_pre, part, cot, d_feed, dgs, held_x, held_z, stage, block, *sems,
 ):
-    greet_tensor()
-    copies = scatter_rows(part, held, send.at[0], recv.at[0], local.at[0])
-    load = load_rows(cotangent, mine, local.at[1])
-    load.wait()
-    signal = summed(held, copies)
-    inverse = inverse_rms(signal)
-    normed = signal * inverse
-    upstream = mine[...].astype(F32)
-    lowered = norm_back(normed, inverse, gains[3:4], upstream).astype(B16)
-    block[...] = lowered
-    finish = spread_rows(block, d_feed, send.at[1], recv.at[1], local.at[2])
-    final[...] = (middle[...] + normed * (1.0 + gains[3:4])).astype(B16)
-    sums[0:1] = over_rows(upstream * normed)
-    sums[1:2] = over_rows(lowered.astype(F32) * signal)
-    for copy in copies:
-        copy.wait_send()
-    finish()
-
-
-def tensor_call(
-    kernel, name, collective_id, depth, loaded, operands, in_specs, outs, out_specs, blocks
-):
+    rows = Rows(part, held_x, held_z, stage, block, d_feed, sems[:3])
+    local_g, local_d, local = sems[3:]
+    greet(rows.peers())
+    loads = [
+        pltpu.make_async_copy(normed_middle.at[w], nm.at[w], local.at[w]) for w in range(3)
+    ] + [pltpu.make_async_copy(cotangent.at[:, rows.zl, rows.x], cot, local.at[3])]
+    for copy in loads:
+        copy.start()
+
+    def load_g(j):
+        cols = pl.ds(pl.multiple_of(j * 256, 256), 256)
+        return pltpu.make_async_copy(w_gu.at[:, cols], wg.at[:, cols], local_g.at[j])
+
+    def load_d(j):
+        tile = pl.ds(pl.multiple_of(j * 256, 256), 256)
+        return pltpu.make_async_copy(w_down.at[tile], wd.at[tile], local_d.at[j])
+
+    for j in range(9):
+        load_g(j).start()
+    for j in range(9):
+        load_d(j).start()
+
+    def forward(w):
+        if w == 0:
+            for copy in loads:
+                copy.wait()
+        stride = STRIDES[w]
+        left = nm[w].reshape(ROWS, WIDE)
+        extra = offset(left, w)
+
+        def gate_up(j, _):
+            cols = pl.ds(pl.multiple_of(j * 256, 256), 256)
+            if w == 0:
+                load_g(j).wait()
+            product = dot(left, half_level(wg[:, cols], w), 1, 0)
+            gu_pre[w, :, cols] = (product + extra) * (scale_gu[:, cols] * stride)
+            return 0
+
+        lax.fori_loop(0, 9, gate_up, 0)
+        gate_pre, up_pre = gu_pre[w, :, :FF], gu_pre[w, :, FF:]
+        grown, _ = gelu_parts(gate_pre)
+        low = (grown * up_pre).astype(B16)
+        hidden[w] = low
+        extra_down = offset(low, w)
+
+        def down(j, _):
+            tile = pl.ds(pl.multiple_of(j * 256, 256), 256)
+            if w == 0:
+                load_d(j).wait()
+            product = dot(low, half_level(wd[tile], w), 1, 1)
+            product = (product + extra_down) * (scale_down[:, tile] * stride)
+            part[w, :, :, :, tile] = product.astype(B16).reshape(2, 4, SLICE, 256)
+            return 0
+
+        lax.fori_loop(0, 9, down, 0)
+        rows.scatter_x(w)
+
+    def norm(w):
+        signal = rows.total(w)
+        inverse = inverse_rms(signal)
+        normed = signal * inverse
+        upstream = cot[w].astype(F32)
+        lowered = norm_back(normed, inverse, gains[3:4], upstream).astype(B16)
+        block[w] = lowered
+        rows.spread(w)
+        final[w] = (middle[w] + normed * (1.0 + gains[3:4])).astype(B16)
+        for i, term in enumerate((upstream * normed, lowered.astype(F32) * signal)):
+            term = jnp.sum(term, axis=0, keepdims=True)
+            sums[i : i + 1] = term if w == 0 else sums[i : i + 1] + term
+
+    def backward(w):
+        stride = STRIDES[w]
+        lowered = d_feed[w].reshape(ROWS, WIDE)
+        turned_feed[:, w * ROWS : (w + 1) * ROWS] = lowered.T
+        scaled = (lowered.astype(F32) * scale_down[...]).astype(B16)
+        extra = offset(scaled, w)
+        for i in range(3):
+            cols = slice(384 * i, 384 * i + 384)
+            ups = slice(FF + 384 * i, FF + 384 * i + 384)
+            d_hidden = (dot(scaled, half_level(wd[:, cols], w), 1, 0) + extra) * float(stride)
+            grown, rate = gelu_parts(gu_pre[w, :, cols])
+            for where, value in ((cols, d_hidden * gu_pre[w, :, ups] * rate), (ups, d_hidden * grown)):
+                low = value.astype(B16)
+                d_gu_low[w, :, where] = low
+                dgs[:, where] = (value * scale_gu[:, where]).astype(B16)
+                term = jnp.sum(low.astype(F32) * gu_pre[w, :, where], axis=0, keepdims=True)
+                term = term / scale_gu[:, where]
+                gu_sums[:, where] = term if w == 0 else gu_sums[:, where] + term
+        left = dgs[...]
+        extra_gu = offset(left, w)
+
+        def gate_up(j, _):
+            tile = pl.ds(pl.multiple_of(j * 256, 256), 256)
+            product = dot(left, half_level(wg[tile], w), 1, 1)
+            product = (product + extra_gu) * float(stride)
+            d_part[w, :, :, :, tile] = product.astype(B16).reshape(2, 4, SLICE, 256)
+            return 0
+
+        lax.fori_loop(0, 9, gate_up, 0)
+
+    forward(0)
+    forward(1)
+    rows.scatter_z(0)
+    forward(2)
+    rows.scatter_z(1)
+    norm(0)
+    rows.scatter_z(2)
+    norm(1)
+    rows.forward(0)
+    norm(2)
+    rows.forward(1)
+    for w in range(3):
+        turned_middle[:, w * ROWS : (w + 1) * ROWS] = nm[w].reshape(ROWS, WIDE).T
+    rows.end(0)
+    backward(0)
+    rows.forward(2)
+    rows.end(1)
+    backward(1)
+    rows.end(2)
+    backward(2)
+    rows.drain()
+
+
+def feed(hbm, vmem):
     return pl.pallas_call(
-        kernel,
-        name=name,
-        out_shape=outs,
-        in_specs=in_specs,
-        out_specs=out_specs,
+        feed_kernel,
+        name="feed",
+        out_shape=[
+            struct((3, 2, 4, SLICE, WIDE), B16),
+            struct((WIDE, 3 * ROWS), B16),
+            struct((WIDE, 3 * ROWS), B16),
+            struct((3, ROWS, 2 * FF), B16),
+            struct((3, ROWS, FF), B16),
+            struct((3, SLICE, WIDE), B16),
+            struct((8, WIDE), F32),
+            struct((1, 2 * FF), F32),
+        ],
+        in_specs=any_space(len(hbm)) + vmem_space(len(vmem)),
+        out_specs=vmem_space(8),
         scratch_shapes=[
-            pltpu.VMEM((TENSOR, depth, SLICE, WIDE), B16),
-            pltpu.VMEM((loaded, SLICE, WIDE), B16),
+            pltpu.VMEM((3, 2, 4, SLICE, WIDE), B16),
+            pltpu.VMEM((WIDE, 2 * FF), B16),
+            pltpu.VMEM((WIDE, FF), B16),
+            pltpu.VMEM((3, ROWS, 2 * FF), F32),
+            pltpu.VMEM((3, 2, 4, SLICE, WIDE), B16),
+            pltpu.VMEM((3, SLICE, WIDE), B16),
+            pltpu.VMEM((3, 2, 4, SLICE, WIDE), B16),
+            pltpu.VMEM((ROWS, 2 * FF), B16),
         ]
-        + blocks
+        + rows_scratch(3)
         + [
-            pltpu.SemaphoreType.DMA((3, TENSOR)),
-            pltpu.SemaphoreType.DMA((3, TENSOR)),
+            pltpu.SemaphoreType.DMA((9,)),
+            pltpu.SemaphoreType.DMA((9,)),
             pltpu.SemaphoreType.DMA((4,)),
         ],
-        compiler_params=params(collective_id),
-    )(*operands)
+        compiler_params=params(6),
+    )(*hbm, *vmem)
 
 
 def unit_owner(micro, width):
@@ -1184,7 +1239,7 @@
 def level(codes, width):
     if width == 0:
         return codes
-    stride = (1, 16, 64)[width]
+    stride = STRIDES[width]
     return jnp.floor(codes * B16(1.0 / stride)) * B16(stride) + B16(stride // 2)
 
 
@@ -1221,7 +1276,6 @@
     gain_third,
     gain_fourth,
 ):
-    widths = range(3)
     z_hi = lax.rem(lax.div(lax.axis_index("dp"), 2), 2)
     tokens = tokens.reshape(ROWS, WIDE)
     cotangent = cotangent.reshape(3, ROWS, WIDE)
@@ -1250,53 +1304,27 @@
     *weights, normed_middle, attended, normed_input, qkv_pre, q_rot, k_rot, v_all, branch, middle = front(
         shards, tokens, gains, scale_qkv, output_column_scale, first, cosine, sine
     )
-    w_qkv, w_out, w_gu, w_down = (gathered.reshape(WIDE, -1) for gathered in weights)
+    w_gu, w_down = (gathered.reshape(WIDE, -1) for gathered in weights[2:])
     attended = attended.reshape(3, ROWS, HD)
-    normed_middle = normed_middle.reshape(3, ROWS, WIDE)
-    gu_pre = jnp.stack([dot(normed_middle[w], level(w_gu, w), 1, 0) * scale_gu for w in widths])
-    half = gu_pre.shape[-1] // 2
-    gate_pre, up_pre = gu_pre[..., :half], gu_pre[..., half:]
-    grown, rate = gelu_parts(gate_pre)
-    hidden = (grown * up_pre).astype(B16)
-    feed_part = jnp.stack(
-        [dot(hidden[w], level(w_down, w), 1, 1) * down_column_scale for w in widths]
-    ).astype(B16)
-    d_feed, final, feed_sums = tensor_call(
-        feed_kernel,
-        "feed",
-        6,
-        3,
-        3,
-        (feed_part, cotangent, middle, gains),
-        any_space(2) + vmem_space(2),
-        [struct((3, ROWS, WIDE), B16), struct((3, SLICE, WIDE), B16), struct((8, WIDE), F32)],
-        any_space(1) + vmem_space(2),
-        [pltpu.VMEM((3, SLICE, WIDE), B16)],
+    grid = (3, 2, 4, SLICE, WIDE)
+    d_part, turned_middle, turned_feed, d_gu, hidden, final, feed_sums, gu_sums = feed(
+        [normed_middle, w_gu, w_down, cotangent.reshape(grid)],
+        [scale_gu[None], down_column_scale[None], middle, gains],
     )
 
-    d_feed_scaled = (d_feed.astype(F32) * down_column_scale).astype(B16)
-    d_hidden = jnp.stack([dot(d_feed_scaled[w], level(w_down, w), 1, 0) for w in widths])
-    d_gu = jnp.concatenate([d_hidden * up_pre * rate, d_hidden * grown], -1)
-    d_gu_low = d_gu.astype(B16)
-    gu_sums = jnp.sum(d_gu_low.astype(F32) * gu_pre, axis=(0, 1)) / scale_gu
-    d_gu_scaled = (d_gu * scale_gu).astype(B16)
-    d_middle_part = jnp.stack([dot(d_gu_scaled[w], level(w_gu, w), 1, 1) for w in widths]).astype(
-        B16
-    )
     flat = (3 * ROWS, -1)
-    grid = (3, 2, 4, SLICE, WIDE)
     results, input_gradient, totals, g_gate, g_up, g_down, g_out, g_qkv = back(
-        [d_middle_part.reshape(grid), cotangent.reshape(grid)],
+        [d_part, cotangent.reshape(grid)],
         [
-            normed_middle.reshape(flat).T,
-            d_feed.reshape(flat).T,
-            d_gu_low.reshape(flat),
+            turned_middle,
+            turned_feed,
+            d_gu.reshape(flat),
             hidden.reshape(flat),
             middle,
             branch,
             final,
             feed_sums,
-            gu_sums[None],
+            gu_sums,
             weights[1],
             weights[0],
             output_column_scale[None],
@@ -1330,8 +1358,8 @@
         totals[7, 256:384],
         totals[7, 384:512],
         rows[4],
-        totals[6, :half],
-        totals[6, half:],
+        totals[6, :FF],
+        totals[6, FF:],
         rows[5],
         rows[0],
         rows[1],

time: 451 us -> 390 us (0.86)
  the two profiles are of different devices: /device:TPU:0 before, /device:TPU:32 now
where the time goes in v4:
time: 390 us; the launch traced here: 383 us
  Pallas kernels  354 us (91%)
  local copies, waits for them, and re-layouts  18.8 us (5%)
  other arithmetic  7.94 us (2%)
    pallas_call x1, Pallas kernels, back(): pl.pallas_call(back_kernel, name='back', out_shape=[struct((3, 2, 4, SLIC...  161 us
    pallas_call x1, Pallas kernels, front(): pl.pallas_call(front_kernel, name='front', out_shape=[struct((16,) + shar...  121 us
    pallas_call x1, Pallas kernels, feed(): pl.pallas_call(feed_kernel, name='feed', out_shape=[struct((3, 2, 4, SLIC...  72.4 us
    unnamed x56, local copies, waits for them, and re-layouts  8.71 us

profile of v4, /device:TPU:32, one launch (start us, length us, event | category | flops | bytes accessed | tf_op | source)
XLA Modules:
  0.0 382.6 jit_solution(16450705975950947428)
XLA Ops:
  0.7 0.0 copy-start
  0.7 0.0 copy-start.14
  0.7 0.0 copy-start.15
  0.7 0.0 copy-start.16
  0.7 0.0 copy-start.17
  0.7 0.0 copy-start.18
  0.7 0.0 copy-start.22
  0.7 0.0 copy-start.24
  0.7 0.0 copy-start.23
  0.8 0.0 copy-start.2
  0.8 0.0 copy-start.3
  0.8 0.6 copy-done
  1.4 0.6 convert_reduce_fusion
  1.9 0.1 reshape.83
  2.0 0.1 copy.55
  2.1 0.1 convert_element_type.29
  2.2 3.0 multiply_sine_fusion
  5.2 0.1 copy.54
  5.3 1.1 broadcast_in_dim_reshape.4.refs_8_.refs_21_
  6.4 0.0 copy-done.14
  6.4 0.0 copy-done.15
  6.5 0.0 copy-done.16
  6.5 0.0 copy-done.17
  6.5 0.7 pad_maximum_fusion.2.refs_5_.gains.refs_16_
  7.2 0.0 copy-done.18
  7.2 0.6 broadcast_in_dim.9.refs_7_.refs_13_
  7.8 0.0 copy-done.22
  7.8 0.0 copy-done.24
  7.8 0.0 copy-done.23
  7.8 0.6 pad_maximum_fusion.4
  8.4 0.0 copy-done.2
  8.4 0.0 copy-done.3
  8.4 0.0 copy-start.9
  8.4 0.0 copy-start.12
  8.5 0.0 copy-start.13
  8.5 0.0 copy-start.10
  8.5 0.9 pad_maximum_fusion.refs_2_
  9.4 0.0 copy-done.4
  9.4 0.8 convert_bitcast_fusion.refs_3_
  10.2 0.0 copy-done.13
  10.2 0.7 pad_maximum_fusion.1.refs_0_
  10.9 0.6 convert_bitcast_fusion.1.refs_1_
  11.6 121.0 %front.1 = (bf16[16,144,512]{2,1,0:T(8,128)(2,1)}, bf16[16,144,256]{2,1,0:T(8,128)(2,1)}, bf16[16,144,2304]{2,1,0:T(8,128)(2,1)}, bf16[16,144,1152]{2,1,0:T(8,12...) custom-call(bf16[144,512]{1,0:T(8,128)(2,1)} %pad_maximum_fusion.1.r, ...), custom_call_target="tpu_custom_call" | custom-call | tf_op jit(solution)/shard_map/front/pallas_call | solution.py:838
  132.6 0.6 broadcast_in_dim.22.scale_down.refs_14_
  133.2 0.0 copy-done.21
  133.2 0.6 broadcast_in_dim.10.scale_gu
  133.8 72.4 %feed.1 = (bf16[3,2,4,16,2304]{4,3,2,1,0:T(8,128)(2,1)}, bf16[2304,384]{1,0:T(8,128)(2,1)}, bf16[2304,384]{1,0:T(8,128)(2,1)}, bf16[3,128,2304]{2,1,0:T(8,128)(2...) custom-call(bf16[3,2,4,16,2304]{4,3,2,1,0:T(8,128)(2,1)} %get-tuple-e, ...), custom_call_target="tpu_custom_call" | custom-call | tf_op jit(solution)/shard_map/feed/pallas_call | solution.py:539
  206.2 161.0 %back.1 = (bf16[3,2,4,16,2304]{4,3,2,1,0:T(8,128)(2,1)}, f32[1,2,4,16,2304]{4,3,2,1,0:T(8,128)}, f32[8,2304]{1,0:T(8,128)}, f32[144,1152]{1,0:T(8,128)}, f32[144...) custom-call(bf16[3,2,4,16,2304]{4,3,2,1,0:T(8,128)(2,1)} %get-tuple-element.53.refs_0_, ...), custom_call_target="tpu_custom_call" | custom-call | tf_op jit(solution)/shard_map/back/pallas_call | solution.py:1223
  367.3 0.0 copy-start.8
  367.3 0.0 copy-start.1
  367.3 3.6 copy.59
  370.9 0.0 copy-done.8
  370.9 0.7 fusion
  371.6 0.7 slice.42
  372.3 1.6 fusion.1
  373.8 1.4 slice_reduce_fusion
  375.3 1.2 slice_bitcast_fusion
  376.5 1.3 slice.45
  377.7 1.2 copy.65
  378.9 0.7 copy.66
  379.6 0.8 copy.67
  380.5 0.8 copy.68
  381.3 0.0 copy-done.5
  381.3 0.8 copy.69
  (30 shorter events, 0.2 us)
Async XLA Ops:
  0.7 0.7 copy-start
  0.7 5.7 %copy-start.14 = (f32[2304]{0:T(1024)S(1)}, f32[2304]{0:T(1024)}, u32[]{:S(2)}) copy-start(f32[2304]{0:T(1024)} %param.38) | copy-start | bytes 27652
  0.7 5.8 %copy-start.15 = (f32[2304]{0:T(1024)S(1)}, f32[2304]{0:T(1024)}, u32[]{:S(2)}) copy-start(f32[2304]{0:T(1024)} %param.39) | copy-start | bytes 27652
  0.7 5.8 %copy-start.16 = (f32[2304]{0:T(1024)S(1)}, f32[2304]{0:T(1024)}, u32[]{:S(2)}) copy-start(f32[2304]{0:T(1024)} %param.40) | copy-start | bytes 27652
  0.7 5.8 %copy-start.17 = (f32[2304]{0:T(1024)S(1)}, f32[2304]{0:T(1024)}, u32[]{:S(2)}) copy-start(f32[2304]{0:T(1024)} %param.41) | copy-start | bytes 27652
  0.7 6.5 %copy-start.18 = (f32[2304]{0:T(1024)S(1)}, f32[2304]{0:T(1024)}, u32[]{:S(2)}) copy-start(f32[2304]{0:T(1024)} %param.34) | copy-start | bytes 27652
  0.7 7.1 %copy-start.22 = (f32[256]{0:T(256)S(1)}, f32[256]{0:T(256)}, u32[]{:S(2)}) copy-start(f32[256]{0:T(256)} %param.31) | copy-start | bytes 3076
  0.7 7.0 %copy-start.24 = (f32[128]{0:T(128)S(1)}, f32[128]{0:T(128)}, u32[]{:S(2)}) copy-start(f32[128]{0:T(128)} %param.32) | copy-start | bytes 1540
  0.7 7.0 %copy-start.23 = (f32[128]{0:T(128)S(1)}, f32[128]{0:T(128)}, u32[]{:S(2)}) copy-start(f32[128]{0:T(128)} %param.33) | copy-start | bytes 1540
  0.8 7.6 %copy-start.2 = (s32[144,1152]{1,0:T(8,128)S(1)}, s32[144,1152]{1,0:T(8,128)}, u32[]{:S(2)}) copy-start(s32[144,1152]{1,0:T(8,128)} %param.28) | copy-start | bytes 1990660
  0.8 7.7 %copy-start.3 = (s32[144,1152]{1,0:T(8,128)S(1)}, s32[144,1152]{1,0:T(8,128)}, u32[]{:S(2)}) copy-start(s32[144,1152]{1,0:T(8,128)} %param.29) | copy-start | bytes 1990660
  6.4 3.0 copy-start.4
  8.4 1.8 copy-start.9
  8.4 1.8 copy-start.12
  8.5 1.8 copy-start.13
  8.5 2.4 copy-start.10
  11.6 121.0 %copy-start.19 = (f32[2304]{0:T(1024)S(1)}, f32[2304]{0:T(1024)}, u32[]{:S(2)}) copy-start(f32[2304]{0:T(1024)} %param.37) | copy-start | bytes 27652
  11.6 121.6 %copy-start.20 = (f32[1152]{0:T(1024)S(1)}, f32[1152]{0:T(1024)}, u32[]{:S(2)}) copy-start(f32[1152]{0:T(1024)} %param.36) | copy-start | bytes 13828
  11.6 121.6 %copy-start.21 = (f32[1152]{0:T(1024)S(1)}, f32[1152]{0:T(1024)}, u32[]{:S(2)}) copy-start(f32[1152]{0:T(1024)} %param.35) | copy-start | bytes 13828
  367.3 3.7 copy-start.8
  367.3 10.5 %copy-start.1 = (bf16[3,2,4,16,2304]{4,3,2,1,0:T(8,128)(2,1)S(1)}, bf16[3,2,4,16,2304]{4,3,2,1,0:T(8,128)(2,1)}, u32[]{:S(2)}) copy-start(bf16[3,2,4,16,2304]{4,3,2,1,0:T(8,128)(2,1)} %get-tuple-element.70) | copy-start | bytes 5308420
  377.7 1.2 copy-start.11
  377.7 1.9 copy-start.7
  377.7 2.7 copy-start.6
  378.9 2.4 copy-start.5
